TPU v7x, 128 devices: a whole 4x4x4 slice. The times are simulated.
128 devices in a mesh: dp: 4 (over x), expert: 32 (over y, z, core).
Axes of the slice: x: 4, y: 4, z: 4, core: 2. Of those that a mesh axis runs over, the one named last changes fastest.
Arguments:
- tokens: bfloat16 [16384, 2048], P(('dp', 'expert')), may hold values from -6 to 6
- grad_out: bfloat16 [16384, 2048], P(('dp', 'expert')), may hold values from -6 to 6
- norm_gain: float32 [2048], replicated, may hold values from 0.5 to 1.5
- router: bfloat16 [2048, 32], replicated, may hold values from -0.125 to 0.125
- w_in0: bfloat16 [32, 2048, 2560], P('expert', None, 'dp'), may hold values from -0.125 to 0.125
- w_in1: bfloat16 [32, 2048, 2560], P('expert', None, 'dp'), may hold values from -0.125 to 0.125
- w_out: bfloat16 [32, 2560, 2048], P('expert', 'dp'), may hold values from -0.125 to 0.125
- slot_rows: int32 [128, 32, 8], P(('dp', 'expert')), may hold values from 0 to 127, as said below
- slot_count: int32 [128, 32], P(('dp', 'expert')), may hold values from 0 to 8, as said below
Outputs:
- d_tokens: bfloat16 [16384, 2048], P(('dp', 'expert'))
- d_gain: float32 [2048], replicated
- d_router: float32 [2048, 32], replicated
- d_w_in0: bfloat16 [32, 2048, 2560], P('expert', None, 'dp')
- d_w_in1: bfloat16 [32, 2048, 2560], P('expert', None, 'dp')
- d_w_out: bfloat16 [32, 2560, 2048], P('expert', 'dp')
Inputs may be any that keep to these rules, and one draw needn't show every extreme that they name: `slot_rows`: for each sender and expert the 8 entries are distinct rows of that sender. Only the first slot_count slots of a block are live; in every routing group each expert's counts over the group's senders sum to exactly 128, and for every expert and group some sender has all 8 slots live and some sender none.
All inputs are finite; a program needn't handle non-finite values.
Results may differ from a plain program's by a relative error of at most 0.0079.
Values may be sent and summed in bfloat16 or wider, within the bound.
No kernel may reach another device: no remote copies, remote signals or barrier semaphores. Data moves between devices by JAX's collectives and lax.ppermute only.
A program may use at most 128 MiB of HBM per device.

v0:
```python
import jax
import jax.numpy as jnp
from jax import lax
from jax.sharding import PartitionSpec as P


def gelu_parts(pre):

    def gelu_tanh(value):
        return jax.nn.gelu(value, approximate=True)

    return jax.vjp(gelu_tanh, pre)


def repeat_blocks(value, copies):
    return jnp.broadcast_to(value[None], (copies,) + value.shape).reshape(
        (copies * value.shape[0],) + value.shape[1:]
    )


def per_device(tokens, grad_out, norm_gain, router, w_in0, w_in1, w_out, slot_rows, slot_count):
    highest = lax.Precision.HIGHEST
    tok_dev, width = tokens.shape
    experts = router.shape[1]
    slots = slot_rows.shape[2]
    n_dp = lax.axis_size("dp")
    n_all = lax.axis_size(("dp", "expert"))
    tok_float = tokens.astype(jnp.float32)
    inv_rms = lax.rsqrt(jnp.mean(tok_float * tok_float, axis=-1, keepdims=True) + 1e-06)
    normed = (tok_float * inv_rms * norm_gain).astype(jnp.bfloat16)
    gate = jax.nn.sigmoid(jnp.dot(normed, router, preferred_element_type=jnp.float32))
    positions = jnp.arange(tok_dev, dtype=jnp.int32)
    live = jnp.arange(slots, dtype=jnp.int32)[None, :] < slot_count[0][:, None]
    select = ((slot_rows[0][..., None] == positions) & live[..., None]).astype(jnp.float32)
    select_flat = select.reshape(experts * slots, tok_dev)
    picker = select_flat.astype(jnp.bfloat16)
    in_rows = (
        jnp.dot(picker, normed, preferred_element_type=jnp.float32)
        .astype(jnp.bfloat16)
        .reshape(experts, slots, width)
    )
    dy_rows = (
        jnp.dot(picker, grad_out, preferred_element_type=jnp.float32)
        .astype(jnp.bfloat16)
        .reshape(experts, slots, width)
    )
    gate_rows = jnp.einsum("est,te->es", select, gate, precision=highest).astype(jnp.bfloat16)
    in_recv, dy_recv, gate_recv = (
        lax.all_to_all(
            repeat_blocks(in_rows, n_dp), ("dp", "expert"), split_axis=0, concat_axis=0, tiled=True
        ),
        lax.all_to_all(
            repeat_blocks(dy_rows, n_dp), ("dp", "expert"), split_axis=0, concat_axis=0, tiled=True
        ),
        lax.all_to_all(
            repeat_blocks(gate_rows, n_dp),
            ("dp", "expert"),
            split_axis=0,
            concat_axis=0,
            tiled=True,
        ),
    )
    total_rows = n_all * slots
    in_all = in_recv.reshape(total_rows, width)
    dy_all = dy_recv.reshape(total_rows, width)
    gate_all = gate_recv.reshape(total_rows)
    weight0 = w_in0[0]
    weight1 = w_in1[0]
    weight_out = w_out[0]
    pre0 = jnp.dot(in_all, weight0, preferred_element_type=jnp.float32)
    pre1 = jnp.dot(in_all, weight1, preferred_element_type=jnp.float32)
    activated, pullback = gelu_parts(pre0)
    act = (activated * pre1).astype(jnp.bfloat16)
    expert_out = jnp.dot(act, weight_out, preferred_element_type=jnp.float32)
    dgate_part = jnp.sum(dy_all.astype(jnp.float32) * expert_out, axis=-1)
    dy_gated = (gate_all.astype(jnp.float32)[:, None] * dy_all.astype(jnp.float32)).astype(
        jnp.bfloat16
    )
    grad_wout = jnp.dot(act.T, dy_gated, preferred_element_type=jnp.float32).astype(jnp.bfloat16)
    d_act = jnp.dot(dy_gated, weight_out.T, preferred_element_type=jnp.float32)
    d_pre1 = (d_act * activated).astype(jnp.bfloat16)
    d_pre0 = pullback(d_act * pre1)[0].astype(jnp.bfloat16)
    grad_w0 = jnp.dot(in_all.T, d_pre0, preferred_element_type=jnp.float32).astype(jnp.bfloat16)
    grad_w1 = jnp.dot(in_all.T, d_pre1, preferred_element_type=jnp.float32).astype(jnp.bfloat16)
    dh_part = jnp.dot(d_pre0, weight0.T, preferred_element_type=jnp.float32) + jnp.dot(
        d_pre1, weight1.T, preferred_element_type=jnp.float32
    )
    dh_blocks = dh_part.reshape(n_all, slots, width)
    dgate_blocks = dgate_part.reshape(n_all, slots)
    back_rows, back_gate = (
        lax.all_to_all(dh_blocks, ("dp", "expert"), split_axis=0, concat_axis=0, tiled=True),
        lax.all_to_all(dgate_blocks, ("dp", "expert"), split_axis=0, concat_axis=0, tiled=True),
    )
    dh_rows = jnp.sum(back_rows.reshape(n_dp, experts, slots, width), axis=0)
    dgate_rows = jnp.sum(back_gate.reshape(n_dp, experts, slots), axis=0)
    dh_expert = jnp.dot(select_flat.T, dh_rows.reshape(experts * slots, width), precision=highest)
    dgate = jnp.einsum("est,es->te", select, dgate_rows, precision=highest)
    dlogit = dgate * gate * (1.0 - gate)
    d_normed = dh_expert + jnp.dot(dlogit, router.astype(jnp.float32).T, precision=highest)
    router_term = jnp.dot(normed.astype(jnp.float32).T, dlogit, precision=highest)
    gain_term = jnp.sum(d_normed * tok_float * inv_rms, axis=0)
    d_router, d_gain = lax.psum((router_term, gain_term), ("dp", "expert"))
    scaled = d_normed * norm_gain
    d_tokens = (
        grad_out.astype(jnp.float32)
        + inv_rms * scaled
        - tok_float * inv_rms**3 * jnp.mean(scaled * tok_float, axis=-1, keepdims=True)
    )
    return (
        d_tokens.astype(jnp.bfloat16),
        d_gain,
        d_router,
        grad_w0[None],
        grad_w1[None],
        grad_wout[None],
    )


def solution(mesh):
    in_specs = (
        P(("dp", "expert"), None),
        P(("dp", "expert"), None),
        P(),
        P(),
        P("expert", None, "dp"),
        P("expert", None, "dp"),
        P("expert", "dp", None),
        P(("dp", "expert"), None, None),
        P(("dp", "expert"), None),
    )
    out_specs = (
        P(("dp", "expert"), None),
        P(),
        P(),
        P("expert", None, "dp"),
        P("expert", None, "dp"),
        P("expert", "dp", None),
    )
    return jax.shard_map(
        per_device, mesh=mesh, in_specs=in_specs, out_specs=out_specs, check_vma=False
    )
```

profile of v0, /device:TPU:1, one launch (start us, length us, event | category | flops | bytes accessed | tf_op | source)
XLA Modules:
  0.0 438.5 jit_solution(7616307419317192651)
XLA Ops:
  7.2 1.4 fusion.58
  10.2 1.4 fusion.57
  12.9 11.5 %all-to-all-start = ((bf16[128,1,8]{2,1,0:T(2,128)(2,1)}), bf16[128,1,8]{2,1,0:T(2,128)(2,1)S(1)}, u32[]{:S(2)}, u32[]{:S(2)}) async-start(bf16[128,1,8]{2,1,0:T(2,128)(2,1)} %copy.22), calls=%async_computation | async-start | bytes 131072 | tf_op jit(solution)/shard_map/all_to_all | solution.py:55
  25.3 2.5 fusion.53
  27.9 5.8 %all-to-all-done = bf16[128,1,8]{2,1,0:T(2,128)(2,1)S(1)} async-done(((bf16[128,1,8]{2,1,0:T(2,128)(2,1)}), bf16[128,1,8]{2,1,0:T(2,128)(2,1)S(1)}, u32[]{:S(2)}, u32[]{:S(2)}) %all-to-all-start) | async-done | bytes 2080 | tf_op jit(solution)/shard_map/all_to_all | solution.py:55
  33.7 3.7 broadcast_in_dim.20
  37.4 5.9 %all-to-all-start.2 = ((bf16[128,8,2048]{2,1,0:T(8,128)(2,1)}), bf16[128,8,2048]{2,1,0:T(8,128)(2,1)}, u32[]{:S(2)}, u32[]{:S(2)}) async-start(bf16[128,8,2048]{2,1,0:T(8,128)(2,1)} %bitcast.104), calls=%async_computation.2 | async-start | bytes 8388608 | tf_op jit(solution)/shard_map/all_to_all | solution.py:49
  43.3 1.5 fusion.52
  44.8 51.4 %all-to-all-done.2 = bf16[128,8,2048]{2,1,0:T(8,128)(2,1)} async-done(((bf16[128,8,2048]{2,1,0:T(8,128)(2,1)}), bf16[128,8,2048]{2,1,0:T(8,128)(2,1)}, u32[]{:S(2)}, u32[]{:S(2)}) %all-to-all-start.2) | async-done | bytes 4194336 | tf_op jit(solution)/shard_map/all_to_all | solution.py:49
  96.2 3.7 broadcast_in_dim.18
  99.9 5.8 %all-to-all-start.1 = ((bf16[128,8,2048]{2,1,0:T(8,128)(2,1)}), bf16[128,8,2048]{2,1,0:T(8,128)(2,1)}, u32[]{:S(2)}, u32[]{:S(2)}) async-start(bf16[128,8,2048]{2,1,0:T(8,128)(2,1)} %bitcast.105), calls=%async_computation.1 | async-start | bytes 8388608 | tf_op jit(solution)/shard_map/all_to_all | solution.py:52
  105.8 7.9 %fusion.14 = f32[1024,640]{1,0:T(8,128)} fusion(bf16[128,8,2048]{2,1,0:T(8,128)(2,1)} %all-to-all-done.2, bf16[1,2048,640]{2,1,0:T(8,128)(2,1)} %param.13), kind=kOutput, calls=%fused_computation.15 | convolution fusion | flops 2684354560 | bytes 9437184 | tf_op jit(solution)/shard_map/dot_general | solution.py:70
  113.7 44.8 %all-to-all-done.1 = bf16[128,8,2048]{2,1,0:T(8,128)(2,1)} async-done(((bf16[128,8,2048]{2,1,0:T(8,128)(2,1)}), bf16[128,8,2048]{2,1,0:T(8,128)(2,1)}, u32[]{:S(2)}, u32[]{:S(2)}) %all-to-all-start.1) | async-done | bytes 4194336 | tf_op jit(solution)/shard_map/all_to_all | solution.py:52
  158.5 6.2 %fusion.6 = f32[1024,640]{1,0:T(8,128)S(1)} fusion(bf16[128,8,2048]{2,1,0:T(8,128)(2,1)} %all-to-all-done.1, f32[128,8]{1,0:T(8,128)S(1)} %bitcast.107, bf16[1,640,2048]{2,1,0:T(8,128)(2,1)} %param.15), kind=kOutput, calls=%fused_computation.9 | convolution fusion | flops 2690646016 | bytes 9441280 | tf_op jit(solution)/shard_map/dot_general | solution.py:80
  164.8 8.9 %multiply_convert_fusion = (bf16[1024,640]{1,0:T(8,128)(2,1)S(1)}, bf16[1024,640]{1,0:T(8,128)(2,1)}, bf16[1024,640]{1,0:T(8,128)(2,1)}) fusion(f32[1024,640]{1,0:T(8,128)S(1)} %copy-done.14, f32[1024,640]{1,0:T(8,128)S(1)} %fusion.6, bf16[1,2048,640]{2,1,0:T(8,128)(2,1)S(1)} %copy-done, bf16[128,8,2048]{2,1,0:T(8,128)(2,1)} %all-to-all-done.2), kind=kOutput, calls=%fused_computation.43 | convolution fusion | flops 2701393920 | bytes 15990784 | tf_op jit(solution)/shard_map/dot_general | solution.py:71
  173.6 1.2 copy-done.9
  174.8 5.4 %fusion.2 = f32[1024]{0:T(1024)S(1)} fusion(bf16[128,8,2048]{2,1,0:T(8,128)(2,1)} %all-to-all-done.1, bf16[1024,640]{1,0:T(8,128)(2,1)S(1)} %get-tuple-element.8, bf16[1,640,2048]{2,1,0:T(8,128)(2,1)S(1)} %copy-done.8), kind=kOutput, calls=%fused_computation.4 | convolution fusion | flops 2690644992 | bytes 8130560 | tf_op jit(solution)/shard_map/dot_general | solution.py:74
  180.9 5.3 %all-to-all-start.4 = ((f32[128,1,8]{2,1,0:T(1,128)}), f32[128,1,8]{2,1,0:T(1,128)S(1)}, u32[]{:S(2)}, u32[]{:S(2)}) async-start(f32[128,1,8]{2,1,0:T(1,128)} %bitcast.19), calls=%async_computation.4 | async-start | bytes 131072 | tf_op jit(solution)/shard_map/all_to_all | solution.py:92
  186.2 5.7 %fusion.45 = f32[1024,2048]{1,0:T(8,128)S(1)} fusion(bf16[1024,640]{1,0:T(8,128)(2,1)} %get-tuple-element.9, bf16[1,2048,640]{2,1,0:T(8,128)(2,1)} %param.13), kind=kOutput, calls=%fused_computation.36 | convolution fusion | flops 2684354560 | bytes 12320768 | tf_op jit(solution)/shard_map/dot_general | solution.py:85
  191.9 5.8 %add_bitcast_fusion = f32[128,8,2048]{2,1,0:T(8,128)} fusion(f32[1024,2048]{1,0:T(8,128)S(1)} %fusion.45, bf16[1024,640]{1,0:T(8,128)(2,1)S(1)} %copy-done.12, bf16[1,2048,640]{2,1,0:T(8,128)(2,1)S(1)} %copy-done), kind=kOutput, calls=%fused_computation.7 | convolution fusion | flops 2686451712 | bytes 20709376 | tf_op jit(solution)/shard_map/dot_general | solution.py:85
  197.7 10.2 %all-to-all-start.3 = ((f32[128,8,2048]{2,1,0:T(8,128)}), f32[128,8,2048]{2,1,0:T(8,128)}, u32[]{:S(2)}, u32[]{:S(2)}) async-start(f32[128,8,2048]{2,1,0:T(8,128)} %add_bitcast_fusion), calls=%async_computation.3 | async-start | bytes 16777216 | tf_op jit(solution)/shard_map/all_to_all | solution.py:91
  208.3 7.3 %fusion.32 = bf16[1,2048,640]{2,1,0:T(8,128)(2,1)} fusion(bf16[1024,640]{1,0:T(8,128)(2,1)S(1)} %copy-done.11, bf16[128,8,2048]{2,1,0:T(8,128)(2,1)} %all-to-all-done.2), kind=kOutput, calls=%fused_computation.27 | convolution fusion | flops 2685665280 | bytes 8126464 | tf_op jit(solution)/shard_map/dot_general | solution.py:83
  215.6 7.3 %fusion.29 = bf16[1,2048,640]{2,1,0:T(8,128)(2,1)} fusion(bf16[1024,640]{1,0:T(8,128)(2,1)S(1)} %copy-done.13, bf16[128,8,2048]{2,1,0:T(8,128)(2,1)} %all-to-all-done.2), kind=kOutput, calls=%fused_computation.26 | convolution fusion | flops 2685665280 | bytes 8126464 | tf_op jit(solution)/shard_map/dot_general | solution.py:84
  222.9 6.9 %fusion.35 = bf16[1,640,2048]{2,1,0:T(8,128)(2,1)} fusion(bf16[1024,640]{1,0:T(8,128)(2,1)S(1)} %copy-done.10, bf16[128,8,2048]{2,1,0:T(8,128)(2,1)} %all-to-all-done.1, f32[1024]{0:T(1024)S(1)} %reshape.124), kind=kOutput, calls=%fused_computation.28 | convolution fusion | flops 2691956736 | bytes 8130560 | tf_op jit(solution)/shard_map/dot_general | solution.py:79
  230.1 1.2 fusion.77
  231.3 79.3 %all-to-all-done.3 = f32[128,8,2048]{2,1,0:T(8,128)} async-done(((f32[128,8,2048]{2,1,0:T(8,128)}), f32[128,8,2048]{2,1,0:T(8,128)}, u32[]{:S(2)}, u32[]{:S(2)}) %all-to-all-start.3) | async-done | bytes 8388640 | tf_op jit(solution)/shard_map/all_to_all | solution.py:91
  310.6 5.8 %reduce_sum.55 = f32[32,8,2048]{2,1,0:T(8,128)} reduce(f32[4,32,8,2048]{3,2,1,0:T(8,128)} %bitcast.16, f32[]{:T(128)} %constant.3.clone.1), dimensions={0}, to_apply=%region_1.0 | reduce | flops 1572864 | bytes 10485764 | tf_op jit(solution)/shard_map/reduce_sum | solution.py:94
  316.4 4.0 convolution_bitcast_fusion
  321.4 1.2 fusion.63
  322.6 71.6 %psum.14 = f32[2048]{0:T(1024)} all-reduce(f32[2048]{0:T(1024)S(1)} %get-tuple-element.6), channel_id=1, replica_groups=mesh['dp'=4,'expert'=32] {'dp','expert'}, use_global_device_ids=true, to_apply=%region_6.0 | all-reduce | flops 2048 | bytes 16384 | tf_op jit(solution)/shard_map/psum | solution.py:102
  394.2 35.8 %all-reduce.2.cloned.1.call-done = f32[2048,32]{0,1:T(8,128)} async-done(((f32[2048,32]{0,1:T(8,128)}), f32[2048,32]{0,1:T(8,128)}) %all-reduce.2.cloned.1.call-update) | async-done | bytes 262160 | tf_op jit(solution)/shard_map/psum | solution.py:102
  430.0 1.7 copy.39
  (52 shorter events, 6.2 us)
Async XLA Ops:
  7.2 157.6 %copy-start = (bf16[1,2048,640]{2,1,0:T(8,128)(2,1)S(1)}, bf16[1,2048,640]{2,1,0:T(8,128)(2,1)}, u32[]{:S(2)}) copy-start(bf16[1,2048,640]{2,1,0:T(8,128)(2,1)} %param.14) | copy-start | bytes 7864324
  12.9 20.8 %all-to-all-start = ((bf16[128,1,8]{2,1,0:T(2,128)(2,1)}), bf16[128,1,8]{2,1,0:T(2,128)(2,1)S(1)}, u32[]{:S(2)}, u32[]{:S(2)}) async-start(bf16[128,1,8]{2,1,0:T(2,128)(2,1)} %copy.22), calls=%async_computation | async-start | bytes 131072 | tf_op jit(solution)/shard_map/all_to_all | solution.py:55
  37.4 5.9 %copy-start.3 = (bf16[128,2048]{1,0:T(8,128)(2,1)S(1)}, bf16[128,2048]{1,0:T(8,128)(2,1)}, u32[]{:S(2)}) copy-start(bf16[128,2048]{1,0:T(8,128)(2,1)} %param.10) | copy-start | bytes 1572868
  37.4 58.8 %all-to-all-start.2 = ((bf16[128,8,2048]{2,1,0:T(8,128)(2,1)}), bf16[128,8,2048]{2,1,0:T(8,128)(2,1)}, u32[]{:S(2)}, u32[]{:S(2)}) async-start(bf16[128,8,2048]{2,1,0:T(8,128)(2,1)} %bitcast.104), calls=%async_computation.2 | async-start | bytes 8388608 | tf_op jit(solution)/shard_map/all_to_all | solution.py:49
  99.9 58.6 %all-to-all-start.1 = ((bf16[128,8,2048]{2,1,0:T(8,128)(2,1)}), bf16[128,8,2048]{2,1,0:T(8,128)(2,1)}, u32[]{:S(2)}, u32[]{:S(2)}) async-start(bf16[128,8,2048]{2,1,0:T(8,128)(2,1)} %bitcast.105), calls=%async_computation.1 | async-start | bytes 8388608 | tf_op jit(solution)/shard_map/all_to_all | solution.py:52
  158.5 6.3 %copy-start.14 = (f32[1024,640]{1,0:T(8,128)S(1)}, f32[1024,640]{1,0:T(8,128)}, u32[]{:S(2)}) copy-start(f32[1024,640]{1,0:T(8,128)} %fusion.14) | copy-start | bytes 7864324
  164.7 10.0 %copy-start.8 = (bf16[1,640,2048]{2,1,0:T(8,128)(2,1)S(1)}, bf16[1,640,2048]{2,1,0:T(8,128)(2,1)}, u32[]{:S(2)}) copy-start(bf16[1,640,2048]{2,1,0:T(8,128)(2,1)} %param.15) | copy-start | bytes 7864324
  173.6 1.2 copy-start.9
  180.9 16.8 %all-to-all-start.4 = ((f32[128,1,8]{2,1,0:T(1,128)}), f32[128,1,8]{2,1,0:T(1,128)S(1)}, u32[]{:S(2)}, u32[]{:S(2)}) async-start(f32[128,1,8]{2,1,0:T(1,128)} %bitcast.19), calls=%async_computation.4 | async-start | bytes 131072 | tf_op jit(solution)/shard_map/all_to_all | solution.py:92
  186.2 5.7 %copy-start.12 = (bf16[1024,640]{1,0:T(8,128)(2,1)S(1)}, bf16[1024,640]{1,0:T(8,128)(2,1)}, u32[]{:S(2)}) copy-start(bf16[1024,640]{1,0:T(8,128)(2,1)} %get-tuple-element.10) | copy-start | bytes 3932164
  197.7 10.6 %copy-start.11 = (bf16[1024,640]{1,0:T(8,128)(2,1)S(1)}, bf16[1024,640]{1,0:T(8,128)(2,1)}, u32[]{:S(2)}) copy-start(bf16[1024,640]{1,0:T(8,128)(2,1)} %get-tuple-element.9) | copy-start | bytes 3932164
  197.7 112.9 %all-to-all-start.3 = ((f32[128,8,2048]{2,1,0:T(8,128)}), f32[128,8,2048]{2,1,0:T(8,128)}, u32[]{:S(2)}, u32[]{:S(2)}) async-start(f32[128,8,2048]{2,1,0:T(8,128)} %add_bitcast_fusion), calls=%async_computation.3 | async-start | bytes 16777216 | tf_op jit(solution)/shard_map/all_to_all | solution.py:91
  207.9 222.1 %all-reduce.2.cloned.1.call-start = ((), (), s32[]{:S(2)}) async-start(), calls=%async_computation.5 | async-start | bytes 524288 | tf_op jit(solution)/shard_map/psum | solution.py:102
  208.3 7.3 %copy-start.13 = (bf16[1024,640]{1,0:T(8,128)(2,1)S(1)}, bf16[1024,640]{1,0:T(8,128)(2,1)}, u32[]{:S(2)}) copy-start(bf16[1024,640]{1,0:T(8,128)(2,1)} %get-tuple-element.10) | copy-start | bytes 3932164
  215.6 7.3 %copy-start.10 = (bf16[1024,640]{1,0:T(8,128)(2,1)S(1)}, bf16[1024,640]{1,0:T(8,128)(2,1)}, u32[]{:S(2)}) copy-start(bf16[1024,640]{1,0:T(8,128)(2,1)} %copy-done.9) | copy-start | bytes 3932164
  222.9 7.2 %copy-start.2 = (bf16[128,2048]{1,0:T(8,128)(2,1)S(1)}, bf16[128,2048]{1,0:T(8,128)(2,1)}, u32[]{:S(2)}) copy-start(bf16[128,2048]{1,0:T(8,128)(2,1)} %param.9) | copy-start | bytes 1572868
  222.9 7.2 %copy-start.6 = (f32[2048]{0:T(1024)S(1)}, f32[2048]{0:T(1024)}, u32[]{:S(2)}) copy-start(f32[2048]{0:T(1024)} %param.11) | copy-start | bytes 24580
  310.6 5.8 %copy-start.7 = (s32[1,32,8]{1,2,0:T(8,128)S(1)}, s32[1,32,8]{1,2,0:T(8,128)}, u32[]{:S(2)}) copy-start(s32[1,32,8]{1,2,0:T(8,128)} %param.16) | copy-start | bytes 3076
  316.4 4.0 copy-start.5
  316.4 5.0 %copy-start.4 = (bf16[128,2048]{1,0:T(8,128)(2,1)S(1)}, bf16[128,2048]{1,0:T(8,128)(2,1)}, u32[]{:S(2)}) copy-start(bf16[128,2048]{1,0:T(8,128)(2,1)} %param.10) | copy-start | bytes 1572868
  316.4 115.3 %copy-start.1 = (bf16[1,2048,640]{2,1,0:T(8,128)(2,1)S(1)}, bf16[1,2048,640]{2,1,0:T(8,128)(2,1)}, u32[]{:S(2)}) copy-start(bf16[1,2048,640]{2,1,0:T(8,128)(2,1)} %param.14) | copy-start | bytes 7864324
Sparse Core Ops, SparseCore 0:
  231.4 198.5 all-reduce.1
where the time goes:
time: 439 us
  waiting for transfers between devices  217 us (49%)
  matrix products  73.4 us (17%)
  blocking collectives  71.6 us (16%)
  starting transfers between devices  38.8 us (9%)
  between operations  14.3 us (3%)
  local copies, waits for them, and re-layouts  13.1 us (3%)
  other arithmetic  10.2 us (2%)
    all_to_all x1, waiting for transfers between devices, per_device(): lax.all_to_all(dh_blocks, ('dp', 'expert'), split_axis=0, concat_axis=0,...  79.3 us
    psum x1, blocking collectives, per_device(): d_router, d_gain = lax.psum((router_term, gain_term), ('dp', 'expert'))  71.6 us
    all_to_all x1, waiting for transfers between devices, per_device(): lax.all_to_all(repeat_blocks(in_rows, n_dp), ('dp', 'expert'), split_axis...  51.4 us
    all_to_all x1, waiting for transfers between devices, per_device(): lax.all_to_all(repeat_blocks(dy_rows, n_dp), ('dp', 'expert'), split_axis...  44.8 us
    psum x1, waiting for transfers between devices, per_device(): d_router, d_gain = lax.psum((router_term, gain_term), ('dp', 'expert'))  35.8 us
    all_to_all x1, starting transfers between devices, per_device(): lax.all_to_all(repeat_blocks(gate_rows, n_dp), ('dp', 'expert'), split_ax...  11.5 us
    all_to_all x1, starting transfers between devices, per_device(): lax.all_to_all(dh_blocks, ('dp', 'expert'), split_axis=0, concat_axis=0,...  10.2 us
    dot_general x1, matrix products, per_device(): pre1 = jnp.dot(in_all, weight1, preferred_element_type=jnp.float32)  8.87 us
  transfers between devices with their start and end apart: 6, of which 5 were waited for; matrix products, arithmetic and copies ran while one was open for 14% of the time, Pallas kernels for 0%

commit v1 on v0

v1 whole, which is shorter than its diff:
```python
import functools

import jax
import jax.numpy as jnp
from jax import lax
from jax.experimental import pallas as pl
from jax.experimental.pallas import tpu as pltpu
from jax.sharding import PartitionSpec as P

F32 = jnp.float32
BF16 = jnp.bfloat16
DEAD = 2.0**100
GELU_SCALE = 0.7978845608028654
GELU_CUBIC = 0.044715


def dot(a, b, dims=((1,), (0,))):
    return lax.dot_general(a, b, (dims, ((), ())), preferred_element_type=F32)


def block_kernel(
    in_ref, dy_ref, w0_ref, w1_ref, wo_ref, rrow_ref, dh_ref, act_ref, d0_ref, d1_ref, col_ref
):
    rows = in_ref[...]
    pre0 = dot(rows, w0_ref[...])
    pre1 = dot(rows, w1_ref[...])
    up = dot(dy_ref[...], wo_ref[...], ((1,), (1,)))
    rows32 = rows.astype(F32)
    rrow = rrow_ref[...]
    logit = jnp.sum(rows32 * rrow, axis=1, keepdims=True)
    gate = 1.0 / (1.0 + jnp.exp(-logit))
    gate_row = gate.astype(BF16).astype(F32)
    square = pre0 * pre0
    tanh = jnp.tanh(GELU_SCALE * pre0 * (1.0 + GELU_CUBIC * square))
    cdf = 0.5 + 0.5 * tanh
    slope = cdf + 0.5 * pre0 * (1.0 - tanh * tanh) * (
        GELU_SCALE * (1.0 + 3.0 * GELU_CUBIC * square)
    )
    gelu = pre0 * cdf
    act = gelu * pre1
    dgate = jnp.sum(act * up, axis=1, keepdims=True)
    d_act = gate_row * up
    d0 = (d_act * pre1 * slope).astype(BF16)
    d1 = (d_act * gelu).astype(BF16)
    act_ref[...] = (gate_row * act).astype(BF16)
    d0_ref[...] = d0
    d1_ref[...] = d1
    dlogit = dgate * gate * (1.0 - gate)
    dh = dot(d0, w0_ref[...], ((1,), (1,))) + dot(d1, w1_ref[...], ((1,), (1,)))
    dh = dh + dlogit * rrow
    dh_ref[...] = dh.astype(dh_ref.dtype)
    col_ref[0:1, :] = jnp.sum(rows32 * dlogit, axis=0, keepdims=True)
    col_ref[1:2, :] = jnp.sum(rows32 * dh, axis=0, keepdims=True)


def block(rows, dy, w0, w1, wo, rrow):
    m, width = rows.shape
    hidden = w0.shape[1]
    whole = pl.BlockSpec(memory_space=pltpu.VMEM)
    return pl.pallas_call(
        block_kernel,
        out_shape=(
            jax.ShapeDtypeStruct((m, width), BF16),
            jax.ShapeDtypeStruct((m, hidden), BF16),
            jax.ShapeDtypeStruct((m, hidden), BF16),
            jax.ShapeDtypeStruct((m, hidden), BF16),
            jax.ShapeDtypeStruct((2, width), F32),
        ),
        in_specs=[whole] * 6,
        out_specs=[whole] * 5,
        compiler_params=pltpu.CompilerParams(vmem_limit_bytes=32 * 1024 * 1024),
        cost_estimate=pl.CostEstimate(
            flops=10 * m * width * hidden, bytes_accessed=6 * width * hidden, transcendentals=0
        ),
        name="block",
    )(rows, dy, w0, w1, wo, rrow)


def shift(value, axis, by):
    n = lax.axis_size(axis)
    return lax.ppermute(value, axis, [(i, (i + by) % n) for i in range(n)])


def exchange(value):
    return lax.all_to_all(value, "expert", split_axis=0, concat_axis=0, tiled=True)


def per_device(tokens, grad_out, norm_gain, router, w_in0, w_in1, w_out, slot_rows, slot_count):
    tok_dev, width = tokens.shape
    experts = router.shape[1]
    slots = slot_rows.shape[2]
    n_dp = lax.axis_size("dp")
    total = experts * slots
    live_rows = total // 2
    w0, w1, wo = w_in0[0], w_in1[0], w_out[0]

    tok_float = tokens.astype(F32)
    inv_rms = lax.rsqrt(jnp.mean(tok_float * tok_float, axis=-1, keepdims=True) + 1e-06)
    normed = (tok_float * inv_rms * norm_gain).astype(BF16)
    live = jnp.arange(slots, dtype=jnp.int32)[None, :] < slot_count[0][:, None]
    named = jnp.where(live, slot_rows[0], -1).reshape(total, 1)
    picker = (named == jnp.arange(tok_dev, dtype=jnp.int32)[None, :]).astype(BF16)
    in_slots = jnp.where(named >= 0, dot(picker, normed), DEAD).astype(BF16)
    dy_slots = dot(picker, grad_out).astype(BF16)
    in_recv = exchange(in_slots.reshape(experts, slots, width)).reshape(total, width)
    dy_recv = exchange(dy_slots.reshape(experts, slots, width)).reshape(total, width)

    alive = (in_recv[:, 0:1] < DEAD / 2).astype(BF16)
    ids = jnp.arange(total, dtype=jnp.int32)
    upto = (ids[:, None] <= ids[None, :]).astype(BF16)
    place = dot(alive, upto, ((0,), (0,)))
    place = jnp.where(alive.reshape(1, total) > 0, place, 0.0)
    wanted = jnp.arange(1, live_rows + 1, dtype=jnp.int32).astype(F32)[:, None]
    compact = (place == wanted).astype(BF16)
    in_own = dot(compact, in_recv).astype(BF16)
    dy_own = dot(compact, dy_recv).astype(BF16)

    expert = lax.axis_index("expert")
    rrow = lax.dynamic_slice_in_dim(router, expert, 1, axis=1).reshape(1, width).astype(F32)

    order = [1, n_dp - 1] + list(range(2, n_dp - 1))
    ins = [in_own] + [shift(in_own, "dp", by) for by in order]
    dys = [dy_own] + [shift(dy_own, "dp", by) for by in order]
    parts = [block(a, b, w0, w1, wo, rrow) for a, b in zip(ins, dys)]

    dh = parts[0][0].astype(F32)
    for by, part in zip(order, parts[1:]):
        dh = dh + shift(part[0], "dp", n_dp - by).astype(F32)
    back = dot(compact, dh.astype(BF16), ((0,), (0,))).astype(BF16)
    back = exchange(back.reshape(experts, slots, width)).reshape(total, width)

    small = sum(part[4] for part in parts)
    small = small + sum(shift(small, "dp", by) for by in order)
    small = exchange(jnp.broadcast_to(small[None], (experts,) + small.shape))
    d_router = small[:, 0, :].T
    d_gain = jnp.sum(small[:, 1, :], axis=0) / norm_gain

    in_all = jnp.concatenate(ins, axis=0)
    dy_all = jnp.concatenate(dys, axis=0)
    act_all, d0_all, d1_all = (jnp.concatenate([p[i] for p in parts], axis=0) for i in (1, 2, 3))
    grad_w0 = dot(in_all, d0_all, ((0,), (0,))).astype(BF16)
    grad_w1 = dot(in_all, d1_all, ((0,), (0,))).astype(BF16)
    grad_wout = dot(act_all, dy_all, ((0,), (0,))).astype(BF16)

    d_normed = dot(picker, back, ((0,), (0,)))
    scaled = d_normed * norm_gain
    d_tokens = (
        grad_out.astype(F32)
        + inv_rms * scaled
        - tok_float * inv_rms**3 * jnp.mean(scaled * tok_float, axis=-1, keepdims=True)
    )
    return (
        d_tokens.astype(BF16),
        d_gain,
        d_router,
        grad_w0[None],
        grad_w1[None],
        grad_wout[None],
    )


def solution(mesh):
    in_specs = (
        P(("dp", "expert"), None),
        P(("dp", "expert"), None),
        P(),
        P(),
        P("expert", None, "dp"),
        P("expert", None, "dp"),
        P("expert", "dp", None),
        P(("dp", "expert"), None, None),
        P(("dp", "expert"), None),
    )
    out_specs = (
        P(("dp", "expert"), None),
        P(),
        P(),
        P("expert", None, "dp"),
        P("expert", None, "dp"),
        P("expert", "dp", None),
    )
    return jax.shard_map(
        per_device, mesh=mesh, in_specs=in_specs, out_specs=out_specs, check_vma=False
    )
```

time: 439 us -> 183 us (0.42)
  waiting for transfers between devices: 217 us -> 65.1 us
  blocking collectives: 71.6 us -> 0 us
  matrix products: 73.4 us -> 26.1 us
  Pallas kernels: 0 us -> 20.5 us
  between operations: 14.3 us -> 1 us
  starting transfers between devices: 38.8 us -> 47.1 us
    all_to_all x5 -> x4, waiting for transfers between devices: 181 us -> 28.7 us  [exchange(): lax.all_to_all(value, 'expert', split_axis=0, concat_axis=0, tiled=True)]
    psum x1 -> x0, blocking collectives: 71.6 us -> none  [per_device(): d_router, d_gain = lax.psum((router_term, gain_term), ('dp', 'expert'))]
    dot_general x17 -> x10, matrix products: 73.4 us -> 26.1 us  [dot(): return lax.dot_general(a, b, (dims, ((), ())), preferred_element_type=F32)]
    ppermute x0 -> x12, waiting for transfers between devices: none -> 36.4 us  [shift(): return lax.ppermute(value, axis, [(i, (i + by) % n) for i in range(n)])]
    psum x1 -> x0, waiting for transfers between devices: 35.8 us -> none  [per_device(): d_router, d_gain = lax.psum((router_term, gain_term), ('dp', 'expert'))]
    pallas_call x0 -> x4, Pallas kernels: none -> 20.5 us  [block(): pl.pallas_call(block_kernel, out_shape=(jax.ShapeDtypeStruct((m, width),...]
    ppermute x0 -> x12, starting transfers between devices: none -> 16.6 us  [shift(): return lax.ppermute(value, axis, [(i, (i + by) % n) for i in range(n)])]
    unnamed x32 -> x88, local copies, waits for them, and re-layouts: 3.66 us -> 13.5 us
  transfers between devices with their start and end apart: 6 -> 16, of which waited for: 5 -> 8; matrix products, arithmetic and copies ran while one was open for 14% -> 15% of each run, Pallas kernels for 0% -> 9%
where the time goes in v1:
time: 183 us; the launch traced here: 182 us
  waiting for transfers between devices  65.1 us (36%)
  starting transfers between devices  47.1 us (26%)
  matrix products  26.1 us (14%)
  Pallas kernels  20.5 us (11%)
  local copies, waits for them, and re-layouts  14.8 us (8%)
  other arithmetic  7.51 us (4%)
    ppermute x12, waiting for transfers between devices, shift(): return lax.ppermute(value, axis, [(i, (i + by) % n) for i in range(n)])  36.4 us
    all_to_all x4, starting transfers between devices, exchange(): lax.all_to_all(value, 'expert', split_axis=0, concat_axis=0, tiled=True)  30.5 us
    all_to_all x4, waiting for transfers between devices, exchange(): lax.all_to_all(value, 'expert', split_axis=0, concat_axis=0, tiled=True)  28.7 us
    dot_general x10, matrix products, dot(): return lax.dot_general(a, b, (dims, ((), ())), preferred_element_type=F32)  26.1 us
    pallas_call x4, Pallas kernels, block(): pl.pallas_call(block_kernel, out_shape=(jax.ShapeDtypeStruct((m, width),...  20.5 us
    ppermute x12, starting transfers between devices, shift(): return lax.ppermute(value, axis, [(i, (i + by) % n) for i in range(n)])  16.6 us
    unnamed x88, local copies, waits for them, and re-layouts  13.5 us
  transfers between devices with their start and end apart: 16, of which 8 were waited for; matrix products, arithmetic and copies ran while one was open for 15% of the time, Pallas kernels for 9%

profile of v1, /device:TPU:1, one launch (start us, length us, event | category | flops | bytes accessed | tf_op | source)
XLA Modules:
  0.0 182.1 jit_solution(9045682520935816571)
XLA Ops:
  0.6 1.2 fusion.14
  3.6 2.5 %fusion.4 = bf16[32,8,2048]{2,1,0:T(8,128)(2,1)} fusion(pred[256]{0:T(512)(128)(4,1)S(1)} %get-tuple-element.48, bf16[128,2048]{1,0:T(8,128)(2,1)} %param.9, f32[2048]{0:T(1024)} %param.11, f32[128]{0:T(128)S(1)} %get-tuple-element.53, s32[256]{0:T(256)S(1)} %get-tuple-element.49), kind=kOutput, calls=%fused_computation.10 | convolution fusion | flops 136347648 | bytes 1582848 | tf_op jit(solution)/shard_map/dot_general | solution.py:18
  6.2 9.6 %all-to-all-start = ((bf16[32,8,2048]{2,1,0:T(8,128)(2,1)}), bf16[32,8,2048]{2,1,0:T(8,128)(2,1)S(1)}, u32[]{:S(2)}, u32[]{:S(2)}) async-start(bf16[32,8,2048]{2,1,0:T(8,128)(2,1)} %fusion.4), calls=%async_computation | async-start | bytes 2097152 | tf_op jit(solution)/shard_map/all_to_all | solution.py:85
  15.8 1.4 fusion.5
  17.2 15.5 %all-to-all-done = bf16[32,8,2048]{2,1,0:T(8,128)(2,1)S(1)} async-done(((bf16[32,8,2048]{2,1,0:T(8,128)(2,1)}), bf16[32,8,2048]{2,1,0:T(8,128)(2,1)S(1)}, u32[]{:S(2)}, u32[]{:S(2)}) %all-to-all-start) | async-done | bytes 1048608 | tf_op jit(solution)/shard_map/all_to_all | solution.py:85
  33.7 4.5 %all-to-all-start.1 = ((bf16[32,8,2048]{2,1,0:T(8,128)(2,1)}), bf16[32,8,2048]{2,1,0:T(8,128)(2,1)}, u32[]{:S(2)}, u32[]{:S(2)}) async-start(bf16[32,8,2048]{2,1,0:T(8,128)(2,1)} %fusion.5), calls=%async_computation.1 | async-start | bytes 2097152 | tf_op jit(solution)/shard_map/all_to_all | solution.py:85
  39.5 1.6 convolution_convert_fusion.6.in_ref
  41.1 1.3 collective-permute-start
  42.3 12.8 %all-to-all-done.1 = bf16[32,8,2048]{2,1,0:T(8,128)(2,1)} async-done(((bf16[32,8,2048]{2,1,0:T(8,128)(2,1)}), bf16[32,8,2048]{2,1,0:T(8,128)(2,1)}, u32[]{:S(2)}, u32[]{:S(2)}) %all-to-all-start.1) | async-done | bytes 1048608 | tf_op jit(solution)/shard_map/all_to_all | solution.py:85
  55.1 2.4 %convolution_convert_fusion.5.dy_ref = bf16[128,2048]{1,0:T(8,128)(2,1)} fusion(bf16[32,8,2048]{2,1,0:T(8,128)(2,1)} %all-to-all-done.1, f32[256]{0:T(256)S(1)} %broadcast_select_fusion, f32[128]{0:T(128)S(1)} %add_convert_fusion.2), kind=kOutput, calls=%fused_computation.14 | convolution fusion | flops 134512640 | bytes 1574400 | tf_op jit(solution)/shard_map/dot_general | solution.py:18
  57.5 1.2 collective-permute-start.1
  58.7 2.5 %collective-permute-start.6 = (bf16[128,2048]{1,0:T(8,128)(2,1)S(1)}, bf16[128,2048]{1,0:T(8,128)(2,1)S(1)}, u32[]{:S(2)}, u32[]{:S(2)}) collective-permute-start(bf16[128,2048]{1,0:T(8,128)(2,1)S(1)} %convolution_convert_fusion.6.in_ref), channel_id=1, source_target_pairs={{0,64},{32,96},{64,0},{96,32},{1,65},{33,97},{65,1},{97,33},{2,66}... | collective-permute-start | bytes 1572872 | tf_op jit(solution)/shard_map/ppermute | solution.py:81
  62.5 2.5 %collective-permute-start.4 = (bf16[128,2048]{1,0:T(8,128)(2,1)}, bf16[128,2048]{1,0:T(8,128)(2,1)S(1)}, u32[]{:S(2)}, u32[]{:S(2)}) collective-permute-start(bf16[128,2048]{1,0:T(8,128)(2,1)} %convolution_convert_fusion.5.dy_ref), channel_id=1, source_target_pairs={{0,96},{32,0},{64,32},{96,64},{1,97},{33,1},{65,33},{97,65},{2,98}... | collective-permute-start | bytes 1572872 | tf_op jit(solution)/shard_map/ppermute | solution.py:81
  65.8 1.7 copy-done.1
  67.5 1.7 copy-done.3
  69.2 5.0 %block.4 = (bf16[128,2048]{1,0:T(8,128)(2,1)S(1)}, bf16[128,640]{1,0:T(8,128)(2,1)S(1)}, bf16[128,640]{1,0:T(8,128)(2,1)S(1)}, bf16[128,640]{1,0:T(8,128)(2,1)S(1)}, f32[2,2048]{1,0:T(2,128)S(1)}) custom-call(bf16[128,2048]{1,0:T(8,128)(2,1)S(1)} %convolution_convert_fusion.6.in_ref, bf16[128,2048]{1,0:T(8,128)(2,1)} %convolution_convert_fusion.5.dy_ref, ...), custom_call_target="tpu_custom_call" | custom-call | flops 1677721600 | bytes 7864320 | tf_op jit(solution)/shard_map/block/pallas_call | solution.py:60
  75.5 6.1 %block.5 = (bf16[128,2048]{1,0:T(8,128)(2,1)}, bf16[128,640]{1,0:T(8,128)(2,1)S(1)}, bf16[128,640]{1,0:T(8,128)(2,1)S(1)}, bf16[128,640]{1,0:T(8,128)(2,1)S(1)}, f32[2,2048]{1,0:T(2,128)S(1)}) custom-call(bf16[128,2048]{1,0:T(8,128)(2,1)} %collective-permute-done.in_ref, bf16[128,2048]{1,0:T(8,128)(2,1)} %collective-permute-done.1.dy_ref, ...), custom_call_target="tpu_custom_call" | custom-call | flops 1677721600 | bytes 7864320 | tf_op jit(solution)/shard_map/block/pallas_call | solution.py:60
  83.6 22.5 %collective-permute-done.4.dy_ref = bf16[128,2048]{1,0:T(8,128)(2,1)S(1)} collective-permute-done((bf16[128,2048]{1,0:T(8,128)(2,1)}, bf16[128,2048]{1,0:T(8,128)(2,1)S(1)}, u32[]{:S(2)}, u32[]{:S(2)}) %collective-permute-start.4) | collective-permute-done | bytes 524320 | tf_op jit(solution)/shard_map/ppermute | solution.py:81
  106.1 4.7 %block.6 = (bf16[128,2048]{1,0:T(8,128)(2,1)}, bf16[128,640]{1,0:T(8,128)(2,1)S(1)}, bf16[128,640]{1,0:T(8,128)(2,1)S(1)}, bf16[128,640]{1,0:T(8,128)(2,1)S(1)}, f32[2,2048]{1,0:T(2,128)S(1)}) custom-call(bf16[128,2048]{1,0:T(8,128)(2,1)S(1)} %collective-permute-done.3.in_ref, bf16[128,2048]{1,0:T(8,128)(2,1)S(1)} %collective-permute-done.4.dy_ref, ...), custom_call_target="tpu_custom_call" | custom-call | flops 1677721600 | bytes 7864320 | tf_op jit(solution)/shard_map/block/pallas_call | solution.py:60
  112.8 4.7 %block.7 = (bf16[128,2048]{1,0:T(8,128)(2,1)}, bf16[128,640]{1,0:T(8,128)(2,1)S(1)}, bf16[128,640]{1,0:T(8,128)(2,1)S(1)}, bf16[128,640]{1,0:T(8,128)(2,1)S(1)}, f32[2,2048]{1,0:T(2,128)S(1)}) custom-call(bf16[128,2048]{1,0:T(8,128)(2,1)S(1)} %collective-permute-done.6.in_ref, bf16[128,2048]{1,0:T(8,128)(2,1)S(1)} %collective-permute-done.7.dy_ref, ...), custom_call_target="tpu_custom_call" | custom-call | flops 1677721600 | bytes 7864320 | tf_op jit(solution)/shard_map/block/pallas_call | solution.py:60
  119.6 2.8 %collective-permute-start.11 = (f32[2,2048]{1,0:T(2,128)S(1)}, f32[2,2048]{1,0:T(2,128)S(1)}, u32[]{:S(2)}, u32[]{:S(2)}) collective-permute-start(f32[2,2048]{1,0:T(2,128)S(1)} %add_add_fusion.1), channel_id=1, source_target_pairs={{0,64},{32,96},{64,0},{96,32},{1,65},{33,97},{65,1},{97,33},{2,66}... | collective-permute-start | bytes 49160 | tf_op jit(solution)/shard_map/ppermute | solution.py:81
  123.9 2.3 %collective-permute-start.2 = (bf16[128,2048]{1,0:T(8,128)(2,1)}, bf16[128,2048]{1,0:T(8,128)(2,1)S(1)}, u32[]{:S(2)}, u32[]{:S(2)}) collective-permute-start(bf16[128,2048]{1,0:T(8,128)(2,1)} %get-tuple-element.27), channel_id=1, source_target_pairs={{0,96},{32,0},{64,32},{96,64},{1,97},{33,1},{65,33},{97,65},{2,98}... | collective-permute-start | bytes 1572872 | tf_op jit(solution)/shard_map/ppermute | solution.py:81
  128.4 7.0 %all-to-all-start.3 = ((f32[32,2,2048]{2,1,0:T(2,128)}), f32[32,2,2048]{2,1,0:T(2,128)}, u32[]{:S(2)}, u32[]{:S(2)}) async-start(f32[32,2,2048]{2,1,0:T(2,128)} %broadcast_in_dim.48), calls=%async_computation.3 | async-start | bytes 1048576 | tf_op jit(solution)/shard_map/all_to_all | solution.py:85
  136.0 4.0 %collective-permute-done.5 = bf16[128,2048]{1,0:T(8,128)(2,1)S(1)} collective-permute-done((bf16[128,2048]{1,0:T(8,128)(2,1)}, bf16[128,2048]{1,0:T(8,128)(2,1)S(1)}, u32[]{:S(2)}, u32[]{:S(2)}) %collective-permute-start.5) | collective-permute-done | bytes 524320 | tf_op jit(solution)/shard_map/ppermute | solution.py:81
  140.0 8.8 %collective-permute-done.8 = bf16[128,2048]{1,0:T(8,128)(2,1)S(1)} collective-permute-done((bf16[128,2048]{1,0:T(8,128)(2,1)}, bf16[128,2048]{1,0:T(8,128)(2,1)S(1)}, u32[]{:S(2)}, u32[]{:S(2)}) %collective-permute-start.8) | collective-permute-done | bytes 524320 | tf_op jit(solution)/shard_map/ppermute | solution.py:81
  149.6 3.0 %fusion.6 = bf16[32,8,2048]{2,1,0:T(8,128)(2,1)} fusion(bf16[128,2048]{1,0:T(8,128)(2,1)} %copy-done.41, bf16[128,2048]{1,0:T(8,128)(2,1)} %copy-done.40, bf16[128,2048]{1,0:T(8,128)(2,1)} %copy-done.39, bf16[128,2048]{1,0:T(8,128)(2,1)S(1)} %copy-done.14, f32[256]{0:T(256)S(1)} %broadcast_select_fusion, f32[128]{0:T(128)S(1)} %add_convert_fusion.2), kind=kOutput, calls=%fused_computation.12 | convolution fusion | flops 136871936 | bytes 3147264 | tf_op jit(solution)/shard_map/dot_general | solution.py:18
  152.7 9.4 %all-to-all-start.2 = ((bf16[32,8,2048]{2,1,0:T(8,128)(2,1)}), bf16[32,8,2048]{2,1,0:T(8,128)(2,1)}, u32[]{:S(2)}, u32[]{:S(2)}) async-start(bf16[32,8,2048]{2,1,0:T(8,128)(2,1)} %fusion.6), calls=%async_computation.2 | async-start | bytes 2097152 | tf_op jit(solution)/shard_map/all_to_all | solution.py:85
  162.2 4.4 %fusion.2 = bf16[1,640,2048]{2,1,0:T(8,128)(2,1)} fusion(bf16[128,2048]{1,0:T(8,128)(2,1)S(1)} %copy-done.10, bf16[128,2048]{1,0:T(8,128)(2,1)S(1)} %copy-done.12, bf16[128,2048]{1,0:T(8,128)(2,1)} %collective-permute-done.1.dy_ref, bf16[128,2048]{1,0:T(8,128)(2,1)} %convolution_convert_fusion.5.dy_ref, bf16[128,640]{1,0:T(8,128)(2,1)S(1)} %copy-done.34, ...), kind=kOutput, calls=%fused_computation.5 | convolution fusion | flops 1354498048 | bytes 5373952 | tf_op jit(solution)/shard_map/dot_general | solution.py:18
  166.7 4.4 %fusion = bf16[1,2048,640]{2,1,0:T(8,128)(2,1)} fusion(bf16[128,640]{1,0:T(8,128)(2,1)S(1)} %copy-done.32, bf16[128,640]{1,0:T(8,128)(2,1)S(1)} %copy-done.26, bf16[128,640]{1,0:T(8,128)(2,1)S(1)} %copy-done.20, bf16[128,640]{1,0:T(8,128)(2,1)S(1)} %copy-done.16, bf16[128,2048]{1,0:T(8,128)(2,1)S(1)} %copy-done.6, bf16[128,2048]{1,0:T(8,128)(2,1)S(1)} %copy-done.8, ...), kind=kOutput, calls=%fused_computation.3 | convolution fusion | flops 1354498048 | bytes 5373952 | tf_op jit(solution)/shard_map/dot_general | solution.py:18
  171.1 4.4 %fusion.1 = bf16[1,2048,640]{2,1,0:T(8,128)(2,1)} fusion(bf16[128,640]{1,0:T(8,128)(2,1)S(1)} %copy-done.28, bf16[128,640]{1,0:T(8,128)(2,1)S(1)} %copy-done.22, bf16[128,640]{1,0:T(8,128)(2,1)S(1)} %get-tuple-element.39, bf16[128,640]{1,0:T(8,128)(2,1)S(1)} %get-tuple-element.38, bf16[128,2048]{1,0:T(8,128)(2,1)S(1)} %copy-done.6, ...), kind=kOutput, calls=%fused_computation.4 | convolution fusion | flops 1354498048 | bytes 5373952 | tf_op jit(solution)/shard_map/dot_general | solution.py:18
  175.5 1.7 fusion.65
  179.2 1.7 fusion.20
  (120 shorter events, 21.6 us)
Async XLA Ops:
  1.9 13.9 %copy-start.37 = (bf16[128,2048]{1,0:T(8,128)(2,1)S(1)}, bf16[128,2048]{1,0:T(8,128)(2,1)}, u32[]{:S(2)}) copy-start(bf16[128,2048]{1,0:T(8,128)(2,1)} %param.10) | copy-start | bytes 1572868
  6.2 26.5 %all-to-all-start = ((bf16[32,8,2048]{2,1,0:T(8,128)(2,1)}), bf16[32,8,2048]{2,1,0:T(8,128)(2,1)S(1)}, u32[]{:S(2)}, u32[]{:S(2)}) async-start(bf16[32,8,2048]{2,1,0:T(8,128)(2,1)} %fusion.4), calls=%async_computation | async-start | bytes 2097152 | tf_op jit(solution)/shard_map/all_to_all | solution.py:85
  33.7 21.4 %all-to-all-start.1 = ((bf16[32,8,2048]{2,1,0:T(8,128)(2,1)}), bf16[32,8,2048]{2,1,0:T(8,128)(2,1)}, u32[]{:S(2)}, u32[]{:S(2)}) async-start(bf16[32,8,2048]{2,1,0:T(8,128)(2,1)} %fusion.5), calls=%async_computation.1 | async-start | bytes 2097152 | tf_op jit(solution)/shard_map/all_to_all | solution.py:85
  38.1 27.6 %copy-start = (bf16[1,2048,640]{2,1,0:T(8,128)(2,1)S(1)}, bf16[1,2048,640]{2,1,0:T(8,128)(2,1)}, u32[]{:S(2)}) copy-start(bf16[1,2048,640]{2,1,0:T(8,128)(2,1)} %param.13) | copy-start | bytes 7864324
  41.1 21.5 %collective-permute-start = (bf16[128,2048]{1,0:T(8,128)(2,1)S(1)}, bf16[128,2048]{1,0:T(8,128)(2,1)}, u32[]{:S(2)}, u32[]{:S(2)}) collective-permute-start(bf16[128,2048]{1,0:T(8,128)(2,1)S(1)} %convolution_convert_fusion.6.in_ref), channel_id=1, source_target_pairs={{0,32},{32,64},{64,96},{96,0},{1,33},{33,65},{65,97},{97,1},{2,34}... | collective-permute-start | bytes 1572872 | tf_op jit(solution)/shard_map/ppermute | solution.py:81
  57.5 18.1 %collective-permute-start.1 = (bf16[128,2048]{1,0:T(8,128)(2,1)}, bf16[128,2048]{1,0:T(8,128)(2,1)}, u32[]{:S(2)}, u32[]{:S(2)}) collective-permute-start(bf16[128,2048]{1,0:T(8,128)(2,1)} %convolution_convert_fusion.5.dy_ref), channel_id=1, source_target_pairs={{0,32},{32,64},{64,96},{96,0},{1,33},{33,65},{65,97},{97,1},{2,34}... | collective-permute-start | bytes 1572872 | tf_op jit(solution)/shard_map/ppermute | solution.py:81
  58.7 54.1 %collective-permute-start.6 = (bf16[128,2048]{1,0:T(8,128)(2,1)S(1)}, bf16[128,2048]{1,0:T(8,128)(2,1)S(1)}, u32[]{:S(2)}, u32[]{:S(2)}) collective-permute-start(bf16[128,2048]{1,0:T(8,128)(2,1)S(1)} %convolution_convert_fusion.6.in_ref), channel_id=1, source_target_pairs={{0,64},{32,96},{64,0},{96,32},{1,65},{33,97},{65,1},{97,33},{2,66}... | collective-permute-start | bytes 1572872 | tf_op jit(solution)/shard_map/ppermute | solution.py:81
  61.1 22.5 %collective-permute-start.3 = (bf16[128,2048]{1,0:T(8,128)(2,1)S(1)}, bf16[128,2048]{1,0:T(8,128)(2,1)S(1)}, u32[]{:S(2)}, u32[]{:S(2)}) collective-permute-start(bf16[128,2048]{1,0:T(8,128)(2,1)S(1)} %convolution_convert_fusion.6.in_ref), channel_id=1, source_target_pairs={{0,96},{32,0},{64,32},{96,64},{1,97},{33,1},{65,33},{97,65},{2,98}... | collective-permute-start | bytes 1572872 | tf_op jit(solution)/shard_map/ppermute | solution.py:81
  62.3 50.5 %collective-permute-start.7 = (bf16[128,2048]{1,0:T(8,128)(2,1)}, bf16[128,2048]{1,0:T(8,128)(2,1)S(1)}, u32[]{:S(2)}, u32[]{:S(2)}) collective-permute-start(bf16[128,2048]{1,0:T(8,128)(2,1)} %convolution_convert_fusion.5.dy_ref), channel_id=1, source_target_pairs={{0,64},{32,96},{64,0},{96,32},{1,65},{33,97},{65,1},{97,33},{2,66}... | collective-permute-start | bytes 1572872 | tf_op jit(solution)/shard_map/ppermute | solution.py:81
  62.5 43.6 %collective-permute-start.4 = (bf16[128,2048]{1,0:T(8,128)(2,1)}, bf16[128,2048]{1,0:T(8,128)(2,1)S(1)}, u32[]{:S(2)}, u32[]{:S(2)}) collective-permute-start(bf16[128,2048]{1,0:T(8,128)(2,1)} %convolution_convert_fusion.5.dy_ref), channel_id=1, source_target_pairs={{0,96},{32,0},{64,32},{96,64},{1,97},{33,1},{65,33},{97,65},{2,98}... | collective-permute-start | bytes 1572872 | tf_op jit(solution)/shard_map/ppermute | solution.py:81
  75.5 30.6 %copy-start.4 = (bf16[1,640,2048]{2,1,0:T(8,128)(2,1)S(1)}, bf16[1,640,2048]{2,1,0:T(8,128)(2,1)}, u32[]{:S(2)}) copy-start(bf16[1,640,2048]{2,1,0:T(8,128)(2,1)} %param.15) | copy-start | bytes 7864324
  83.0 29.8 %copy-start.2 = (bf16[1,2048,640]{2,1,0:T(8,128)(2,1)S(1)}, bf16[1,2048,640]{2,1,0:T(8,128)(2,1)}, u32[]{:S(2)}) copy-start(bf16[1,2048,640]{2,1,0:T(8,128)(2,1)} %param.14) | copy-start | bytes 7864324
  83.6 27.2 %copy-start.7 = (bf16[128,2048]{1,0:T(8,128)(2,1)}, bf16[128,2048]{1,0:T(8,128)(2,1)S(1)}, u32[]{:S(2)}) copy-start(bf16[128,2048]{1,0:T(8,128)(2,1)S(1)} %collective-permute-done.3.in_ref) | copy-start | bytes 1572868
  119.6 30.0 %copy-start.14 = (bf16[128,2048]{1,0:T(8,128)(2,1)S(1)}, bf16[128,2048]{1,0:T(8,128)(2,1)}, u32[]{:S(2)}) copy-start(bf16[128,2048]{1,0:T(8,128)(2,1)} %copy-done.13) | copy-start | bytes 1572868
  119.6 6.6 %collective-permute-start.11 = (f32[2,2048]{1,0:T(2,128)S(1)}, f32[2,2048]{1,0:T(2,128)S(1)}, u32[]{:S(2)}, u32[]{:S(2)}) collective-permute-start(f32[2,2048]{1,0:T(2,128)S(1)} %add_add_fusion.1), channel_id=1, source_target_pairs={{0,64},{32,96},{64,0},{96,32},{1,65},{33,97},{65,1},{97,33},{2,66}... | collective-permute-start | bytes 49160 | tf_op jit(solution)/shard_map/ppermute | solution.py:81
  122.4 5.0 %collective-permute-start.10 = (f32[2,2048]{1,0:T(2,128)S(1)}, f32[2,2048]{1,0:T(2,128)S(1)}, u32[]{:S(2)}, u32[]{:S(2)}) collective-permute-start(f32[2,2048]{1,0:T(2,128)S(1)} %add_add_fusion.1), channel_id=1, source_target_pairs={{0,96},{32,0},{64,32},{96,64},{1,97},{33,1},{65,33},{97,65},{2,98}... | collective-permute-start | bytes 49160 | tf_op jit(solution)/shard_map/ppermute | solution.py:81
  123.5 3.9 %collective-permute-start.9 = (f32[2,2048]{1,0:T(2,128)S(1)}, f32[2,2048]{1,0:T(2,128)S(1)}, u32[]{:S(2)}, u32[]{:S(2)}) collective-permute-start(f32[2,2048]{1,0:T(2,128)S(1)} %add_add_fusion.1), channel_id=1, source_target_pairs={{0,32},{32,64},{64,96},{96,0},{1,33},{33,65},{65,97},{97,1},{2,34}... | collective-permute-start | bytes 49160 | tf_op jit(solution)/shard_map/ppermute | solution.py:81
  123.9 12.2 %collective-permute-start.2 = (bf16[128,2048]{1,0:T(8,128)(2,1)}, bf16[128,2048]{1,0:T(8,128)(2,1)S(1)}, u32[]{:S(2)}, u32[]{:S(2)}) collective-permute-start(bf16[128,2048]{1,0:T(8,128)(2,1)} %get-tuple-element.27), channel_id=1, source_target_pairs={{0,96},{32,0},{64,32},{96,64},{1,97},{33,1},{65,33},{97,65},{2,98}... | collective-permute-start | bytes 1572872 | tf_op jit(solution)/shard_map/ppermute | solution.py:81
  126.2 13.8 %collective-permute-start.5 = (bf16[128,2048]{1,0:T(8,128)(2,1)}, bf16[128,2048]{1,0:T(8,128)(2,1)S(1)}, u32[]{:S(2)}, u32[]{:S(2)}) collective-permute-start(bf16[128,2048]{1,0:T(8,128)(2,1)} %get-tuple-element.28), channel_id=1, source_target_pairs={{0,32},{32,64},{64,96},{96,0},{1,33},{33,65},{65,97},{97,1},{2,34}... | collective-permute-start | bytes 1572872 | tf_op jit(solution)/shard_map/ppermute | solution.py:81
  126.2 22.6 %collective-permute-start.8 = (bf16[128,2048]{1,0:T(8,128)(2,1)}, bf16[128,2048]{1,0:T(8,128)(2,1)S(1)}, u32[]{:S(2)}, u32[]{:S(2)}) collective-permute-start(bf16[128,2048]{1,0:T(8,128)(2,1)} %get-tuple-element.29), channel_id=1, source_target_pairs={{0,64},{32,96},{64,0},{96,32},{1,65},{33,97},{65,1},{97,33},{2,66}... | collective-permute-start | bytes 1572872 | tf_op jit(solution)/shard_map/ppermute | solution.py:81
  128.4 24.2 %all-to-all-start.3 = ((f32[32,2,2048]{2,1,0:T(2,128)}), f32[32,2,2048]{2,1,0:T(2,128)}, u32[]{:S(2)}, u32[]{:S(2)}) async-start(f32[32,2,2048]{2,1,0:T(2,128)} %broadcast_in_dim.48), calls=%async_computation.3 | async-start | bytes 1048576 | tf_op jit(solution)/shard_map/all_to_all | solution.py:85
  136.0 12.8 %copy-start.39 = (bf16[128,2048]{1,0:T(8,128)(2,1)}, bf16[128,2048]{1,0:T(8,128)(2,1)S(1)}, u32[]{:S(2)}) copy-start(bf16[128,2048]{1,0:T(8,128)(2,1)S(1)} %collective-permute-done.2) | copy-start | bytes 1572868
  140.0 8.8 %copy-start.40 = (bf16[128,2048]{1,0:T(8,128)(2,1)}, bf16[128,2048]{1,0:T(8,128)(2,1)S(1)}, u32[]{:S(2)}) copy-start(bf16[128,2048]{1,0:T(8,128)(2,1)S(1)} %collective-permute-done.5) | copy-start | bytes 1572868
  149.6 12.5 %copy-start.10 = (bf16[128,2048]{1,0:T(8,128)(2,1)S(1)}, bf16[128,2048]{1,0:T(8,128)(2,1)}, u32[]{:S(2)}) copy-start(bf16[128,2048]{1,0:T(8,128)(2,1)} %copy-done.9) | copy-start | bytes 1572868
  149.6 12.5 %copy-start.12 = (bf16[128,2048]{1,0:T(8,128)(2,1)S(1)}, bf16[128,2048]{1,0:T(8,128)(2,1)}, u32[]{:S(2)}) copy-start(bf16[128,2048]{1,0:T(8,128)(2,1)} %copy-done.11) | copy-start | bytes 1572868
  149.6 12.5 %copy-start.18 = (bf16[128,640]{1,0:T(8,128)(2,1)S(1)}, bf16[128,640]{1,0:T(8,128)(2,1)}, u32[]{:S(2)}) copy-start(bf16[128,640]{1,0:T(8,128)(2,1)} %copy-done.17) | copy-start | bytes 491524
  149.6 12.5 %copy-start.24 = (bf16[128,640]{1,0:T(8,128)(2,1)S(1)}, bf16[128,640]{1,0:T(8,128)(2,1)}, u32[]{:S(2)}) copy-start(bf16[128,640]{1,0:T(8,128)(2,1)} %copy-done.23) | copy-start | bytes 491524
  149.6 12.5 %copy-start.30 = (bf16[128,640]{1,0:T(8,128)(2,1)S(1)}, bf16[128,640]{1,0:T(8,128)(2,1)}, u32[]{:S(2)}) copy-start(bf16[128,640]{1,0:T(8,128)(2,1)} %copy-done.29) | copy-start | bytes 491524
  149.6 12.5 %copy-start.34 = (bf16[128,640]{1,0:T(8,128)(2,1)S(1)}, bf16[128,640]{1,0:T(8,128)(2,1)}, u32[]{:S(2)}) copy-start(bf16[128,640]{1,0:T(8,128)(2,1)} %copy-done.33) | copy-start | bytes 491524
  152.7 26.5 %all-to-all-start.2 = ((bf16[32,8,2048]{2,1,0:T(8,128)(2,1)}), bf16[32,8,2048]{2,1,0:T(8,128)(2,1)}, u32[]{:S(2)}, u32[]{:S(2)}) async-start(bf16[32,8,2048]{2,1,0:T(8,128)(2,1)} %fusion.6), calls=%async_computation.2 | async-start | bytes 2097152 | tf_op jit(solution)/shard_map/all_to_all | solution.py:85
  171.1 7.0 %copy-start.42 = (f32[2048]{0:T(1024)S(1)}, f32[2048]{0:T(1024)}, u32[]{:S(2)}) copy-start(f32[2048]{0:T(1024)} %param.11) | copy-start | bytes 24580
  171.1 8.1 %copy-start.35 = (bf16[128,2048]{1,0:T(8,128)(2,1)S(1)}, bf16[128,2048]{1,0:T(8,128)(2,1)}, u32[]{:S(2)}) copy-start(bf16[128,2048]{1,0:T(8,128)(2,1)} %param.9) | copy-start | bytes 1572868
  (27 other events, 73.0 us)

commit v2 on v1

v2 whole, which is shorter than its diff:
```python
import functools

import jax
import jax.numpy as jnp
from jax import lax
from jax.experimental import pallas as pl
from jax.experimental.pallas import tpu as pltpu
from jax.sharding import PartitionSpec as P

F32 = jnp.float32
BF16 = jnp.bfloat16
DEAD = 2.0**100
GELU_SCALE = 0.7978845608028654
GELU_CUBIC = 0.044715


def dot(a, b, dims=((1,), (0,))):
    return lax.dot_general(a, b, (dims, ((), ())), preferred_element_type=F32)


WHOLE = pl.BlockSpec(memory_space=pltpu.VMEM)
PARAMS = pltpu.CompilerParams(vmem_limit_bytes=24 * 1024 * 1024)
TAIL = 16
COST = pl.CostEstimate(flops=1, bytes_accessed=1, transcendentals=0)


def stack(refs):
    values = [ref[...] for ref in refs]
    return values[0] if len(values) == 1 else jnp.concatenate(values, axis=0)


def iota(shape, axis):
    return lax.broadcasted_iota(jnp.int32, shape, axis)


def one_hot_of_slots(slot_rows_ref, count_ref, tok_dev, copies):
    slots, experts = slot_rows_ref.shape
    total = copies * slots * experts
    mine = iota((total, experts), 1) == iota((total, experts), 0) // (copies * slots)
    names = dot(
        mine.astype(BF16), slot_rows_ref[...].astype(F32).astype(BF16), ((1,), (1,))
    )
    place = iota((total, slots), 0) % slots
    name = jnp.where(place == iota((total, slots), 1), names, 0.0)
    name = jnp.sum(name, axis=1, keepdims=True)
    count = jnp.where(mine, count_ref[...].astype(F32), 0.0)
    live = place[:, :1].astype(F32) < jnp.sum(count, axis=1, keepdims=True)
    hot = (iota((total, tok_dev), 1).astype(F32) == name) & live
    return hot.astype(BF16), live


def pick_kernel(tokens_ref, grad_ref, gain_ref, slot_rows_ref, count_ref, slots_ref, picker_ref):
    tok_dev = picker_ref.shape[1]
    slots = slot_rows_ref.shape[0]
    picker_ref[...], _ = one_hot_of_slots(slot_rows_ref, count_ref, tok_dev, 1)
    tok = tokens_ref[...].astype(F32)
    inv_rms = lax.rsqrt(jnp.mean(tok * tok, axis=1, keepdims=True) + 1e-06)
    normed = (tok * inv_rms * gain_ref[...]).astype(BF16)
    hot, live = one_hot_of_slots(slot_rows_ref, count_ref, tok_dev, 2)
    second = iota(hot.shape, 0) // slots % 2 == 1
    hot = jnp.concatenate(
        [jnp.where(second, 0.0, hot), jnp.where(second, hot, 0.0)], axis=1
    ).astype(BF16)
    rows = dot(hot, jnp.concatenate([normed, grad_ref[...]], axis=0))
    slots_ref[...] = jnp.where(live, rows, DEAD).astype(BF16)


def pick(tokens, grad_out, norm_gain, slot_rows, slot_count):
    total = slot_rows.shape[0] * slot_rows.shape[1]
    tok_dev, width = tokens.shape
    return pl.pallas_call(
        pick_kernel,
        out_shape=(
            jax.ShapeDtypeStruct((2 * total, width), BF16),
            jax.ShapeDtypeStruct((total, tok_dev), BF16),
        ),
        in_specs=[WHOLE] * 5,
        out_specs=[WHOLE] * 2,
        compiler_params=pltpu.CompilerParams(vmem_limit_bytes=56 * 1024 * 1024),
        cost_estimate=COST,
        name="pick",
    )(tokens, grad_out, norm_gain, slot_rows, slot_count)


def pack_kernel(slots, rows_ref, in_ref, dy_ref, home_ref):
    both = rows_ref.shape[0]
    total, live_rows = home_ref.shape
    rows = rows_ref[...]
    alive = jnp.broadcast_to((rows[:, :1].astype(F32) < DEAD / 2).astype(F32), (both, total))
    second = iota((both, both), 0) // slots % 2
    earlier = (iota((both, both), 1) < iota((both, both), 0)) & (
        iota((both, both), 1) // slots % 2 == second
    )
    index = dot(earlier.astype(BF16), alive.astype(BF16))
    index = index + (live_rows * second[:, :total]).astype(F32)
    wanted = iota((both, total), 1).astype(F32)
    home = ((index == wanted) & (alive > 0.0)).astype(BF16)
    live = dot(home, rows, ((0,), (0,))).astype(BF16)
    in_ref[...] = live[:live_rows]
    dy_ref[...] = live[live_rows:]
    line = iota((total, both), 0)
    source = line // slots * (2 * slots) + line % slots
    first = (iota((total, both), 1) == source).astype(BF16)
    home_ref[...] = dot(first, home[:, :live_rows]).astype(BF16)


def pack(rows, slots):
    both, width = rows.shape
    total = both // 2
    live_rows = total // 2
    return pl.pallas_call(
        functools.partial(pack_kernel, slots),
        out_shape=(
            jax.ShapeDtypeStruct((live_rows, width), BF16),
            jax.ShapeDtypeStruct((live_rows, width), BF16),
            jax.ShapeDtypeStruct((total, live_rows), BF16),
        ),
        in_specs=[WHOLE],
        out_specs=[WHOLE] * 3,
        compiler_params=PARAMS,
        cost_estimate=COST,
        name="pack",
    )(rows)


def hidden_kernel(sizes, *refs):
    pieces = sum(sizes)
    w0_ref, w1_ref = refs[pieces : pieces + 2]
    outs = refs[pieces + 2 :]
    rows = stack(refs[:pieces])
    pre0 = dot(rows, w0_ref[...])
    pre1 = dot(rows, w1_ref[...])
    square = pre0 * pre0
    tanh = jnp.tanh(GELU_SCALE * pre0 * (1.0 + GELU_CUBIC * square))
    cdf = 0.5 + 0.5 * tanh
    slope = cdf + 0.5 * pre0 * (1.0 - tanh * tanh) * (
        GELU_SCALE * (1.0 + 3.0 * GELU_CUBIC * square)
    )
    gelu = pre0 * cdf
    mix = pre1 * slope
    act = gelu * pre1
    start = 0
    for k in range(len(sizes)):
        stop = start + outs[3 * k].shape[0]
        outs[3 * k][...] = gelu[start:stop]
        outs[3 * k + 1][...] = mix[start:stop]
        outs[3 * k + 2][...] = act[start:stop]
        start = stop


def hidden(sets, w0, w1):
    width, units = w0.shape
    sizes = tuple(len(pieces) for pieces in sets)
    rows = [sum(piece.shape[0] for piece in pieces) for pieces in sets]
    flat = pl.pallas_call(
        functools.partial(hidden_kernel, sizes),
        out_shape=[jax.ShapeDtypeStruct((m, units), F32) for m in rows for _ in range(3)],
        in_specs=[WHOLE] * (sum(sizes) + 2),
        out_specs=[WHOLE] * (3 * len(sets)),
        compiler_params=PARAMS,
        cost_estimate=COST,
        name="hidden",
    )(*[piece for pieces in sets for piece in pieces], w0, w1)
    return [flat[3 * k : 3 * k + 3] for k in range(len(sets))]


def block_kernel(n_in, n_dy, outs_n, *refs):
    in_refs, dy_refs, refs = refs[:n_in], refs[n_in : n_in + n_dy], refs[n_in + n_dy :]
    gelu_ref, mix_ref, act_ref, w0_ref, w1_ref, wo_ref, rrow_ref, before_ref = refs[:8]
    outs = refs[8:]
    dh_refs = outs[:outs_n]
    actg_ref, d0_ref, d1_ref, small_ref = outs[outs_n:]
    rrow = rrow_ref[...]
    up = dot(stack(dy_refs), wo_ref[...], ((1,), (1,)))
    rows32 = stack(in_refs).astype(F32)
    logit = jnp.sum(rows32 * rrow, axis=1, keepdims=True)
    gate = 1.0 / (1.0 + jnp.exp(-logit))
    gate_row = gate.astype(BF16).astype(F32)
    act = act_ref[...]
    dgate = jnp.sum(act * up, axis=1, keepdims=True)
    d_act = gate_row * up
    d0 = (d_act * mix_ref[...]).astype(BF16)
    d1 = (d_act * gelu_ref[...]).astype(BF16)
    actg_ref[...] = (gate_row * act).astype(BF16)
    d0_ref[...] = d0
    d1_ref[...] = d1
    dlogit = dgate * gate * (1.0 - gate)
    dh = dot(d0, w0_ref[...], ((1,), (1,))) + dot(d1, w1_ref[...], ((1,), (1,)))
    dh = dh + dlogit * rrow
    col = jnp.sum(rows32 * dlogit, axis=0, keepdims=True)
    gain = jnp.sum(rows32 * dh, axis=0, keepdims=True)
    small = before_ref[...] + jnp.concatenate([col, gain], axis=0)
    small_ref[...] = small
    start = 0
    for ref in dh_refs:
        rows_here = dh.shape[0] // len(dh_refs)
        ref[:rows_here, :] = dh[start : start + rows_here].astype(BF16)
        start += rows_here
        if ref.shape[0] > rows_here:
            high = small.astype(BF16)
            low = (small - high.astype(F32)).astype(BF16)
            rest = jnp.zeros((TAIL - 4, small.shape[1]), BF16)
            ref[rows_here:, :] = jnp.concatenate([high, low, rest], axis=0)


def block(ins, dys, mids, weights, before, outs_n, tail=0):
    w0 = weights[0]
    width, units = w0.shape
    m = sum(piece.shape[0] for piece in ins)
    flat = pl.pallas_call(
        functools.partial(block_kernel, len(ins), len(dys), outs_n),
        out_shape=[jax.ShapeDtypeStruct((m // outs_n + tail, width), BF16)] * outs_n
        + [jax.ShapeDtypeStruct((m, units), BF16)] * 3
        + [jax.ShapeDtypeStruct((2, width), F32)],
        in_specs=[WHOLE] * (len(ins) + len(dys) + 8),
        out_specs=[WHOLE] * (outs_n + 4),
        compiler_params=PARAMS,
        cost_estimate=COST,
        name="block",
    )(*ins, *dys, *mids, *weights, before)
    return flat[:outs_n], flat[outs_n : outs_n + 3], flat[-1]


def expand_kernel(own_ref, after_ref, before_ref, far_ref, home_ref, small_ref, *refs):
    *others, out_ref = refs
    rows, width = own_ref.shape
    dh = sum(ref[...].astype(F32) for ref in (own_ref, after_ref, before_ref))
    dh = dh + far_ref[:rows, :].astype(F32)
    out_ref[:, :width] = dot(home_ref[...], dh.astype(BF16)).astype(BF16)
    carried = far_ref[rows:, :].astype(F32)
    small = small_ref[...] + carried[0:2] + carried[2:4]
    for ref in others:
        small = small + ref[...]
    part = out_ref.shape[1] - width
    lines = [small[k : k + 1, at : at + part] for k in range(2) for at in range(0, width, part)]
    lines = jnp.concatenate(lines, axis=0).astype(BF16)
    out_ref[:, width:] = jnp.concatenate([lines] * (out_ref.shape[0] // lines.shape[0]), axis=0)


def expand(own, after, before, far, home, slots, *smalls):
    total = home.shape[0]
    width = own.shape[1]
    return pl.pallas_call(
        expand_kernel,
        out_shape=jax.ShapeDtypeStruct((total, width + 2 * width // slots), BF16),
        in_specs=[WHOLE] * (5 + len(smalls)),
        out_specs=WHOLE,
        compiler_params=PARAMS,
        cost_estimate=COST,
        name="expand",
    )(own, after, before, far, home, *smalls)


def finish_kernel(
    back_ref, picker_ref, tokens_ref, grad_ref, gain_ref, d_tokens_ref, d_gain_ref, d_router_ref
):
    total = back_ref.shape[0]
    width = tokens_ref.shape[1]
    experts = d_router_ref.shape[0]
    slots = total // experts
    half = slots // 2
    part = back_ref.shape[1] - width
    gain = gain_ref[...]
    tok = tokens_ref[...].astype(F32)
    inv_rms = lax.rsqrt(jnp.mean(tok * tok, axis=1, keepdims=True) + 1e-06)
    d_normed = dot(picker_ref[...], back_ref[:, :width], ((0,), (0,)))
    scaled = d_normed * gain
    inner = jnp.mean(scaled * tok, axis=1, keepdims=True)
    d_tokens_ref[...] = (
        grad_ref[...].astype(F32) + inv_rms * scaled - tok * (inv_rms * inv_rms * inv_rms * inner)
    ).astype(BF16)
    extra = back_ref[:, width:]
    slot = lax.broadcasted_iota(jnp.int32, (experts, total), 1)
    home = slots * lax.broadcasted_iota(jnp.int32, (experts, total), 0)
    place = lax.broadcasted_iota(jnp.int32, (slots, total), 1) % slots
    line = lax.broadcasted_iota(jnp.int32, (slots, total), 0)
    sums = dot((place == line).astype(BF16), extra)
    for q in range(half):
        at = slice(q * part, (q + 1) * part)
        d_router_ref[:, at] = dot((slot == home + q).astype(BF16), extra)
        d_gain_ref[:, at] = sums[half + q : half + q + 1, :] / gain[:, at]


def finish(back, picker, tokens, grad_out, norm_gain, experts):
    width = tokens.shape[1]
    return pl.pallas_call(
        finish_kernel,
        out_shape=(
            jax.ShapeDtypeStruct(tokens.shape, BF16),
            jax.ShapeDtypeStruct((1, width), F32),
            jax.ShapeDtypeStruct((experts, width), F32),
        ),
        in_specs=[WHOLE] * 5,
        out_specs=[WHOLE] * 3,
        compiler_params=PARAMS,
        cost_estimate=COST,
        name="finish",
    )(back, picker, tokens, grad_out, norm_gain)


def in_grads_kernel(n, *refs):
    w0_ref, w1_ref, pair_ref = refs[-3:]
    grads = refs[n:-3]
    units = w0_ref.shape[1]

    @pl.when(pl.program_id(0) == 0)
    def _():
        pair_ref[:, :units] = stack(grads[0::2])
        pair_ref[:, units:] = stack(grads[1::2])

    pair = dot(stack(refs[:n]), pair_ref[...], ((0,), (0,)))
    w0_ref[...] = pair[:, :units].astype(BF16)
    w1_ref[...] = pair[:, units:].astype(BF16)


def out_grad_kernel(n, *refs):
    wo_ref, act_ref = refs[-2:]

    @pl.when(pl.program_id(0) == 0)
    def _():
        act_ref[...] = stack(refs[n:-2]).T

    wo_ref[...] = dot(act_ref[...], stack(refs[:n])).astype(BF16)


def weight_grads(kernel, pieces, factors, outs, scratch, tile=512):
    width = pieces[0].shape[1]
    return pl.pallas_call(
        functools.partial(kernel, len(pieces)),
        grid=(width // tile,),
        out_shape=[jax.ShapeDtypeStruct(shape, BF16) for shape in outs],
        in_specs=[pl.BlockSpec((piece.shape[0], tile), lambda i: (0, i)) for piece in pieces]
        + [pl.BlockSpec(value.shape, lambda i: (0, 0)) for value in factors],
        out_specs=[
            pl.BlockSpec((tile, shape[1]), lambda i: (i, 0))
            if shape[0] == width
            else pl.BlockSpec((shape[0], tile), lambda i: (0, i))
            for shape in outs
        ],
        scratch_shapes=[pltpu.VMEM(scratch, BF16)],
        compiler_params=PARAMS,
        cost_estimate=pl.CostEstimate(flops=1000000000, bytes_accessed=1, transcendentals=0),
        name="weight_grads",
    )(*pieces, *factors)


def shift(value, axis, by):
    n = lax.axis_size(axis)
    return lax.ppermute(value, axis, [(i, (i + by) % n) for i in range(n)])


def exchange(value):
    return lax.all_to_all(value, "expert", split_axis=0, concat_axis=0, tiled=True)


def pass_on(after, before):
    half = after.shape[0] // 2
    return [shift(after[:half], "dp", 1), shift(before[half:], "dp", -1)]


def per_device(tokens, grad_out, norm_gain, router, w_in0, w_in1, w_out, slot_rows, slot_count):
    tok_dev, width = tokens.shape
    experts = router.shape[1]
    slots = slot_rows.shape[2]
    total = experts * slots
    w0, w1, wo = w_in0[0], w_in1[0], w_out[0]

    expert = lax.axis_index("expert")
    rrow = lax.dynamic_slice_in_dim(router.T, expert, 1, axis=0).astype(F32)
    both, picker = pick(
        tokens, grad_out, norm_gain.reshape(1, width), slot_rows[0].T, slot_count
    )
    both = exchange(both.reshape(experts, 2 * slots, width)).reshape(2 * total, width)
    both, rrow = lax.optimization_barrier((both, rrow))
    in_own, dy_own, home = pack(both, slots)
    in_near = [shift(in_own, "dp", by) for by in (1, -1)]
    dy_near = [shift(dy_own, "dp", by) for by in (1, -1)]
    in_far = pass_on(*in_near)
    weights = (w0, w1, wo, rrow)
    mids_own, mids_near = hidden([[in_own], in_near], w0, w1)
    start = jnp.zeros((2, width), F32)
    (dh_own,), grads_own, small = block([in_own], [dy_own], mids_own, weights, start, 1)
    dy_near, small = lax.optimization_barrier((dy_near, small))
    dy_far = pass_on(*dy_near)
    dh_near, grads_near, small = block(in_near, dy_near, mids_near, weights, small, 2)
    in_far, small = lax.optimization_barrier((in_far, small))
    (mids_far,) = hidden([in_far], w0, w1)
    (dh_far,), grads_far, small = block(in_far, dy_far, mids_far, weights, small, 1, TAIL)
    back_near = [shift(dh_near[0], "dp", -1), shift(dh_near[1], "dp", 1)]
    back_far = shift(dh_far, "dp", 2)
    smalls = [small, shift(small, "dp", 1), shift(small, "dp", -1)]

    grads = (*grads_own, *grads_near, *grads_far)
    rows, units = sum(part.shape[0] for part in grads[0::3]), w0.shape[1]
    grad_w0, grad_w1 = weight_grads(
        in_grads_kernel,
        [in_own] + in_near + in_far,
        [part for k, part in enumerate(grads) if k % 3],
        [w0.shape, w1.shape],
        (rows, 2 * units),
    )
    acts, back_near = lax.optimization_barrier((grads[0::3], back_near))
    (grad_wout,) = weight_grads(
        out_grad_kernel, [dy_own] + dy_near + dy_far, list(acts), [wo.shape], (units, rows)
    )
    back_far, grad_w0, grad_w1, grad_wout = lax.optimization_barrier(
        (back_far, grad_w0, grad_w1, grad_wout)
    )

    back = expand(dh_own, *back_near, back_far, home, slots, *smalls)
    back = exchange(back.reshape(experts, slots, -1)).reshape(total, -1)
    d_tokens, d_gain, d_router = finish(
        back, picker, tokens, grad_out, norm_gain.reshape(1, width), experts
    )
    return (
        d_tokens,
        d_gain.reshape(width),
        d_router.T,
        grad_w0[None],
        grad_w1[None],
        grad_wout[None],
    )


def solution(mesh):
    in_specs = (
        P(("dp", "expert"), None),
        P(("dp", "expert"), None),
        P(),
        P(),
        P("expert", None, "dp"),
        P("expert", None, "dp"),
        P("expert", "dp", None),
        P(("dp", "expert"), None, None),
        P(("dp", "expert"), None),
    )
    out_specs = (
        P(("dp", "expert"), None),
        P(),
        P(),
        P("expert", None, "dp"),
        P("expert", None, "dp"),
        P("expert", "dp", None),
    )
    return jax.shard_map(
        per_device, mesh=mesh, in_specs=in_specs, out_specs=out_specs, check_vma=False
    )
```

time: 183 us -> 136 us (0.74)
  blocking collectives: 0 us -> 27.5 us
  matrix products: 26.1 us -> 0 us
  starting transfers between devices: 47.1 us -> 27.3 us
  waiting for transfers between devices: 65.1 us -> 46.9 us
  local copies, waits for them, and re-layouts: 14.8 us -> 1.85 us
  Pallas kernels: 20.5 us -> 30.1 us
  other arithmetic: 7.51 us -> 0.92 us
    all_to_all x0 -> x1, blocking collectives: none -> 27.5 us  [exchange(): lax.all_to_all(value, 'expert', split_axis=0, concat_axis=0, tiled=True)]
    dot_general x10 -> x0, matrix products: 26.1 us -> none  [dot(): return lax.dot_general(a, b, (dims, ((), ())), preferred_element_type=F32)]
    all_to_all x4 -> x1, starting transfers between devices: 30.5 us -> 9.66 us  [exchange(): lax.all_to_all(value, 'expert', split_axis=0, concat_axis=0, tiled=True)]
    ppermute x12 -> x13, waiting for transfers between devices: 36.4 us -> 19.5 us  [shift(): return lax.ppermute(value, axis, [(i, (i + by) % n) for i in range(n)])]
    unnamed x88 -> x14, local copies, waits for them, and re-layouts: 13.5 us -> 1.77 us
    pallas_call x4 -> x11, Pallas kernels: 20.5 us -> 30.1 us  [the longest x3 9.5 us: block(): pl.pallas_call(functools.partial(block_kernel, len(ins), len(dys), outs_n...]
    lt x2 -> x0, other arithmetic: 1.93 us -> none  [the longest x1 1.14 us: per_device(): alive = (in_recv[:, 0:1] < DEAD / 2).astype(BF16)]
    all_to_all x4 -> x1, waiting for transfers between devices: 28.7 us -> 27.4 us  [exchange(): lax.all_to_all(value, 'expert', split_axis=0, concat_axis=0, tiled=True)]
  transfers between devices with their start and end apart: 16 -> 14, of which waited for: 8 -> 5; matrix products, arithmetic and copies ran while one was open for 15% -> 1% of each run, Pallas kernels for 9% -> 16%
where the time goes in v2:
time: 136 us
  waiting for transfers between devices  46.9 us (34%)
  Pallas kernels  30.1 us (22%)
  blocking collectives  27.5 us (20%)
  starting transfers between devices  27.3 us (20%)
  local copies, waits for them, and re-layouts  1.85 us (1%)
    all_to_all x1, blocking collectives, exchange(): lax.all_to_all(value, 'expert', split_axis=0, concat_axis=0, tiled=True)  27.5 us
    all_to_all x1, waiting for transfers between devices, exchange(): lax.all_to_all(value, 'expert', split_axis=0, concat_axis=0, tiled=True)  27.4 us
    ppermute x13, waiting for transfers between devices, shift(): return lax.ppermute(value, axis, [(i, (i + by) % n) for i in range(n)])  19.5 us
    ppermute x13, starting transfers between devices, shift(): return lax.ppermute(value, axis, [(i, (i + by) % n) for i in range(n)])  17.7 us
    all_to_all x1, starting transfers between devices, exchange(): lax.all_to_all(value, 'expert', split_axis=0, concat_axis=0, tiled=True)  9.66 us
    pallas_call x3, Pallas kernels, block(): pl.pallas_call(functools.partial(block_kernel, len(ins), len(dys), outs_n...  9.5 us
    pallas_call x2, Pallas kernels, weight_grads(): pl.pallas_call(functools.partial(kernel, len(pieces)), grid=(width // til...  8.47 us
    pallas_call x2, Pallas kernels, hidden(): pl.pallas_call(functools.partial(hidden_kernel, sizes), out_shape=[jax.Sh...  3.67 us
  transfers between devices with their start and end apart: 14, of which 5 were waited for; matrix products, arithmetic and copies ran while one was open for 1% of the time, Pallas kernels for 16%

profile of v2, /device:TPU:1, one launch (start us, length us, event | category | flops | bytes accessed | tf_op | source)
XLA Modules:
  0.0 135.5 jit_solution(5744437990995363930)
XLA Ops:
  0.6 3.6 %pick.1 = (bf16[512,2048]{1,0:T(8,128)(2,1)}, bf16[256,128]{1,0:T(8,128)(2,1)}) custom-call(bf16[128,2048]{1,0:T(8,128)(2,1)} %tokens_ref.3, bf16[128,2048]{1,0:T(8,128)(2,1)} %grad_ref.3, f32[1,2048]{1,0:T(1,128)} %bitcast.34, s32[8,32]{1,0:T(8,128)} %bitcast.38, s32[1,32]{1,0:T(1,128)} %count_ref.1), custom_call_target="tpu_custom_call" | custom-call | flops 1 | bytes 1 | tf_op jit(solution)/shard_map/pick/pallas_call | solution.py:71
  4.2 9.7 %all-to-all-start = ((bf16[32,16,2048]{2,1,0:T(8,128)(2,1)}), bf16[32,16,2048]{2,1,0:T(8,128)(2,1)}, u32[]{:S(2)}, u32[]{:S(2)}) async-start(bf16[32,16,2048]{2,1,0:T(8,128)(2,1)} %bitcast.37), calls=%async_computation | async-start | bytes 4194304 | tf_op jit(solution)/shard_map/all_to_all | solution.py:353
  13.9 0.9 bitcast_convert_fusion.refs_8_.refs_10_
  14.8 27.4 %all-to-all-done = bf16[32,16,2048]{2,1,0:T(8,128)(2,1)} async-done(((bf16[32,16,2048]{2,1,0:T(8,128)(2,1)}), bf16[32,16,2048]{2,1,0:T(8,128)(2,1)}, u32[]{:S(2)}, u32[]{:S(2)}) %all-to-all-start) | async-done | bytes 2097184 | tf_op jit(solution)/shard_map/all_to_all | solution.py:353
  42.2 2.9 %pack.1 = (bf16[128,2048]{1,0:T(8,128)(2,1)S(1)}, bf16[128,2048]{1,0:T(8,128)(2,1)S(1)}, bf16[256,128]{1,0:T(8,128)(2,1)S(1)}) custom-call(bf16[512,2048]{1,0:T(8,128)(2,1)} %bitcast.4.rows_ref), custom_call_target="tpu_custom_call" | custom-call | flops 1 | bytes 1 | tf_op jit(solution)/shard_map/pack/pallas_call | solution.py:111
  45.2 1.3 collective-permute-start
  46.5 1.5 %collective-permute-start.1 = (bf16[128,2048]{1,0:T(8,128)(2,1)S(1)}, bf16[128,2048]{1,0:T(8,128)(2,1)S(1)}, u32[]{:S(2)}, u32[]{:S(2)}) collective-permute-start(bf16[128,2048]{1,0:T(8,128)(2,1)S(1)} %get-tuple-element.60.refs_0_), channel_id=1, source_target_pairs={{0,96},{32,0},{64,32},{96,64},{1,97},{33,1},{65,33},{97,65},{2,98}... | collective-permute-start | bytes 1572872 | tf_op jit(solution)/shard_map/ppermute | solution.py:349
  47.9 2.7 %collective-permute-start.3 = (bf16[128,2048]{1,0:T(8,128)(2,1)S(1)}, bf16[128,2048]{1,0:T(8,128)(2,1)S(1)}, u32[]{:S(2)}, u32[]{:S(2)}) collective-permute-start(bf16[128,2048]{1,0:T(8,128)(2,1)S(1)} %get-tuple-element.61.refs_1_.refs_0_), channel_id=1, source_target_pairs={{0,96},{32,0},{64,32},{96,64},{1,97},{33,1},{65,33},{97,65},{2,98}... | collective-permute-start | bytes 1572872 | tf_op jit(solution)/shard_map/ppermute | solution.py:349
  50.6 8.4 %collective-permute-done.refs_1_.refs_0_ = bf16[128,2048]{1,0:T(8,128)(2,1)S(1)} collective-permute-done((bf16[128,2048]{1,0:T(8,128)(2,1)S(1)}, bf16[128,2048]{1,0:T(8,128)(2,1)S(1)}, u32[]{:S(2)}, u32[]{:S(2)}) %collective-permute-start) | collective-permute-done | bytes 524320 | tf_op jit(solution)/shard_map/ppermute | solution.py:349
  59.0 0.1 collective-permute-start.4
  59.2 2.7 %collective-permute-start.5 = (bf16[64,2048]{1,0:T(8,128)(2,1)S(1)}, bf16[64,2048]{1,0:T(8,128)(2,1)S(1)}, u32[]{:S(2)}, u32[]{:S(2)}) collective-permute-start(bf16[64,2048]{1,0:T(8,128)(2,1)S(1)} %slice.17), channel_id=1, source_target_pairs={{0,96},{32,0},{64,32},{96,64},{1,97},{33,1},{65,33},{97,65},{2,98}... | collective-permute-start | bytes 786440 | tf_op jit(solution)/shard_map/ppermute | solution.py:349
  61.9 1.7 %copy-done.1 = bf16[1,2048,640]{2,1,0:T(8,128)(2,1)S(1)} copy-done((bf16[1,2048,640]{2,1,0:T(8,128)(2,1)S(1)}, bf16[1,2048,640]{2,1,0:T(8,128)(2,1)}, u32[]{:S(2)}) %copy-start.1) | copy-done | bytes 2621464
  63.6 2.7 %hidden.2 = (f32[128,640]{1,0:T(8,128)S(1)}, f32[128,640]{1,0:T(8,128)S(1)}, f32[128,640]{1,0:T(8,128)S(1)}, f32[256,640]{1,0:T(8,128)S(1)}, f32[256,640]{1,0:T(8,128)S(1)}, /*index=5*/f32[256,640]{1,0:T(8,128)S(1)}) custom-call(bf16[128,2048]{1,0:T(8,128)(2,1)S(1)} %get-tuple-element.60.refs_0_, bf16[128,2048]{1,0:T(8,128)(2,1)S(1)} %collective-permute-done.refs_1_.refs_0_, ...), custom_call_target="tpu_custom_call" | custom-call | flops 1 | bytes 1 | tf_op jit(solution)/shard_map/hidden/pallas_call | solution.py:155
  66.3 3.0 %block.3 = (bf16[128,2048]{1,0:T(8,128)(2,1)S(1)}, bf16[128,640]{1,0:T(8,128)(2,1)S(1)}, bf16[128,640]{1,0:T(8,128)(2,1)S(1)}, bf16[128,640]{1,0:T(8,128)(2,1)S(1)}, f32[2,2048]{1,0:T(2,128)S(1)}) custom-call(bf16[128,2048]{1,0:T(8,128)(2,1)S(1)} %get-tuple-element.60.refs_0_, bf16[128,2048]{1,0:T(8,128)(2,1)S(1)} %get-tuple-element.61.refs_1_.refs_0_, ...), custom_call_target="tpu_custom_call" | custom-call | flops 1 | bytes 1 | tf_op jit(solution)/shard_map/block/pallas_call | solution.py:210
  69.3 1.0 collective-permute-done.2.refs_2_.refs_1_
  70.3 1.0 collective-permute-start.6
  71.3 2.0 %collective-permute-start.7 = (bf16[64,2048]{1,0:T(8,128)(2,1)S(1)}, bf16[64,2048]{1,0:T(8,128)(2,1)S(1)}, u32[]{:S(2)}, u32[]{:S(2)}) collective-permute-start(bf16[64,2048]{1,0:T(8,128)(2,1)S(1)} %slice.15), channel_id=1, source_target_pairs={{0,96},{32,0},{64,32},{96,64},{1,97},{33,1},{65,33},{97,65},{2,98}... | collective-permute-start | bytes 786440 | tf_op jit(solution)/shard_map/ppermute | solution.py:349
  73.3 3.6 %block.4 = (bf16[128,2048]{1,0:T(8,128)(2,1)S(1)}, bf16[128,2048]{1,0:T(8,128)(2,1)S(1)}, bf16[256,640]{1,0:T(8,128)(2,1)S(1)}, bf16[256,640]{1,0:T(8,128)(2,1)S...) custom-call(bf16[128,2048]{1,0:T(8,128)(2,1)S(1)} %collective-permute-done.refs_1_.refs_0_, ...), custom_call_target="tpu_custom_call" | custom-call | flops 1 | bytes 1 | tf_op jit(solution)/shard_map/block/pallas_call | solution.py:210
  76.9 1.2 collective-permute-start.8
  78.1 0.3 collective-permute-start.9
  78.4 1.0 hidden.3
  79.4 2.1 %collective-permute-done.6.refs_2_.refs_3_ = bf16[64,2048]{1,0:T(8,128)(2,1)S(1)} collective-permute-done((bf16[64,2048]{1,0:T(8,128)(2,1)S(1)}, bf16[64,2048]{1,0:T(8,128)(2,1)S(1)}, u32[]{:S(2)}, u32[]{:S(2)}) %collective-permute-start.6) | collective-permute-done | bytes 262176 | tf_op jit(solution)/shard_map/ppermute | solution.py:349
  81.5 3.0 %block.5 = (bf16[144,2048]{1,0:T(8,128)(2,1)S(1)}, bf16[128,640]{1,0:T(8,128)(2,1)S(1)}, bf16[128,640]{1,0:T(8,128)(2,1)S(1)}, bf16[128,640]{1,0:T(8,128)(2,1)S(1)}, f32[2,2048]{1,0:T(2,128)S(1)}) custom-call(bf16[64,2048]{1,0:T(8,128)(2,1)S(1)} %collective-permute-done.4.refs_0_.refs_3_, bf16[64,2048]{1,0:T(8,128)(2,1)S(1)} %collective-permute-done.5.refs_1_.refs_4_, ...), custom_call_target="tpu_custom_call" | custom-call | flops 1 | bytes 1 | tf_op jit(solution)/shard_map/block/pallas_call | solution.py:210
  84.5 2.2 %collective-permute-start.10 = (bf16[144,2048]{1,0:T(8,128)(2,1)S(1)}, bf16[144,2048]{1,0:T(8,128)(2,1)S(1)}, u32[]{:S(2)}, u32[]{:S(2)}) collective-permute-start(bf16[144,2048]{1,0:T(8,128)(2,1)S(1)} %get-tuple-element.88), channel_id=1, source_target_pairs={{0,64},{32,96},{64,0},{96,32},{1,65},{33,97},{65,1},{97,33},{2,66}... | collective-permute-start | bytes 1769480 | tf_op jit(solution)/shard_map/ppermute | solution.py:349
  86.7 0.8 collective-permute-start.11
  87.5 1.9 %collective-permute-start.12 = (f32[2,2048]{1,0:T(2,128)S(1)}, f32[2,2048]{1,0:T(2,128)S(1)}, u32[]{:S(2)}, u32[]{:S(2)}) collective-permute-start(f32[2,2048]{1,0:T(2,128)S(1)} %get-tuple-element.102.small_ref), channel_id=1, source_target_pairs={{0,96},{32,0},{64,32},{96,64},{1,97},{33,1},{65,33},{97,65},{2,98}... | collective-permute-start | bytes 49160 | tf_op jit(solution)/shard_map/ppermute | solution.py:349
  89.4 4.8 %weight_grads.2 = (bf16[2048,640]{1,0:T(8,128)(2,1)}, bf16[2048,640]{1,0:T(8,128)(2,1)}) custom-call(bf16[128,2048]{1,0:T(8,128)(2,1)S(1)} %get-tuple-element.60.refs_0_, bf16[128,2048]{1,0:T(8,128)(2,1)S(1)} %collective-permute-done.refs_1_.refs_0_, bf16[128,2048]{1,0:T(8,128)(2,1)S(1)} %collective-permute-done.1.refs_2_.refs_1_, ...), custom_call_target="tpu_custom_call" | custom-call | flops 1000000000 | bytes 1 | tf_op jit(solution)/shard_map/weight_grads/pallas_call | solution.py:328
  94.2 3.6 %weight_grads.3 = bf16[640,2048]{1,0:T(8,128)(2,1)} custom-call(bf16[128,2048]{1,0:T(8,128)(2,1)S(1)} %get-tuple-element.61.refs_1_.refs_0_, bf16[128,2048]{1,0:T(8,128)(2,1)S(1)} %collective-permute-done.2.refs_2_.refs_1_, bf16[128,2048]{1,0:T(8,128)(2,1)S(1)} %collective-permute-done.3.refs_3_.refs_2_, ...), custom_call_target="tpu_custom_call" | custom-call | flops 1000000000 | bytes 1 | tf_op jit(solution)/shard_map/weight_grads/pallas_call | solution.py:328
  97.9 8.0 %collective-permute-done.10.far_ref = bf16[144,2048]{1,0:T(8,128)(2,1)S(1)} collective-permute-done((bf16[144,2048]{1,0:T(8,128)(2,1)S(1)}, bf16[144,2048]{1,0:T(8,128)(2,1)S(1)}, u32[]{:S(2)}, u32[]{:S(2)}) %collective-permute-start.10) | collective-permute-done | bytes 589856 | tf_op jit(solution)/shard_map/ppermute | solution.py:349
  106.0 0.5 expand.1
  106.4 27.5 %all_to_all.10 = bf16[32,8,2560]{2,1,0:T(8,128)(2,1)S(1)} all-to-all(bf16[32,8,2560]{2,1,0:T(8,128)(2,1)S(1)} %bitcast.32), channel_id=1, replica_groups=mesh['dp'=4,'expert'=32] {'expert'}, dimensions={0} | all-to-all | bytes 2621440 | tf_op jit(solution)/shard_map/all_to_all | solution.py:353
  134.0 1.5 %finish.1 = (bf16[128,2048]{1,0:T(8,128)(2,1)}, f32[1,2048]{1,0:T(1,128)}, f32[32,2048]{1,0:T(8,128)}) custom-call(bf16[256,2560]{1,0:T(8,128)(2,1)S(1)} %bitcast.33, bf16[256,128]{1,0:T(8,128)(2,1)S(1)} %copy-done.5, bf16[128,2048]{1,0:T(8,128)(2,1)S(1)} %copy-done.3, bf16[128,2048]{1,0:T(8,128)(2,1)S(1)} %copy-done.4, f32[1,2048]{1,0:T(1,128)S(1)} %bitcast.35), custom_call_target="tpu_custom_call" | custom-call | flops 1 | bytes 1 | tf_op jit(solution)/shard_map/finish/pallas_call | solution.py:286
  (28 shorter events, 0.1 us)
Async XLA Ops:
  4.2 38.0 %all-to-all-start = ((bf16[32,16,2048]{2,1,0:T(8,128)(2,1)}), bf16[32,16,2048]{2,1,0:T(8,128)(2,1)}, u32[]{:S(2)}, u32[]{:S(2)}) async-start(bf16[32,16,2048]{2,1,0:T(8,128)(2,1)} %bitcast.37), calls=%async_computation | async-start | bytes 4194304 | tf_op jit(solution)/shard_map/all_to_all | solution.py:353
  13.9 48.0 %copy-start = (bf16[1,2048,640]{2,1,0:T(8,128)(2,1)S(1)}, bf16[1,2048,640]{2,1,0:T(8,128)(2,1)}, u32[]{:S(2)}) copy-start(bf16[1,2048,640]{2,1,0:T(8,128)(2,1)} %param.13) | copy-start | bytes 7864324
  45.2 13.9 %collective-permute-start = (bf16[128,2048]{1,0:T(8,128)(2,1)S(1)}, bf16[128,2048]{1,0:T(8,128)(2,1)S(1)}, u32[]{:S(2)}, u32[]{:S(2)}) collective-permute-start(bf16[128,2048]{1,0:T(8,128)(2,1)S(1)} %get-tuple-element.60.refs_0_), channel_id=1, source_target_pairs={{0,32},{32,64},{64,96},{96,0},{1,33},{33,65},{65,97},{97,1},{2,34}... | collective-permute-start | bytes 1572872 | tf_op jit(solution)/shard_map/ppermute | solution.py:349
  46.5 12.7 %collective-permute-start.1 = (bf16[128,2048]{1,0:T(8,128)(2,1)S(1)}, bf16[128,2048]{1,0:T(8,128)(2,1)S(1)}, u32[]{:S(2)}, u32[]{:S(2)}) collective-permute-start(bf16[128,2048]{1,0:T(8,128)(2,1)S(1)} %get-tuple-element.60.refs_0_), channel_id=1, source_target_pairs={{0,96},{32,0},{64,32},{96,64},{1,97},{33,1},{65,33},{97,65},{2,98}... | collective-permute-start | bytes 1572872 | tf_op jit(solution)/shard_map/ppermute | solution.py:349
  47.9 22.3 %collective-permute-start.2 = (bf16[128,2048]{1,0:T(8,128)(2,1)S(1)}, bf16[128,2048]{1,0:T(8,128)(2,1)S(1)}, u32[]{:S(2)}, u32[]{:S(2)}) collective-permute-start(bf16[128,2048]{1,0:T(8,128)(2,1)S(1)} %get-tuple-element.61.refs_1_.refs_0_), channel_id=1, source_target_pairs={{0,32},{32,64},{64,96},{96,0},{1,33},{33,65},{65,97},{97,1},{2,34}... | collective-permute-start | bytes 1572872 | tf_op jit(solution)/shard_map/ppermute | solution.py:349
  47.9 22.3 %collective-permute-start.3 = (bf16[128,2048]{1,0:T(8,128)(2,1)S(1)}, bf16[128,2048]{1,0:T(8,128)(2,1)S(1)}, u32[]{:S(2)}, u32[]{:S(2)}) collective-permute-start(bf16[128,2048]{1,0:T(8,128)(2,1)S(1)} %get-tuple-element.61.refs_1_.refs_0_), channel_id=1, source_target_pairs={{0,96},{32,0},{64,32},{96,64},{1,97},{33,1},{65,33},{97,65},{2,98}... | collective-permute-start | bytes 1572872 | tf_op jit(solution)/shard_map/ppermute | solution.py:349
  59.0 19.1 %collective-permute-start.4 = (bf16[64,2048]{1,0:T(8,128)(2,1)S(1)}, bf16[64,2048]{1,0:T(8,128)(2,1)S(1)}, u32[]{:S(2)}, u32[]{:S(2)}) collective-permute-start(bf16[64,2048]{1,0:T(8,128)(2,1)S(1)} %slice.16), channel_id=1, source_target_pairs={{0,32},{32,64},{64,96},{96,0},{1,33},{33,65},{65,97},{97,1},{2,34}... | collective-permute-start | bytes 786440 | tf_op jit(solution)/shard_map/ppermute | solution.py:349
  59.2 19.2 %collective-permute-start.5 = (bf16[64,2048]{1,0:T(8,128)(2,1)S(1)}, bf16[64,2048]{1,0:T(8,128)(2,1)S(1)}, u32[]{:S(2)}, u32[]{:S(2)}) collective-permute-start(bf16[64,2048]{1,0:T(8,128)(2,1)S(1)} %slice.17), channel_id=1, source_target_pairs={{0,96},{32,0},{64,32},{96,64},{1,97},{33,1},{65,33},{97,65},{2,98}... | collective-permute-start | bytes 786440 | tf_op jit(solution)/shard_map/ppermute | solution.py:349
  61.9 1.7 %copy-start.1 = (bf16[1,2048,640]{2,1,0:T(8,128)(2,1)S(1)}, bf16[1,2048,640]{2,1,0:T(8,128)(2,1)}, u32[]{:S(2)}) copy-start(bf16[1,2048,640]{2,1,0:T(8,128)(2,1)} %param.14) | copy-start | bytes 7864324
  63.6 2.7 %copy-start.2 = (bf16[1,640,2048]{2,1,0:T(8,128)(2,1)S(1)}, bf16[1,640,2048]{2,1,0:T(8,128)(2,1)}, u32[]{:S(2)}) copy-start(bf16[1,640,2048]{2,1,0:T(8,128)(2,1)} %param.15) | copy-start | bytes 7864324
  70.3 11.2 %collective-permute-start.6 = (bf16[64,2048]{1,0:T(8,128)(2,1)S(1)}, bf16[64,2048]{1,0:T(8,128)(2,1)S(1)}, u32[]{:S(2)}, u32[]{:S(2)}) collective-permute-start(bf16[64,2048]{1,0:T(8,128)(2,1)S(1)} %slice.14), channel_id=1, source_target_pairs={{0,32},{32,64},{64,96},{96,0},{1,33},{33,65},{65,97},{97,1},{2,34}... | collective-permute-start | bytes 786440 | tf_op jit(solution)/shard_map/ppermute | solution.py:349
  71.3 10.2 %collective-permute-start.7 = (bf16[64,2048]{1,0:T(8,128)(2,1)S(1)}, bf16[64,2048]{1,0:T(8,128)(2,1)S(1)}, u32[]{:S(2)}, u32[]{:S(2)}) collective-permute-start(bf16[64,2048]{1,0:T(8,128)(2,1)S(1)} %slice.15), channel_id=1, source_target_pairs={{0,96},{32,0},{64,32},{96,64},{1,97},{33,1},{65,33},{97,65},{2,98}... | collective-permute-start | bytes 786440 | tf_op jit(solution)/shard_map/ppermute | solution.py:349
  76.9 17.4 %collective-permute-start.8 = (bf16[128,2048]{1,0:T(8,128)(2,1)S(1)}, bf16[128,2048]{1,0:T(8,128)(2,1)S(1)}, u32[]{:S(2)}, u32[]{:S(2)}) collective-permute-start(bf16[128,2048]{1,0:T(8,128)(2,1)S(1)} %get-tuple-element.84), channel_id=1, source_target_pairs={{0,96},{32,0},{64,32},{96,64},{1,97},{33,1},{65,33},{97,65},{2,98}... | collective-permute-start | bytes 1572872 | tf_op jit(solution)/shard_map/ppermute | solution.py:349
  78.1 16.2 %collective-permute-start.9 = (bf16[128,2048]{1,0:T(8,128)(2,1)S(1)}, bf16[128,2048]{1,0:T(8,128)(2,1)S(1)}, u32[]{:S(2)}, u32[]{:S(2)}) collective-permute-start(bf16[128,2048]{1,0:T(8,128)(2,1)S(1)} %get-tuple-element.85), channel_id=1, source_target_pairs={{0,32},{32,64},{64,96},{96,0},{1,33},{33,65},{65,97},{97,1},{2,34}... | collective-permute-start | bytes 1572872 | tf_op jit(solution)/shard_map/ppermute | solution.py:349
  84.5 21.4 %collective-permute-start.10 = (bf16[144,2048]{1,0:T(8,128)(2,1)S(1)}, bf16[144,2048]{1,0:T(8,128)(2,1)S(1)}, u32[]{:S(2)}, u32[]{:S(2)}) collective-permute-start(bf16[144,2048]{1,0:T(8,128)(2,1)S(1)} %get-tuple-element.88), channel_id=1, source_target_pairs={{0,64},{32,96},{64,0},{96,32},{1,65},{33,97},{65,1},{97,33},{2,66}... | collective-permute-start | bytes 1769480 | tf_op jit(solution)/shard_map/ppermute | solution.py:349
  86.7 19.2 %collective-permute-start.11 = (f32[2,2048]{1,0:T(2,128)S(1)}, f32[2,2048]{1,0:T(2,128)S(1)}, u32[]{:S(2)}, u32[]{:S(2)}) collective-permute-start(f32[2,2048]{1,0:T(2,128)S(1)} %get-tuple-element.102.small_ref), channel_id=1, source_target_pairs={{0,32},{32,64},{64,96},{96,0},{1,33},{33,65},{65,97},{97,1},{2,34}... | collective-permute-start | bytes 49160 | tf_op jit(solution)/shard_map/ppermute | solution.py:349
  87.5 18.4 %collective-permute-start.12 = (f32[2,2048]{1,0:T(2,128)S(1)}, f32[2,2048]{1,0:T(2,128)S(1)}, u32[]{:S(2)}, u32[]{:S(2)}) collective-permute-start(f32[2,2048]{1,0:T(2,128)S(1)} %get-tuple-element.102.small_ref), channel_id=1, source_target_pairs={{0,96},{32,0},{64,32},{96,64},{1,97},{33,1},{65,33},{97,65},{2,98}... | collective-permute-start | bytes 49160 | tf_op jit(solution)/shard_map/ppermute | solution.py:349
  105.9 28.1 %copy-start.3 = (bf16[128,2048]{1,0:T(8,128)(2,1)S(1)}, bf16[128,2048]{1,0:T(8,128)(2,1)}, u32[]{:S(2)}) copy-start(bf16[128,2048]{1,0:T(8,128)(2,1)} %tokens_ref.3) | copy-start | bytes 1572868
  105.9 28.1 %copy-start.4 = (bf16[128,2048]{1,0:T(8,128)(2,1)S(1)}, bf16[128,2048]{1,0:T(8,128)(2,1)}, u32[]{:S(2)}) copy-start(bf16[128,2048]{1,0:T(8,128)(2,1)} %grad_ref.3) | copy-start | bytes 1572868
  105.9 28.1 %copy-start.5 = (bf16[256,128]{1,0:T(8,128)(2,1)S(1)}, bf16[256,128]{1,0:T(8,128)(2,1)}, u32[]{:S(2)}) copy-start(bf16[256,128]{1,0:T(8,128)(2,1)} %get-tuple-element.103.picker_ref) | copy-start | bytes 196612
  105.9 28.1 %copy-start.6 = (f32[2048]{0:T(1024)S(1)}, f32[2048]{0:T(1024)}, u32[]{:S(2)}) copy-start(f32[2048]{0:T(1024)} %param.11) | copy-start | bytes 24580

commit v3 on v2

v3 whole, which is shorter than its diff:
```python
import functools

import jax
import jax.numpy as jnp
from jax import lax
from jax.experimental import pallas as pl
from jax.experimental.pallas import tpu as pltpu
from jax.sharding import PartitionSpec as P

F32 = jnp.float32
BF16 = jnp.bfloat16
DEAD = 2.0**100
GELU_SCALE = 0.7978845608028654
GELU_CUBIC = 0.044715


def dot(a, b, dims=((1,), (0,))):
    return lax.dot_general(a, b, (dims, ((), ())), preferred_element_type=F32)


WHOLE = pl.BlockSpec(memory_space=pltpu.VMEM)
PARAMS = pltpu.CompilerParams(vmem_limit_bytes=24 * 1024 * 1024)
TAIL = 16
COST = pl.CostEstimate(flops=1, bytes_accessed=1, transcendentals=0)


def stack(values):
    return values[0] if len(values) == 1 else jnp.concatenate(values, axis=0)


def iota(shape, axis):
    return lax.broadcasted_iota(jnp.int32, shape, axis)


def one_hot_of_slots(slot_rows_ref, count_ref, tok_dev, copies):
    slots, experts = slot_rows_ref.shape
    total = copies * slots * experts
    line = iota((total, 1), 0)
    mine = iota((total, experts), 1) == line // (copies * slots)
    names = dot(
        mine.astype(BF16), slot_rows_ref[...].astype(F32).astype(BF16), ((1,), (1,))
    )
    place = line % slots
    name = jnp.where(place == iota((total, slots), 1), names, 0.0)
    name = jnp.sum(name, axis=1, keepdims=True)
    count = jnp.where(mine, count_ref[...].astype(F32), 0.0)
    live = place.astype(F32) < jnp.sum(count, axis=1, keepdims=True)
    name = jnp.where(live, name, -1.0)
    return iota((total, tok_dev), 1).astype(F32) == name, live


def pick_kernel(tokens_ref, grad_ref, gain_ref, slot_rows_ref, count_ref, slots_ref, picker_ref):
    tok_dev = picker_ref.shape[1]
    slots = slot_rows_ref.shape[0]
    tok = tokens_ref[...].astype(F32)
    inv_rms = lax.rsqrt(jnp.mean(tok * tok, axis=1, keepdims=True) + 1e-06)
    normed = (tok * inv_rms * gain_ref[...]).astype(BF16)
    hot, live = one_hot_of_slots(slot_rows_ref, count_ref, tok_dev, 2)
    second = iota((hot.shape[0], 1), 0) // slots % 2 == 1
    both = jnp.concatenate([hot & ~second, hot & second], axis=1).astype(BF16)
    rows = dot(both, jnp.concatenate([normed, grad_ref[...]], axis=0))
    slots_ref[...] = rows.astype(BF16)
    slots_ref[:, :128] = jnp.where(live, rows[:, :128], DEAD).astype(BF16)
    hot, _ = one_hot_of_slots(slot_rows_ref, count_ref, tok_dev, 1)
    picker_ref[...] = hot.astype(BF16)


def pick(tokens, grad_out, norm_gain, slot_rows, slot_count):
    total = slot_rows.shape[0] * slot_rows.shape[1]
    tok_dev, width = tokens.shape
    return pl.pallas_call(
        pick_kernel,
        out_shape=(
            jax.ShapeDtypeStruct((2 * total, width), BF16),
            jax.ShapeDtypeStruct((total, tok_dev), BF16),
        ),
        in_specs=[WHOLE] * 5,
        out_specs=[WHOLE] * 2,
        compiler_params=pltpu.CompilerParams(vmem_limit_bytes=56 * 1024 * 1024),
        cost_estimate=COST,
        name="pick",
    )(tokens, grad_out, norm_gain, slot_rows, slot_count)


def pack_kernel(slots, rows_ref, first_ref, second_ref, home_ref):
    both = rows_ref.shape[0]
    total, live_rows = home_ref.shape
    half = live_rows // 2
    line = iota((both, 1), 0)
    kind = line // slots % 2
    other = iota((1, both), 1)
    earlier = (other < line) & (other // slots % 2 == kind)
    alive = rows_ref[:, :1].astype(F32) < DEAD / 2
    flags = jnp.broadcast_to(alive.astype(F32), (both, live_rows)).astype(BF16)
    index = dot(earlier.astype(BF16), flags)
    hot = (index == iota((both, live_rows), 1).astype(F32)) & alive
    home = jnp.concatenate([hot & (kind == 0), hot & (kind == 1)], axis=1).astype(BF16)
    live = dot(home, rows_ref[...], ((0,), (0,))).astype(BF16)
    first_ref[:half, :] = live[:half]
    first_ref[half:, :] = live[live_rows : live_rows + half]
    second_ref[:half, :] = live[half:live_rows]
    second_ref[half:, :] = live[live_rows + half :]
    slot = iota((total, 1), 0)
    source = slot // slots * (2 * slots) + slot % slots
    mine = (iota((total, both), 1) == source).astype(BF16)
    home_ref[...] = dot(mine, home[:, :live_rows]).astype(BF16)


def pack(rows, slots):
    both, width = rows.shape
    total = both // 2
    return pl.pallas_call(
        functools.partial(pack_kernel, slots),
        out_shape=(
            jax.ShapeDtypeStruct((total // 2, width), BF16),
            jax.ShapeDtypeStruct((total // 2, width), BF16),
            jax.ShapeDtypeStruct((total, total // 2), BF16),
        ),
        in_specs=[WHOLE],
        out_specs=[WHOLE] * 3,
        compiler_params=PARAMS,
        cost_estimate=COST,
        name="pack",
    )(rows)


def hidden_kernel(n, *refs):
    w0_ref, w1_ref = refs[n : n + 2]
    outs = refs[n + 2 :]
    half = refs[0].shape[0] // 2
    rows = stack([ref[:half, :] for ref in refs[:n]])
    pre0 = dot(rows, w0_ref[...])
    pre1 = dot(rows, w1_ref[...])
    square = pre0 * pre0
    tanh = jnp.tanh(GELU_SCALE * pre0 * (1.0 + GELU_CUBIC * square))
    cdf = 0.5 + 0.5 * tanh
    slope = cdf + 0.5 * pre0 * (1.0 - tanh * tanh) * (
        GELU_SCALE * (1.0 + 3.0 * GELU_CUBIC * square)
    )
    gelu = pre0 * cdf
    mix = pre1 * slope
    act = gelu * pre1
    size = outs[0].shape[0]
    for k in range(len(outs) // 3):
        at = slice(k * size, (k + 1) * size)
        outs[3 * k][...] = gelu[at]
        outs[3 * k + 1][...] = mix[at]
        outs[3 * k + 2][...] = act[at]


def hidden(sets, w0, w1):
    width, units = w0.shape
    parts = [part for each in sets for part in each]
    m = len(sets[0]) * parts[0].shape[0] // 2
    flat = pl.pallas_call(
        functools.partial(hidden_kernel, len(parts)),
        out_shape=[jax.ShapeDtypeStruct((m, units), F32)] * (3 * len(sets)),
        in_specs=[WHOLE] * (len(parts) + 2),
        out_specs=[WHOLE] * (3 * len(sets)),
        compiler_params=PARAMS,
        cost_estimate=COST,
        name="hidden",
    )(*parts, w0, w1)
    return [flat[3 * k : 3 * k + 3] for k in range(len(sets))]


def block_kernel(n, sets, places, *refs):
    part_refs, mid_refs, refs = refs[:n], refs[n : n + 3 * sets], refs[n + 3 * sets :]
    w0_ref, w1_ref, wo_ref, rrow_ref, before_ref = refs[:5]
    *dh_refs, act_ref, d0_ref, d1_ref, small_ref = refs[5:]
    half = part_refs[0].shape[0] // 2
    gelu, mix, act = (stack([ref[...] for ref in mid_refs[k::3]]) for k in range(3))
    rrow = rrow_ref[...]
    up = dot(stack([ref[half:, :] for ref in part_refs]), wo_ref[...], ((1,), (1,)))
    rows32 = stack([ref[:half, :] for ref in part_refs]).astype(F32)
    logit = jnp.sum(rows32 * rrow, axis=1, keepdims=True)
    gate = 1.0 / (1.0 + jnp.exp(-logit))
    gate_row = gate.astype(BF16).astype(F32)
    dgate = jnp.sum(act * up, axis=1, keepdims=True)
    d_act = gate_row * up
    d0 = (d_act * mix).astype(BF16)
    d1 = (d_act * gelu).astype(BF16)
    act_ref[...] = (gate_row * act).astype(BF16)
    d0_ref[...] = d0
    d1_ref[...] = d1
    dlogit = dgate * gate * (1.0 - gate)
    dh = dot(d0, w0_ref[...], ((1,), (1,))) + dot(d1, w1_ref[...], ((1,), (1,)))
    dh = dh + dlogit * rrow
    col = jnp.sum(rows32 * dlogit, axis=0, keepdims=True)
    gain = jnp.sum(rows32 * dh, axis=0, keepdims=True)
    small = before_ref[...] + jnp.concatenate([col, gain], axis=0)
    small_ref[...] = small
    for k, (which, at) in enumerate(places):
        dh_refs[which][at * half : (at + 1) * half, :] = dh[k * half : (k + 1) * half].astype(BF16)
    for ref in dh_refs:
        if ref.shape[0] > 2 * half:
            high = small.astype(BF16)
            low = (small - high.astype(F32)).astype(BF16)
            rest = jnp.zeros((TAIL - 4, small.shape[1]), BF16)
            ref[2 * half :, :] = jnp.concatenate([high, low, rest], axis=0)


def block(parts, mids, weights, before, places, tail=0):
    width, units = weights[0].shape
    half = parts[0].shape[0] // 2
    m = half * len(parts)
    outs_n = len(parts) // 2
    flat = pl.pallas_call(
        functools.partial(block_kernel, len(parts), len(mids), places),
        out_shape=[jax.ShapeDtypeStruct((2 * half + tail, width), BF16)] * outs_n
        + [jax.ShapeDtypeStruct((m, units), BF16)] * 3
        + [jax.ShapeDtypeStruct((2, width), F32)],
        in_specs=[WHOLE] * (len(parts) + 3 * len(mids) + 5),
        out_specs=[WHOLE] * (outs_n + 4),
        compiler_params=PARAMS,
        cost_estimate=COST,
        name="block",
    )(*parts, *[value for mid in mids for value in mid], *weights, before)
    return flat[:outs_n], flat[outs_n : outs_n + 3], flat[-1]


def total_kernel(*refs):
    *part_refs, out_ref = refs
    out_ref[...] = sum(ref[...].astype(F32) for ref in part_refs)


def total_of(parts):
    return pl.pallas_call(
        total_kernel,
        out_shape=jax.ShapeDtypeStruct(parts[0].shape, F32),
        in_specs=[WHOLE] * len(parts),
        out_specs=WHOLE,
        compiler_params=PARAMS,
        cost_estimate=pl.CostEstimate(flops=1000000000, bytes_accessed=1, transcendentals=0),
        name="total_of",
    )(*parts)


def expand_kernel(dh_ref, far_ref, home_ref, small_ref, *refs):
    *others, out_ref = refs
    rows, width = dh_ref.shape
    dh = dh_ref[...] + far_ref[:rows, :].astype(F32)
    out_ref[:, :width] = dot(home_ref[...], dh.astype(BF16)).astype(BF16)
    carried = far_ref[rows:, :].astype(F32)
    small = small_ref[...] + carried[0:2] + carried[2:4]
    for ref in others:
        small = small + ref[...]
    part = out_ref.shape[1] - width
    lines = [small[k : k + 1, at : at + part] for k in range(2) for at in range(0, width, part)]
    lines = jnp.concatenate(lines, axis=0).astype(BF16)
    out_ref[:, width:] = jnp.concatenate([lines] * (out_ref.shape[0] // lines.shape[0]), axis=0)


def expand(dh, far, home, slots, *smalls):
    total = home.shape[0]
    width = dh.shape[1]
    return pl.pallas_call(
        expand_kernel,
        out_shape=jax.ShapeDtypeStruct((total, width + 2 * width // slots), BF16),
        in_specs=[WHOLE] * (3 + len(smalls)),
        out_specs=WHOLE,
        compiler_params=PARAMS,
        cost_estimate=COST,
        name="expand",
    )(dh, far, home, *smalls)


def finish_kernel(
    back_ref, picker_ref, tokens_ref, grad_ref, gain_ref, d_tokens_ref, d_gain_ref, d_router_ref
):
    total = back_ref.shape[0]
    width = tokens_ref.shape[1]
    experts = d_router_ref.shape[0]
    slots = total // experts
    half = slots // 2
    part = back_ref.shape[1] - width
    gain = gain_ref[...]
    tok = tokens_ref[...].astype(F32)
    inv_rms = lax.rsqrt(jnp.mean(tok * tok, axis=1, keepdims=True) + 1e-06)
    d_normed = dot(picker_ref[...], back_ref[:, :width], ((0,), (0,)))
    scaled = d_normed * gain
    inner = jnp.mean(scaled * tok, axis=1, keepdims=True)
    d_tokens_ref[...] = (
        grad_ref[...].astype(F32) + inv_rms * scaled - tok * (inv_rms * inv_rms * inv_rms * inner)
    ).astype(BF16)
    extra = back_ref[:, width:]
    slot = lax.broadcasted_iota(jnp.int32, (experts, total), 1)
    home = slots * lax.broadcasted_iota(jnp.int32, (experts, total), 0)
    place = lax.broadcasted_iota(jnp.int32, (slots, total), 1) % slots
    line = lax.broadcasted_iota(jnp.int32, (slots, total), 0)
    sums = dot((place == line).astype(BF16), extra)
    for q in range(half):
        at = slice(q * part, (q + 1) * part)
        d_router_ref[:, at] = dot((slot == home + q).astype(BF16), extra)
        d_gain_ref[:, at] = sums[half + q : half + q + 1, :] / gain[:, at]


def finish(back, picker, tokens, grad_out, norm_gain, experts):
    width = tokens.shape[1]
    return pl.pallas_call(
        finish_kernel,
        out_shape=(
            jax.ShapeDtypeStruct(tokens.shape, BF16),
            jax.ShapeDtypeStruct((1, width), F32),
            jax.ShapeDtypeStruct((experts, width), F32),
        ),
        in_specs=[WHOLE] * 5,
        out_specs=[WHOLE] * 3,
        compiler_params=PARAMS,
        cost_estimate=COST,
        name="finish",
    )(back, picker, tokens, grad_out, norm_gain)


def in_grads_kernel(n, *refs):
    w0_ref, w1_ref, pair_ref = refs[-3:]
    grads = refs[n:-3]
    units = w0_ref.shape[1]

    @pl.when(pl.program_id(0) == 0)
    def _():
        pair_ref[:, :units] = stack([ref[...] for ref in grads[0::2]])
        pair_ref[:, units:] = stack([ref[...] for ref in grads[1::2]])

    pair = dot(stack([ref[...] for ref in refs[:n]]), pair_ref[...], ((0,), (0,)))
    w0_ref[...] = pair[:, :units].astype(BF16)
    w1_ref[...] = pair[:, units:].astype(BF16)


def out_grad_kernel(n, *refs):
    wo_ref, act_ref = refs[-2:]

    @pl.when(pl.program_id(0) == 0)
    def _():
        act_ref[...] = stack([ref[...] for ref in refs[n:-2]]).T

    wo_ref[...] = dot(act_ref[...], stack([ref[...] for ref in refs[:n]])).astype(BF16)


def weight_grads(kernel, parts, which, factors, outs, scratch, tile=512):
    half, width = parts[0].shape[0] // 2, parts[0].shape[1]
    return pl.pallas_call(
        functools.partial(kernel, len(parts)),
        grid=(width // tile,),
        out_shape=[jax.ShapeDtypeStruct(shape, BF16) for shape in outs],
        in_specs=[pl.BlockSpec((half, tile), lambda i: (which, i))] * len(parts)
        + [pl.BlockSpec(value.shape, lambda i: (0, 0)) for value in factors],
        out_specs=[
            pl.BlockSpec((tile, shape[1]), lambda i: (i, 0))
            if shape[0] == width
            else pl.BlockSpec((shape[0], tile), lambda i: (0, i))
            for shape in outs
        ],
        scratch_shapes=[pltpu.VMEM(scratch, BF16)],
        compiler_params=PARAMS,
        cost_estimate=pl.CostEstimate(flops=2000000000, bytes_accessed=1, transcendentals=0),
        name="weight_grads",
    )(*parts, *factors)


def shift(value, axis, by):
    n = lax.axis_size(axis)
    return lax.ppermute(value, axis, [(i, (i + by) % n) for i in range(n)])


def exchange(value):
    return lax.all_to_all(value, "expert", split_axis=0, concat_axis=0, tiled=True)


def per_device(tokens, grad_out, norm_gain, router, w_in0, w_in1, w_out, slot_rows, slot_count):
    tok_dev, width = tokens.shape
    experts = router.shape[1]
    slots = slot_rows.shape[2]
    total = experts * slots
    w0, w1, wo = w_in0[0], w_in1[0], w_out[0]

    expert = lax.axis_index("expert")
    rrow = lax.dynamic_slice_in_dim(router.T, expert, 1, axis=0).astype(F32)
    both, picker = pick(
        tokens, grad_out, norm_gain.reshape(1, width), slot_rows[0].T, slot_count
    )
    both = exchange(both.reshape(experts, 2 * slots, width)).reshape(2 * total, width)
    both, rrow = lax.optimization_barrier((both, rrow))
    first, second, home = pack(both, slots)
    weights = (w0, w1, wo, rrow)
    early = [shift(first, "dp", 1), shift(second, "dp", -1)]
    late = [shift(second, "dp", 1), shift(first, "dp", -1)]
    far = [shift(early[0], "dp", 1), shift(early[1], "dp", -1)]
    one = ((0, 0), (0, 1))
    mid_own, mid_early = hidden([[first, second], early], w0, w1)
    small = jnp.zeros((2, width), F32)
    (dh_own,), grads_own, small = block([first, second], [mid_own], weights, small, one)
    late, small = lax.optimization_barrier((late, small))
    (mid_late,) = hidden([late], w0, w1)
    dh_near, grads_near, small = block(
        early + late, [mid_early, mid_late], weights, small, ((0, 0), (1, 1), (0, 1), (1, 0))
    )
    far, small = lax.optimization_barrier((far, small))
    (mid_far,) = hidden([far], w0, w1)
    (dh_far,), grads_far, small = block(far, [mid_far], weights, small, one, TAIL)
    back_near = [shift(dh_near[0], "dp", -1), shift(dh_near[1], "dp", 1)]
    back_far = shift(dh_far, "dp", 2)
    smalls = [small, shift(small, "dp", 1), shift(small, "dp", -1)]

    parts = [first, second] + early + late + far
    grads = (*grads_own, *grads_near, *grads_far)
    rows, units = 4 * first.shape[0], w0.shape[1]
    grad_w0, grad_w1 = weight_grads(
        in_grads_kernel,
        parts,
        0,
        [part for k, part in enumerate(grads) if k % 3],
        [w0.shape, w1.shape],
        (rows, 2 * units),
    )
    (grad_wout,) = weight_grads(
        out_grad_kernel, parts, 1, list(grads[0::3]), [wo.shape], (units, rows)
    )
    back_far, grad_w0, grad_w1, grad_wout = lax.optimization_barrier(
        (back_far, grad_w0, grad_w1, grad_wout)
    )

    back = expand(total_of([dh_own, *back_near]), back_far, home, slots, *smalls)
    back = exchange(back.reshape(experts, slots, -1)).reshape(total, -1)
    d_tokens, d_gain, d_router = finish(
        back, picker, tokens, grad_out, norm_gain.reshape(1, width), experts
    )
    return (
        d_tokens,
        d_gain.reshape(width),
        d_router.T,
        grad_w0[None],
        grad_w1[None],
        grad_wout[None],
    )


def solution(mesh):
    in_specs = (
        P(("dp", "expert"), None),
        P(("dp", "expert"), None),
        P(),
        P(),
        P("expert", None, "dp"),
        P("expert", None, "dp"),
        P("expert", "dp", None),
        P(("dp", "expert"), None, None),
        P(("dp", "expert"), None),
    )
    out_specs = (
        P(("dp", "expert"), None),
        P(),
        P(),
        P("expert", None, "dp"),
        P("expert", None, "dp"),
        P("expert", "dp", None),
    )
    return jax.shard_map(
        per_device, mesh=mesh, in_specs=in_specs, out_specs=out_specs, check_vma=False
    )
```

time: 136 us -> 134 us (0.985)
  waiting for transfers between devices: 46.9 us -> 49.4 us
  blocking collectives: 27.5 us -> 25.2 us
  starting transfers between devices: 27.3 us -> 25.3 us
    all_to_all x1, blocking collectives: 27.5 us -> 25.2 us  [exchange(): lax.all_to_all(value, 'expert', split_axis=0, concat_axis=0, tiled=True)]
    ppermute x13 -> x11, waiting for transfers between devices: 19.5 us -> 21.8 us  [shift(): return lax.ppermute(value, axis, [(i, (i + by) % n) for i in range(n)])]
    ppermute x13 -> x11, starting transfers between devices: 17.7 us -> 15.4 us  [shift(): return lax.ppermute(value, axis, [(i, (i + by) % n) for i in range(n)])]
    pallas_call x7 -> x9, Pallas kernels: 21.6 us -> 22.1 us  [the longest x3 9.43 us: block(): pl.pallas_call(functools.partial(block_kernel, len(parts), len(mids), pla...]
  transfers between devices with their start and end apart: 14 -> 12, of which waited for: 5 -> 5; matrix products, arithmetic and copies ran while one was open for 1% -> 1% of each run, Pallas kernels for 16% -> 17%
where the time goes in v3:
time: 134 us
  waiting for transfers between devices  49.4 us (37%)
  Pallas kernels  30.5 us (23%)
  starting transfers between devices  25.3 us (19%)
  blocking collectives  25.2 us (19%)
  local copies, waits for them, and re-layouts  1.78 us (1%)
    all_to_all x1, waiting for transfers between devices, exchange(): lax.all_to_all(value, 'expert', split_axis=0, concat_axis=0, tiled=True)  27.6 us
    all_to_all x1, blocking collectives, exchange(): lax.all_to_all(value, 'expert', split_axis=0, concat_axis=0, tiled=True)  25.2 us
    ppermute x11, waiting for transfers between devices, shift(): return lax.ppermute(value, axis, [(i, (i + by) % n) for i in range(n)])  21.8 us
    ppermute x11, starting transfers between devices, shift(): return lax.ppermute(value, axis, [(i, (i + by) % n) for i in range(n)])  15.4 us
    all_to_all x1, starting transfers between devices, exchange(): lax.all_to_all(value, 'expert', split_axis=0, concat_axis=0, tiled=True)  9.92 us
    pallas_call x3, Pallas kernels, block(): pl.pallas_call(functools.partial(block_kernel, len(parts), len(mids), pla...  9.43 us
    pallas_call x2, Pallas kernels, weight_grads(): pl.pallas_call(functools.partial(kernel, len(parts)), grid=(width // tile...  8.59 us
    pallas_call x3, Pallas kernels, hidden(): pl.pallas_call(functools.partial(hidden_kernel, len(parts)), out_shape=[j...  3.9 us
  transfers between devices with their start and end apart: 12, of which 5 were waited for; matrix products, arithmetic and copies ran while one was open for 1% of the time, Pallas kernels for 17%

profile of v3, /device:TPU:1, one launch (start us, length us, event | category | flops | bytes accessed | tf_op | source)
XLA Modules:
  0.0 133.8 jit_solution(5625047879252077639)
XLA Ops:
  0.6 3.5 %pick.1 = (bf16[512,2048]{1,0:T(8,128)(2,1)}, bf16[256,128]{1,0:T(8,128)(2,1)}) custom-call(bf16[128,2048]{1,0:T(8,128)(2,1)} %tokens_ref.3, bf16[128,2048]{1,0:T(8,128)(2,1)} %grad_ref.3, f32[1,2048]{1,0:T(1,128)} %bitcast.36, s32[8,32]{1,0:T(8,128)} %bitcast.40, s32[1,32]{1,0:T(1,128)} %count_ref.1), custom_call_target="tpu_custom_call" | custom-call | flops 1 | bytes 1 | tf_op jit(solution)/shard_map/pick/pallas_call | solution.py:71
  4.2 9.9 %all-to-all-start = ((bf16[32,16,2048]{2,1,0:T(8,128)(2,1)}), bf16[32,16,2048]{2,1,0:T(8,128)(2,1)}, u32[]{:S(2)}, u32[]{:S(2)}) async-start(bf16[32,16,2048]{2,1,0:T(8,128)(2,1)} %bitcast.39), calls=%async_computation | async-start | bytes 4194304 | tf_op jit(solution)/shard_map/all_to_all | solution.py:367
  14.1 0.8 bitcast_convert_fusion.refs_8_.refs_13_
  14.9 27.6 %all-to-all-done = bf16[32,16,2048]{2,1,0:T(8,128)(2,1)} async-done(((bf16[32,16,2048]{2,1,0:T(8,128)(2,1)}), bf16[32,16,2048]{2,1,0:T(8,128)(2,1)}, u32[]{:S(2)}, u32[]{:S(2)}) %all-to-all-start) | async-done | bytes 2097184 | tf_op jit(solution)/shard_map/all_to_all | solution.py:367
  42.5 3.0 %pack.1 = (bf16[128,2048]{1,0:T(8,128)(2,1)S(1)}, bf16[128,2048]{1,0:T(8,128)(2,1)S(1)}, bf16[256,128]{1,0:T(8,128)(2,1)S(1)}) custom-call(bf16[512,2048]{1,0:T(8,128)(2,1)} %bitcast.4.rows_ref), custom_call_target="tpu_custom_call" | custom-call | flops 1 | bytes 1 | tf_op jit(solution)/shard_map/pack/pallas_call | solution.py:112
  45.4 1.3 collective-permute-start
  46.7 1.5 %collective-permute-start.1 = (bf16[128,2048]{1,0:T(8,128)(2,1)S(1)}, bf16[128,2048]{1,0:T(8,128)(2,1)S(1)}, u32[]{:S(2)}, u32[]{:S(2)}) collective-permute-start(bf16[128,2048]{1,0:T(8,128)(2,1)S(1)} %get-tuple-element.59.refs_1_), channel_id=1, source_target_pairs={{0,96},{32,0},{64,32},{96,64},{1,97},{33,1},{65,33},{97,65},{2,98}... | collective-permute-start | bytes 1572872 | tf_op jit(solution)/shard_map/ppermute | solution.py:363
  48.2 0.0 collective-permute-start.2
  48.2 2.7 %collective-permute-start.3 = (bf16[128,2048]{1,0:T(8,128)(2,1)S(1)}, bf16[128,2048]{1,0:T(8,128)(2,1)S(1)}, u32[]{:S(2)}, u32[]{:S(2)}) collective-permute-start(bf16[128,2048]{1,0:T(8,128)(2,1)S(1)} %get-tuple-element.58.refs_0_), channel_id=1, source_target_pairs={{0,96},{32,0},{64,32},{96,64},{1,97},{33,1},{65,33},{97,65},{2,98}... | collective-permute-start | bytes 1572872 | tf_op jit(solution)/shard_map/ppermute | solution.py:363
  50.8 8.4 %collective-permute-done.refs_2_.refs_0_ = bf16[128,2048]{1,0:T(8,128)(2,1)S(1)} collective-permute-done((bf16[128,2048]{1,0:T(8,128)(2,1)S(1)}, bf16[128,2048]{1,0:T(8,128)(2,1)S(1)}, u32[]{:S(2)}, u32[]{:S(2)}) %collective-permute-start) | collective-permute-done | bytes 524320 | tf_op jit(solution)/shard_map/ppermute | solution.py:363
  59.3 2.7 %collective-permute-start.7 = (bf16[128,2048]{1,0:T(8,128)(2,1)S(1)}, bf16[128,2048]{1,0:T(8,128)(2,1)S(1)}, u32[]{:S(2)}, u32[]{:S(2)}) collective-permute-start(bf16[128,2048]{1,0:T(8,128)(2,1)S(1)} %collective-permute-done.1.refs_3_.refs_1_), channel_id=1, source_target_pairs={{0,96},{32,0},{64,32},{96,64},{1,97},{33,1},{65,33},{97,65},{2,98}... | collective-permute-start | bytes 1572872 | tf_op jit(solution)/shard_map/ppermute | solution.py:363
  62.0 1.7 %copy-done.1 = bf16[1,2048,640]{2,1,0:T(8,128)(2,1)S(1)} copy-done((bf16[1,2048,640]{2,1,0:T(8,128)(2,1)S(1)}, bf16[1,2048,640]{2,1,0:T(8,128)(2,1)}, u32[]{:S(2)}) %copy-start.1) | copy-done | bytes 2621464
  63.7 1.9 %hidden.3 = (f32[128,640]{1,0:T(8,128)S(1)}, f32[128,640]{1,0:T(8,128)S(1)}, f32[128,640]{1,0:T(8,128)S(1)}, f32[128,640]{1,0:T(8,128)S(1)}, f32[128,640]{1,0:T(8,128)S(1)}, /*index=5*/f32[128,640]{1,0:T(8,128)S(1)}) custom-call(bf16[128,2048]{1,0:T(8,128)(2,1)S(1)} %get-tuple-element.58.refs_0_, bf16[128,2048]{1,0:T(8,128)(2,1)S(1)} %get-tuple-element.59.refs_1_, ...), custom_call_target="tpu_custom_call" | custom-call | flops 1 | bytes 1 | tf_op jit(solution)/shard_map/hidden/pallas_call | solution.py:155
  65.6 2.9 %block.3 = (bf16[128,2048]{1,0:T(8,128)(2,1)S(1)}, bf16[128,640]{1,0:T(8,128)(2,1)S(1)}, bf16[128,640]{1,0:T(8,128)(2,1)S(1)}, bf16[128,640]{1,0:T(8,128)(2,1)S(1)}, f32[2,2048]{1,0:T(2,128)S(1)}) custom-call(bf16[128,2048]{1,0:T(8,128)(2,1)S(1)} %get-tuple-element.58.refs_0_, bf16[128,2048]{1,0:T(8,128)(2,1)S(1)} %get-tuple-element.59.refs_1_, ...), custom_call_target="tpu_custom_call" | custom-call | flops 1 | bytes 1 | tf_op jit(solution)/shard_map/block/pallas_call | solution.py:208
  68.5 2.0 %collective-permute-done.2.refs_0_.refs_2_.refs_4_ = bf16[128,2048]{1,0:T(8,128)(2,1)S(1)} collective-permute-done((bf16[128,2048]{1,0:T(8,128)(2,1)S(1)}, bf16[128,2048]{1,0:T(8,128)(2,1)S(1)}, u32[]{:S(2)}, u32[]{:S(2)}) %collective-permute-start.2) | collective-permute-done | bytes 524320 | tf_op jit(solution)/shard_map/ppermute | solution.py:363
  70.5 1.0 hidden.4
  71.5 3.5 %block.4 = (bf16[128,2048]{1,0:T(8,128)(2,1)S(1)}, bf16[128,2048]{1,0:T(8,128)(2,1)S(1)}, bf16[256,640]{1,0:T(8,128)(2,1)S(1)}, bf16[256,640]{1,0:T(8,128)(2,1)S...) custom-call(bf16[128,2048]{1,0:T(8,128)(2,1)S(1)} %collective-permute-done.refs_2_.refs_0_, ...), custom_call_target="tpu_custom_call" | custom-call | flops 1 | bytes 1 | tf_op jit(solution)/shard_map/block/pallas_call | solution.py:208
  75.1 2.4 %collective-permute-start.4 = (bf16[128,2048]{1,0:T(8,128)(2,1)S(1)}, bf16[128,2048]{1,0:T(8,128)(2,1)S(1)}, u32[]{:S(2)}, u32[]{:S(2)}) collective-permute-start(bf16[128,2048]{1,0:T(8,128)(2,1)S(1)} %get-tuple-element.75), channel_id=1, source_target_pairs={{0,96},{32,0},{64,32},{96,64},{1,97},{33,1},{65,33},{97,65},{2,98}... | collective-permute-start | bytes 1572872 | tf_op jit(solution)/shard_map/ppermute | solution.py:363
  77.5 4.2 %collective-permute-done.6.refs_0_.refs_6_ = bf16[128,2048]{1,0:T(8,128)(2,1)S(1)} collective-permute-done((bf16[128,2048]{1,0:T(8,128)(2,1)S(1)}, bf16[128,2048]{1,0:T(8,128)(2,1)S(1)}, u32[]{:S(2)}, u32[]{:S(2)}) %collective-permute-start.6) | collective-permute-done | bytes 524320 | tf_op jit(solution)/shard_map/ppermute | solution.py:363
  81.7 1.0 hidden.5
  82.8 3.0 %block.5 = (bf16[144,2048]{1,0:T(8,128)(2,1)S(1)}, bf16[128,640]{1,0:T(8,128)(2,1)S(1)}, bf16[128,640]{1,0:T(8,128)(2,1)S(1)}, bf16[128,640]{1,0:T(8,128)(2,1)S(1)}, f32[2,2048]{1,0:T(2,128)S(1)}) custom-call(bf16[128,2048]{1,0:T(8,128)(2,1)S(1)} %collective-permute-done.6.refs_0_.refs_6_, bf16[128,2048]{1,0:T(8,128)(2,1)S(1)} %collective-permute-done.7.refs_1_.refs_7_, ...), custom_call_target="tpu_custom_call" | custom-call | flops 1 | bytes 1 | tf_op jit(solution)/shard_map/block/pallas_call | solution.py:208
  85.7 2.2 %collective-permute-start.8 = (bf16[144,2048]{1,0:T(8,128)(2,1)S(1)}, bf16[144,2048]{1,0:T(8,128)(2,1)S(1)}, u32[]{:S(2)}, u32[]{:S(2)}) collective-permute-start(bf16[144,2048]{1,0:T(8,128)(2,1)S(1)} %get-tuple-element.84), channel_id=1, source_target_pairs={{0,64},{32,96},{64,0},{96,32},{1,65},{33,97},{65,1},{97,33},{2,66}... | collective-permute-start | bytes 1769480 | tf_op jit(solution)/shard_map/ppermute | solution.py:363
  87.9 0.8 collective-permute-start.9
  88.8 1.9 %collective-permute-start.10 = (f32[2,2048]{1,0:T(2,128)S(1)}, f32[2,2048]{1,0:T(2,128)S(1)}, u32[]{:S(2)}, u32[]{:S(2)}) collective-permute-start(f32[2,2048]{1,0:T(2,128)S(1)} %get-tuple-element.98.small_ref), channel_id=1, source_target_pairs={{0,96},{32,0},{64,32},{96,64},{1,97},{33,1},{65,33},{97,65},{2,98}... | collective-permute-start | bytes 49160 | tf_op jit(solution)/shard_map/ppermute | solution.py:363
  90.6 3.7 %weight_grads.3 = bf16[640,2048]{1,0:T(8,128)(2,1)} custom-call(bf16[128,2048]{1,0:T(8,128)(2,1)S(1)} %get-tuple-element.58.refs_0_, bf16[128,2048]{1,0:T(8,128)(2,1)S(1)} %get-tuple-element.59.refs_1_, bf16[128,2048]{1,0:T(8,128)(2,1)S(1)} %collective-permute-done.refs_2_.refs_0_, bf16[128,2048]{1,0:T(8,128)(2,1)S(1)} %collective-permute-done.1.refs_3_.refs_1_, ...), custom_call_target="tpu_custom_call" | custom-call | flops 2000000000 | bytes 1 | tf_op jit(solution)/shard_map/weight_grads/pallas_call | solution.py:342
  94.3 4.9 %weight_grads.2 = (bf16[2048,640]{1,0:T(8,128)(2,1)}, bf16[2048,640]{1,0:T(8,128)(2,1)}) custom-call(bf16[128,2048]{1,0:T(8,128)(2,1)S(1)} %get-tuple-element.58.refs_0_, bf16[128,2048]{1,0:T(8,128)(2,1)S(1)} %get-tuple-element.59.refs_1_, bf16[128,2048]{1,0:T(8,128)(2,1)S(1)} %collective-permute-done.refs_2_.refs_0_, ...), custom_call_target="tpu_custom_call" | custom-call | flops 2000000000 | bytes 1 | tf_op jit(solution)/shard_map/weight_grads/pallas_call | solution.py:342
  99.2 0.2 total_of.1.dh_ref
  99.4 7.2 %collective-permute-done.8.far_ref = bf16[144,2048]{1,0:T(8,128)(2,1)S(1)} collective-permute-done((bf16[144,2048]{1,0:T(8,128)(2,1)S(1)}, bf16[144,2048]{1,0:T(8,128)(2,1)S(1)}, u32[]{:S(2)}, u32[]{:S(2)}) %collective-permute-start.8) | collective-permute-done | bytes 589856 | tf_op jit(solution)/shard_map/ppermute | solution.py:363
  106.6 0.0 copy-start.4
  106.6 0.4 expand.1
  107.1 25.2 %all_to_all.10 = bf16[32,8,2560]{2,1,0:T(8,128)(2,1)S(1)} all-to-all(bf16[32,8,2560]{2,1,0:T(8,128)(2,1)S(1)} %bitcast.34), channel_id=1, replica_groups=mesh['dp'=4,'expert'=32] {'expert'}, dimensions={0} | all-to-all | bytes 2621440 | tf_op jit(solution)/shard_map/all_to_all | solution.py:367
  132.3 1.5 %finish.1 = (bf16[128,2048]{1,0:T(8,128)(2,1)}, f32[1,2048]{1,0:T(1,128)}, f32[32,2048]{1,0:T(8,128)}) custom-call(bf16[256,2560]{1,0:T(8,128)(2,1)S(1)} %bitcast.35, bf16[256,128]{1,0:T(8,128)(2,1)S(1)} %copy-done.5, bf16[128,2048]{1,0:T(8,128)(2,1)S(1)} %copy-done.3, bf16[128,2048]{1,0:T(8,128)(2,1)S(1)} %copy-done.4, f32[1,2048]{1,0:T(1,128)S(1)} %bitcast.37), custom_call_target="tpu_custom_call" | custom-call | flops 1 | bytes 1 | tf_op jit(solution)/shard_map/finish/pallas_call | solution.py:300
  (22 shorter events, 0.1 us)
Async XLA Ops:
  4.2 57.8 %copy-start = (bf16[1,2048,640]{2,1,0:T(8,128)(2,1)S(1)}, bf16[1,2048,640]{2,1,0:T(8,128)(2,1)}, u32[]{:S(2)}) copy-start(bf16[1,2048,640]{2,1,0:T(8,128)(2,1)} %param.13) | copy-start | bytes 7864324
  4.2 38.3 %all-to-all-start = ((bf16[32,16,2048]{2,1,0:T(8,128)(2,1)}), bf16[32,16,2048]{2,1,0:T(8,128)(2,1)}, u32[]{:S(2)}, u32[]{:S(2)}) async-start(bf16[32,16,2048]{2,1,0:T(8,128)(2,1)} %bitcast.39), calls=%async_computation | async-start | bytes 4194304 | tf_op jit(solution)/shard_map/all_to_all | solution.py:367
  45.4 13.9 %collective-permute-start = (bf16[128,2048]{1,0:T(8,128)(2,1)S(1)}, bf16[128,2048]{1,0:T(8,128)(2,1)S(1)}, u32[]{:S(2)}, u32[]{:S(2)}) collective-permute-start(bf16[128,2048]{1,0:T(8,128)(2,1)S(1)} %get-tuple-element.58.refs_0_), channel_id=1, source_target_pairs={{0,32},{32,64},{64,96},{96,0},{1,33},{33,65},{65,97},{97,1},{2,34}... | collective-permute-start | bytes 1572872 | tf_op jit(solution)/shard_map/ppermute | solution.py:363
  46.7 12.6 %collective-permute-start.1 = (bf16[128,2048]{1,0:T(8,128)(2,1)S(1)}, bf16[128,2048]{1,0:T(8,128)(2,1)S(1)}, u32[]{:S(2)}, u32[]{:S(2)}) collective-permute-start(bf16[128,2048]{1,0:T(8,128)(2,1)S(1)} %get-tuple-element.59.refs_1_), channel_id=1, source_target_pairs={{0,96},{32,0},{64,32},{96,64},{1,97},{33,1},{65,33},{97,65},{2,98}... | collective-permute-start | bytes 1572872 | tf_op jit(solution)/shard_map/ppermute | solution.py:363
  48.2 22.3 %collective-permute-start.2 = (bf16[128,2048]{1,0:T(8,128)(2,1)S(1)}, bf16[128,2048]{1,0:T(8,128)(2,1)S(1)}, u32[]{:S(2)}, u32[]{:S(2)}) collective-permute-start(bf16[128,2048]{1,0:T(8,128)(2,1)S(1)} %get-tuple-element.59.refs_1_), channel_id=1, source_target_pairs={{0,32},{32,64},{64,96},{96,0},{1,33},{33,65},{65,97},{97,1},{2,34}... | collective-permute-start | bytes 1572872 | tf_op jit(solution)/shard_map/ppermute | solution.py:363
  48.2 22.3 %collective-permute-start.3 = (bf16[128,2048]{1,0:T(8,128)(2,1)S(1)}, bf16[128,2048]{1,0:T(8,128)(2,1)S(1)}, u32[]{:S(2)}, u32[]{:S(2)}) collective-permute-start(bf16[128,2048]{1,0:T(8,128)(2,1)S(1)} %get-tuple-element.58.refs_0_), channel_id=1, source_target_pairs={{0,96},{32,0},{64,32},{96,64},{1,97},{33,1},{65,33},{97,65},{2,98}... | collective-permute-start | bytes 1572872 | tf_op jit(solution)/shard_map/ppermute | solution.py:363
  59.3 22.5 %collective-permute-start.6 = (bf16[128,2048]{1,0:T(8,128)(2,1)S(1)}, bf16[128,2048]{1,0:T(8,128)(2,1)S(1)}, u32[]{:S(2)}, u32[]{:S(2)}) collective-permute-start(bf16[128,2048]{1,0:T(8,128)(2,1)S(1)} %collective-permute-done.refs_2_.refs_0_), channel_id=1, source_target_pairs={{0,32},{32,64},{64,96},{96,0},{1,33},{33,65},{65,97},{97,1},{2,34}... | collective-permute-start | bytes 1572872 | tf_op jit(solution)/shard_map/ppermute | solution.py:363
  59.3 22.5 %collective-permute-start.7 = (bf16[128,2048]{1,0:T(8,128)(2,1)S(1)}, bf16[128,2048]{1,0:T(8,128)(2,1)S(1)}, u32[]{:S(2)}, u32[]{:S(2)}) collective-permute-start(bf16[128,2048]{1,0:T(8,128)(2,1)S(1)} %collective-permute-done.1.refs_3_.refs_1_), channel_id=1, source_target_pairs={{0,96},{32,0},{64,32},{96,64},{1,97},{33,1},{65,33},{97,65},{2,98}... | collective-permute-start | bytes 1572872 | tf_op jit(solution)/shard_map/ppermute | solution.py:363
  62.0 1.7 %copy-start.1 = (bf16[1,2048,640]{2,1,0:T(8,128)(2,1)S(1)}, bf16[1,2048,640]{2,1,0:T(8,128)(2,1)}, u32[]{:S(2)}) copy-start(bf16[1,2048,640]{2,1,0:T(8,128)(2,1)} %param.14) | copy-start | bytes 7864324
  63.7 1.9 %copy-start.2 = (bf16[1,640,2048]{2,1,0:T(8,128)(2,1)S(1)}, bf16[1,640,2048]{2,1,0:T(8,128)(2,1)}, u32[]{:S(2)}) copy-start(bf16[1,640,2048]{2,1,0:T(8,128)(2,1)} %param.15) | copy-start | bytes 7864324
  75.1 24.1 %collective-permute-start.4 = (bf16[128,2048]{1,0:T(8,128)(2,1)S(1)}, bf16[128,2048]{1,0:T(8,128)(2,1)S(1)}, u32[]{:S(2)}, u32[]{:S(2)}) collective-permute-start(bf16[128,2048]{1,0:T(8,128)(2,1)S(1)} %get-tuple-element.75), channel_id=1, source_target_pairs={{0,96},{32,0},{64,32},{96,64},{1,97},{33,1},{65,33},{97,65},{2,98}... | collective-permute-start | bytes 1572872 | tf_op jit(solution)/shard_map/ppermute | solution.py:363
  77.5 21.7 %collective-permute-start.5 = (bf16[128,2048]{1,0:T(8,128)(2,1)S(1)}, bf16[128,2048]{1,0:T(8,128)(2,1)S(1)}, u32[]{:S(2)}, u32[]{:S(2)}) collective-permute-start(bf16[128,2048]{1,0:T(8,128)(2,1)S(1)} %get-tuple-element.76), channel_id=1, source_target_pairs={{0,32},{32,64},{64,96},{96,0},{1,33},{33,65},{65,97},{97,1},{2,34}... | collective-permute-start | bytes 1572872 | tf_op jit(solution)/shard_map/ppermute | solution.py:363
  85.7 20.9 %collective-permute-start.8 = (bf16[144,2048]{1,0:T(8,128)(2,1)S(1)}, bf16[144,2048]{1,0:T(8,128)(2,1)S(1)}, u32[]{:S(2)}, u32[]{:S(2)}) collective-permute-start(bf16[144,2048]{1,0:T(8,128)(2,1)S(1)} %get-tuple-element.84), channel_id=1, source_target_pairs={{0,64},{32,96},{64,0},{96,32},{1,65},{33,97},{65,1},{97,33},{2,66}... | collective-permute-start | bytes 1769480 | tf_op jit(solution)/shard_map/ppermute | solution.py:363
  87.9 18.7 %collective-permute-start.9 = (f32[2,2048]{1,0:T(2,128)S(1)}, f32[2,2048]{1,0:T(2,128)S(1)}, u32[]{:S(2)}, u32[]{:S(2)}) collective-permute-start(f32[2,2048]{1,0:T(2,128)S(1)} %get-tuple-element.98.small_ref), channel_id=1, source_target_pairs={{0,32},{32,64},{64,96},{96,0},{1,33},{33,65},{65,97},{97,1},{2,34}... | collective-permute-start | bytes 49160 | tf_op jit(solution)/shard_map/ppermute | solution.py:363
  88.8 17.9 %collective-permute-start.10 = (f32[2,2048]{1,0:T(2,128)S(1)}, f32[2,2048]{1,0:T(2,128)S(1)}, u32[]{:S(2)}, u32[]{:S(2)}) collective-permute-start(f32[2,2048]{1,0:T(2,128)S(1)} %get-tuple-element.98.small_ref), channel_id=1, source_target_pairs={{0,96},{32,0},{64,32},{96,64},{1,97},{33,1},{65,33},{97,65},{2,98}... | collective-permute-start | bytes 49160 | tf_op jit(solution)/shard_map/ppermute | solution.py:363
  106.6 25.6 %copy-start.3 = (bf16[128,2048]{1,0:T(8,128)(2,1)S(1)}, bf16[128,2048]{1,0:T(8,128)(2,1)}, u32[]{:S(2)}) copy-start(bf16[128,2048]{1,0:T(8,128)(2,1)} %tokens_ref.3) | copy-start | bytes 1572868
  106.6 25.6 %copy-start.4 = (bf16[128,2048]{1,0:T(8,128)(2,1)S(1)}, bf16[128,2048]{1,0:T(8,128)(2,1)}, u32[]{:S(2)}) copy-start(bf16[128,2048]{1,0:T(8,128)(2,1)} %grad_ref.3) | copy-start | bytes 1572868
  106.6 25.6 %copy-start.5 = (bf16[256,128]{1,0:T(8,128)(2,1)S(1)}, bf16[256,128]{1,0:T(8,128)(2,1)}, u32[]{:S(2)}) copy-start(bf16[256,128]{1,0:T(8,128)(2,1)} %get-tuple-element.99.picker_ref) | copy-start | bytes 196612
  106.6 25.6 %copy-start.6 = (f32[2048]{0:T(1024)S(1)}, f32[2048]{0:T(1024)}, u32[]{:S(2)}) copy-start(f32[2048]{0:T(1024)} %param.11) | copy-start | bytes 24580

commit v4 on v3

--- a/solution.py
+++ b/solution.py
@@ -20,7 +20,7 @@
 
 WHOLE = pl.BlockSpec(memory_space=pltpu.VMEM)
 PARAMS = pltpu.CompilerParams(vmem_limit_bytes=24 * 1024 * 1024)
-TAIL = 16
+TAIL = 128
 COST = pl.CostEstimate(flops=1, bytes_accessed=1, transcendentals=0)
 
 
@@ -162,6 +162,11 @@
         name="hidden",
     )(*parts, w0, w1)
     return [flat[3 * k : 3 * k + 3] for k in range(len(sets))]
+
+
+def lined(sums, part):
+    width = sums.shape[1]
+    return stack([sums[k : k + 1, at : at + part] for k in range(2) for at in range(0, width, part)])
 
 
 def block_kernel(n, sets, places, *refs):
@@ -191,13 +196,15 @@
     small = before_ref[...] + jnp.concatenate([col, gain], axis=0)
     small_ref[...] = small
     for k, (which, at) in enumerate(places):
-        dh_refs[which][at * half : (at + 1) * half, :] = dh[k * half : (k + 1) * half].astype(BF16)
+        lines = dh[k * half : (k + 1) * half].astype(BF16)
+        dh_refs[which][at * half : (at + 1) * half, : dh.shape[1]] = lines
     for ref in dh_refs:
-        if ref.shape[0] > 2 * half:
-            high = small.astype(BF16)
-            low = (small - high.astype(F32)).astype(BF16)
-            rest = jnp.zeros((TAIL - 4, small.shape[1]), BF16)
-            ref[2 * half :, :] = jnp.concatenate([high, low, rest], axis=0)
+        if ref.shape[1] > dh.shape[1]:
+            high = small.astype(BF16).astype(F32)
+            lines = [lined(value, TAIL) for value in (high, small - high)]
+            rest = ref.shape[0] - 2 * lines[0].shape[0]
+            lines.append(jnp.zeros((rest, TAIL), F32))
+            ref[:, dh.shape[1] :] = stack(lines).astype(BF16)
 
 
 def block(parts, mids, weights, before, places, tail=0):
@@ -207,7 +214,7 @@
     outs_n = len(parts) // 2
     flat = pl.pallas_call(
         functools.partial(block_kernel, len(parts), len(mids), places),
-        out_shape=[jax.ShapeDtypeStruct((2 * half + tail, width), BF16)] * outs_n
+        out_shape=[jax.ShapeDtypeStruct((2 * half, width + tail), BF16)] * outs_n
         + [jax.ShapeDtypeStruct((m, units), BF16)] * 3
         + [jax.ShapeDtypeStruct((2, width), F32)],
         in_specs=[WHOLE] * (len(parts) + 3 * len(mids) + 5),
@@ -239,15 +246,22 @@
 def expand_kernel(dh_ref, far_ref, home_ref, small_ref, *refs):
     *others, out_ref = refs
     rows, width = dh_ref.shape
-    dh = dh_ref[...] + far_ref[:rows, :].astype(F32)
+    dh = dh_ref[...] + far_ref[:, :width].astype(F32)
     out_ref[:, :width] = dot(home_ref[...], dh.astype(BF16)).astype(BF16)
-    carried = far_ref[rows:, :].astype(F32)
-    small = small_ref[...] + carried[0:2] + carried[2:4]
+    small = small_ref[...]
     for ref in others:
         small = small + ref[...]
     part = out_ref.shape[1] - width
-    lines = [small[k : k + 1, at : at + part] for k in range(2) for at in range(0, width, part)]
-    lines = jnp.concatenate(lines, axis=0).astype(BF16)
+    lines = lined(small, part)
+    count = 2 * width // TAIL
+    carried = far_ref[:, width:].astype(F32)
+    carried = carried[:count] + carried[count : 2 * count]
+    each = part // TAIL
+    pieces = [
+        jnp.concatenate([carried[q * each + k : q * each + k + 1] for k in range(each)], axis=1)
+        for q in range(lines.shape[0])
+    ]
+    lines = (lines + stack(pieces)).astype(BF16)
     out_ref[:, width:] = jnp.concatenate([lines] * (out_ref.shape[0] // lines.shape[0]), axis=0)
 
 

time: 134 us -> 133 us (level)
  no operation moved by 1% of the time
where the time goes in v4:
time: 133 us
  waiting for transfers between devices  48.7 us (37%)
  Pallas kernels  30.5 us (23%)
  starting transfers between devices  25.3 us (19%)
  blocking collectives  25.2 us (19%)
  local copies, waits for them, and re-layouts  1.78 us (1%)
    all_to_all x1, waiting for transfers between devices, exchange(): lax.all_to_all(value, 'expert', split_axis=0, concat_axis=0, tiled=True)  27.6 us
    all_to_all x1, blocking collectives, exchange(): lax.all_to_all(value, 'expert', split_axis=0, concat_axis=0, tiled=True)  25.2 us
    ppermute x11, waiting for transfers between devices, shift(): return lax.ppermute(value, axis, [(i, (i + by) % n) for i in range(n)])  21.1 us
    ppermute x11, starting transfers between devices, shift(): return lax.ppermute(value, axis, [(i, (i + by) % n) for i in range(n)])  15.4 us
    all_to_all x1, starting transfers between devices, exchange(): lax.all_to_all(value, 'expert', split_axis=0, concat_axis=0, tiled=True)  9.92 us
    pallas_call x3, Pallas kernels, block(): pl.pallas_call(functools.partial(block_kernel, len(parts), len(mids), pla...  9.43 us
    pallas_call x2, Pallas kernels, weight_grads(): pl.pallas_call(functools.partial(kernel, len(parts)), grid=(width // tile...  8.59 us
    pallas_call x3, Pallas kernels, hidden(): pl.pallas_call(functools.partial(hidden_kernel, len(parts)), out_shape=[j...  3.9 us
  transfers between devices with their start and end apart: 12, of which 5 were waited for; matrix products, arithmetic and copies ran while one was open for 1% of the time, Pallas kernels for 17%

profile of v4, /device:TPU:1, one launch (start us, length us, event | category | flops | bytes accessed | tf_op | source)
XLA Modules:
  0.0 133.1 jit_solution(11554615439211081487)
XLA Ops:
  0.6 3.5 %pick.1 = (bf16[512,2048]{1,0:T(8,128)(2,1)}, bf16[256,128]{1,0:T(8,128)(2,1)}) custom-call(bf16[128,2048]{1,0:T(8,128)(2,1)} %tokens_ref.3, bf16[128,2048]{1,0:T(8,128)(2,1)} %grad_ref.3, f32[1,2048]{1,0:T(1,128)} %bitcast.36, s32[8,32]{1,0:T(8,128)} %bitcast.40, s32[1,32]{1,0:T(1,128)} %count_ref.1), custom_call_target="tpu_custom_call" | custom-call | flops 1 | bytes 1 | tf_op jit(solution)/shard_map/pick/pallas_call | solution.py:71
  4.2 9.9 %all-to-all-start = ((bf16[32,16,2048]{2,1,0:T(8,128)(2,1)}), bf16[32,16,2048]{2,1,0:T(8,128)(2,1)}, u32[]{:S(2)}, u32[]{:S(2)}) async-start(bf16[32,16,2048]{2,1,0:T(8,128)(2,1)} %bitcast.39), calls=%async_computation | async-start | bytes 4194304 | tf_op jit(solution)/shard_map/all_to_all | solution.py:381
  14.1 0.8 bitcast_convert_fusion.refs_8_.refs_13_
  14.9 27.6 %all-to-all-done = bf16[32,16,2048]{2,1,0:T(8,128)(2,1)} async-done(((bf16[32,16,2048]{2,1,0:T(8,128)(2,1)}), bf16[32,16,2048]{2,1,0:T(8,128)(2,1)}, u32[]{:S(2)}, u32[]{:S(2)}) %all-to-all-start) | async-done | bytes 2097184 | tf_op jit(solution)/shard_map/all_to_all | solution.py:381
  42.5 3.0 %pack.1 = (bf16[128,2048]{1,0:T(8,128)(2,1)S(1)}, bf16[128,2048]{1,0:T(8,128)(2,1)S(1)}, bf16[256,128]{1,0:T(8,128)(2,1)S(1)}) custom-call(bf16[512,2048]{1,0:T(8,128)(2,1)} %bitcast.4.rows_ref), custom_call_target="tpu_custom_call" | custom-call | flops 1 | bytes 1 | tf_op jit(solution)/shard_map/pack/pallas_call | solution.py:112
  45.4 1.3 collective-permute-start
  46.7 1.5 %collective-permute-start.1 = (bf16[128,2048]{1,0:T(8,128)(2,1)S(1)}, bf16[128,2048]{1,0:T(8,128)(2,1)S(1)}, u32[]{:S(2)}, u32[]{:S(2)}) collective-permute-start(bf16[128,2048]{1,0:T(8,128)(2,1)S(1)} %get-tuple-element.59.refs_1_), channel_id=1, source_target_pairs={{0,96},{32,0},{64,32},{96,64},{1,97},{33,1},{65,33},{97,65},{2,98}... | collective-permute-start | bytes 1572872 | tf_op jit(solution)/shard_map/ppermute | solution.py:377
  48.2 0.0 collective-permute-start.2
  48.2 2.7 %collective-permute-start.3 = (bf16[128,2048]{1,0:T(8,128)(2,1)S(1)}, bf16[128,2048]{1,0:T(8,128)(2,1)S(1)}, u32[]{:S(2)}, u32[]{:S(2)}) collective-permute-start(bf16[128,2048]{1,0:T(8,128)(2,1)S(1)} %get-tuple-element.58.refs_0_), channel_id=1, source_target_pairs={{0,96},{32,0},{64,32},{96,64},{1,97},{33,1},{65,33},{97,65},{2,98}... | collective-permute-start | bytes 1572872 | tf_op jit(solution)/shard_map/ppermute | solution.py:377
  50.8 8.4 %collective-permute-done.refs_2_.refs_0_ = bf16[128,2048]{1,0:T(8,128)(2,1)S(1)} collective-permute-done((bf16[128,2048]{1,0:T(8,128)(2,1)S(1)}, bf16[128,2048]{1,0:T(8,128)(2,1)S(1)}, u32[]{:S(2)}, u32[]{:S(2)}) %collective-permute-start) | collective-permute-done | bytes 524320 | tf_op jit(solution)/shard_map/ppermute | solution.py:377
  59.3 2.7 %collective-permute-start.7 = (bf16[128,2048]{1,0:T(8,128)(2,1)S(1)}, bf16[128,2048]{1,0:T(8,128)(2,1)S(1)}, u32[]{:S(2)}, u32[]{:S(2)}) collective-permute-start(bf16[128,2048]{1,0:T(8,128)(2,1)S(1)} %collective-permute-done.1.refs_3_.refs_1_), channel_id=1, source_target_pairs={{0,96},{32,0},{64,32},{96,64},{1,97},{33,1},{65,33},{97,65},{2,98}... | collective-permute-start | bytes 1572872 | tf_op jit(solution)/shard_map/ppermute | solution.py:377
  62.0 1.7 %copy-done.1 = bf16[1,2048,640]{2,1,0:T(8,128)(2,1)S(1)} copy-done((bf16[1,2048,640]{2,1,0:T(8,128)(2,1)S(1)}, bf16[1,2048,640]{2,1,0:T(8,128)(2,1)}, u32[]{:S(2)}) %copy-start.1) | copy-done | bytes 2621464
  63.7 1.9 %hidden.3 = (f32[128,640]{1,0:T(8,128)S(1)}, f32[128,640]{1,0:T(8,128)S(1)}, f32[128,640]{1,0:T(8,128)S(1)}, f32[128,640]{1,0:T(8,128)S(1)}, f32[128,640]{1,0:T(8,128)S(1)}, /*index=5*/f32[128,640]{1,0:T(8,128)S(1)}) custom-call(bf16[128,2048]{1,0:T(8,128)(2,1)S(1)} %get-tuple-element.58.refs_0_, bf16[128,2048]{1,0:T(8,128)(2,1)S(1)} %get-tuple-element.59.refs_1_, ...), custom_call_target="tpu_custom_call" | custom-call | flops 1 | bytes 1 | tf_op jit(solution)/shard_map/hidden/pallas_call | solution.py:155
  65.6 2.9 %block.3 = (bf16[128,2048]{1,0:T(8,128)(2,1)S(1)}, bf16[128,640]{1,0:T(8,128)(2,1)S(1)}, bf16[128,640]{1,0:T(8,128)(2,1)S(1)}, bf16[128,640]{1,0:T(8,128)(2,1)S(1)}, f32[2,2048]{1,0:T(2,128)S(1)}) custom-call(bf16[128,2048]{1,0:T(8,128)(2,1)S(1)} %get-tuple-element.58.refs_0_, bf16[128,2048]{1,0:T(8,128)(2,1)S(1)} %get-tuple-element.59.refs_1_, ...), custom_call_target="tpu_custom_call" | custom-call | flops 1 | bytes 1 | tf_op jit(solution)/shard_map/block/pallas_call | solution.py:215
  68.5 2.0 %collective-permute-done.2.refs_0_.refs_2_.refs_4_ = bf16[128,2048]{1,0:T(8,128)(2,1)S(1)} collective-permute-done((bf16[128,2048]{1,0:T(8,128)(2,1)S(1)}, bf16[128,2048]{1,0:T(8,128)(2,1)S(1)}, u32[]{:S(2)}, u32[]{:S(2)}) %collective-permute-start.2) | collective-permute-done | bytes 524320 | tf_op jit(solution)/shard_map/ppermute | solution.py:377
  70.5 1.0 hidden.4
  71.5 3.5 %block.4 = (bf16[128,2048]{1,0:T(8,128)(2,1)S(1)}, bf16[128,2048]{1,0:T(8,128)(2,1)S(1)}, bf16[256,640]{1,0:T(8,128)(2,1)S(1)}, bf16[256,640]{1,0:T(8,128)(2,1)S...) custom-call(bf16[128,2048]{1,0:T(8,128)(2,1)S(1)} %collective-permute-done.refs_2_.refs_0_, ...), custom_call_target="tpu_custom_call" | custom-call | flops 1 | bytes 1 | tf_op jit(solution)/shard_map/block/pallas_call | solution.py:215
  75.1 2.4 %collective-permute-start.4 = (bf16[128,2048]{1,0:T(8,128)(2,1)S(1)}, bf16[128,2048]{1,0:T(8,128)(2,1)S(1)}, u32[]{:S(2)}, u32[]{:S(2)}) collective-permute-start(bf16[128,2048]{1,0:T(8,128)(2,1)S(1)} %get-tuple-element.75), channel_id=1, source_target_pairs={{0,96},{32,0},{64,32},{96,64},{1,97},{33,1},{65,33},{97,65},{2,98}... | collective-permute-start | bytes 1572872 | tf_op jit(solution)/shard_map/ppermute | solution.py:377
  77.5 4.2 %collective-permute-done.6.refs_0_.refs_6_ = bf16[128,2048]{1,0:T(8,128)(2,1)S(1)} collective-permute-done((bf16[128,2048]{1,0:T(8,128)(2,1)S(1)}, bf16[128,2048]{1,0:T(8,128)(2,1)S(1)}, u32[]{:S(2)}, u32[]{:S(2)}) %collective-permute-start.6) | collective-permute-done | bytes 524320 | tf_op jit(solution)/shard_map/ppermute | solution.py:377
  81.7 1.0 hidden.5
  82.8 3.0 %block.5 = (bf16[128,2176]{1,0:T(8,128)(2,1)S(1)}, bf16[128,640]{1,0:T(8,128)(2,1)S(1)}, bf16[128,640]{1,0:T(8,128)(2,1)S(1)}, bf16[128,640]{1,0:T(8,128)(2,1)S(1)}, f32[2,2048]{1,0:T(2,128)S(1)}) custom-call(bf16[128,2048]{1,0:T(8,128)(2,1)S(1)} %collective-permute-done.6.refs_0_.refs_6_, bf16[128,2048]{1,0:T(8,128)(2,1)S(1)} %collective-permute-done.7.refs_1_.refs_7_, ...), custom_call_target="tpu_custom_call" | custom-call | flops 1 | bytes 1 | tf_op jit(solution)/shard_map/block/pallas_call | solution.py:215
  85.7 2.2 %collective-permute-start.8 = (bf16[128,2176]{1,0:T(8,128)(2,1)S(1)}, bf16[128,2176]{1,0:T(8,128)(2,1)S(1)}, u32[]{:S(2)}, u32[]{:S(2)}) collective-permute-start(bf16[128,2176]{1,0:T(8,128)(2,1)S(1)} %get-tuple-element.84), channel_id=1, source_target_pairs={{0,64},{32,96},{64,0},{96,32},{1,65},{33,97},{65,1},{97,33},{2,66}... | collective-permute-start | bytes 1671176 | tf_op jit(solution)/shard_map/ppermute | solution.py:377
  87.9 0.8 collective-permute-start.9
  88.8 1.9 %collective-permute-start.10 = (f32[2,2048]{1,0:T(2,128)S(1)}, f32[2,2048]{1,0:T(2,128)S(1)}, u32[]{:S(2)}, u32[]{:S(2)}) collective-permute-start(f32[2,2048]{1,0:T(2,128)S(1)} %get-tuple-element.98.small_ref), channel_id=1, source_target_pairs={{0,96},{32,0},{64,32},{96,64},{1,97},{33,1},{65,33},{97,65},{2,98}... | collective-permute-start | bytes 49160 | tf_op jit(solution)/shard_map/ppermute | solution.py:377
  90.6 3.7 %weight_grads.3 = bf16[640,2048]{1,0:T(8,128)(2,1)} custom-call(bf16[128,2048]{1,0:T(8,128)(2,1)S(1)} %get-tuple-element.58.refs_0_, bf16[128,2048]{1,0:T(8,128)(2,1)S(1)} %get-tuple-element.59.refs_1_, bf16[128,2048]{1,0:T(8,128)(2,1)S(1)} %collective-permute-done.refs_2_.refs_0_, bf16[128,2048]{1,0:T(8,128)(2,1)S(1)} %collective-permute-done.1.refs_3_.refs_1_, ...), custom_call_target="tpu_custom_call" | custom-call | flops 2000000000 | bytes 1 | tf_op jit(solution)/shard_map/weight_grads/pallas_call | solution.py:356
  94.3 4.9 %weight_grads.2 = (bf16[2048,640]{1,0:T(8,128)(2,1)}, bf16[2048,640]{1,0:T(8,128)(2,1)}) custom-call(bf16[128,2048]{1,0:T(8,128)(2,1)S(1)} %get-tuple-element.58.refs_0_, bf16[128,2048]{1,0:T(8,128)(2,1)S(1)} %get-tuple-element.59.refs_1_, bf16[128,2048]{1,0:T(8,128)(2,1)S(1)} %collective-permute-done.refs_2_.refs_0_, ...), custom_call_target="tpu_custom_call" | custom-call | flops 2000000000 | bytes 1 | tf_op jit(solution)/shard_map/weight_grads/pallas_call | solution.py:356
  99.2 0.2 total_of.1.dh_ref
  99.4 6.5 %collective-permute-done.8.far_ref = bf16[128,2176]{1,0:T(8,128)(2,1)S(1)} collective-permute-done((bf16[128,2176]{1,0:T(8,128)(2,1)S(1)}, bf16[128,2176]{1,0:T(8,128)(2,1)S(1)}, u32[]{:S(2)}, u32[]{:S(2)}) %collective-permute-start.8) | collective-permute-done | bytes 557088 | tf_op jit(solution)/shard_map/ppermute | solution.py:377
  105.9 0.0 copy-start.4
  105.9 0.4 expand.1
  106.4 25.2 %all_to_all.10 = bf16[32,8,2560]{2,1,0:T(8,128)(2,1)S(1)} all-to-all(bf16[32,8,2560]{2,1,0:T(8,128)(2,1)S(1)} %bitcast.34), channel_id=1, replica_groups=mesh['dp'=4,'expert'=32] {'expert'}, dimensions={0} | all-to-all | bytes 2621440 | tf_op jit(solution)/shard_map/all_to_all | solution.py:381
  131.6 1.5 %finish.1 = (bf16[128,2048]{1,0:T(8,128)(2,1)}, f32[1,2048]{1,0:T(1,128)}, f32[32,2048]{1,0:T(8,128)}) custom-call(bf16[256,2560]{1,0:T(8,128)(2,1)S(1)} %bitcast.35, bf16[256,128]{1,0:T(8,128)(2,1)S(1)} %copy-done.5, bf16[128,2048]{1,0:T(8,128)(2,1)S(1)} %copy-done.3, bf16[128,2048]{1,0:T(8,128)(2,1)S(1)} %copy-done.4, f32[1,2048]{1,0:T(1,128)S(1)} %bitcast.37), custom_call_target="tpu_custom_call" | custom-call | flops 1 | bytes 1 | tf_op jit(solution)/shard_map/finish/pallas_call | solution.py:314
  (22 shorter events, 0.1 us)
Async XLA Ops:
  4.2 57.8 %copy-start = (bf16[1,2048,640]{2,1,0:T(8,128)(2,1)S(1)}, bf16[1,2048,640]{2,1,0:T(8,128)(2,1)}, u32[]{:S(2)}) copy-start(bf16[1,2048,640]{2,1,0:T(8,128)(2,1)} %param.13) | copy-start | bytes 7864324
  4.2 38.3 %all-to-all-start = ((bf16[32,16,2048]{2,1,0:T(8,128)(2,1)}), bf16[32,16,2048]{2,1,0:T(8,128)(2,1)}, u32[]{:S(2)}, u32[]{:S(2)}) async-start(bf16[32,16,2048]{2,1,0:T(8,128)(2,1)} %bitcast.39), calls=%async_computation | async-start | bytes 4194304 | tf_op jit(solution)/shard_map/all_to_all | solution.py:381
  45.4 13.9 %collective-permute-start = (bf16[128,2048]{1,0:T(8,128)(2,1)S(1)}, bf16[128,2048]{1,0:T(8,128)(2,1)S(1)}, u32[]{:S(2)}, u32[]{:S(2)}) collective-permute-start(bf16[128,2048]{1,0:T(8,128)(2,1)S(1)} %get-tuple-element.58.refs_0_), channel_id=1, source_target_pairs={{0,32},{32,64},{64,96},{96,0},{1,33},{33,65},{65,97},{97,1},{2,34}... | collective-permute-start | bytes 1572872 | tf_op jit(solution)/shard_map/ppermute | solution.py:377
  46.7 12.6 %collective-permute-start.1 = (bf16[128,2048]{1,0:T(8,128)(2,1)S(1)}, bf16[128,2048]{1,0:T(8,128)(2,1)S(1)}, u32[]{:S(2)}, u32[]{:S(2)}) collective-permute-start(bf16[128,2048]{1,0:T(8,128)(2,1)S(1)} %get-tuple-element.59.refs_1_), channel_id=1, source_target_pairs={{0,96},{32,0},{64,32},{96,64},{1,97},{33,1},{65,33},{97,65},{2,98}... | collective-permute-start | bytes 1572872 | tf_op jit(solution)/shard_map/ppermute | solution.py:377
  48.2 22.3 %collective-permute-start.2 = (bf16[128,2048]{1,0:T(8,128)(2,1)S(1)}, bf16[128,2048]{1,0:T(8,128)(2,1)S(1)}, u32[]{:S(2)}, u32[]{:S(2)}) collective-permute-start(bf16[128,2048]{1,0:T(8,128)(2,1)S(1)} %get-tuple-element.59.refs_1_), channel_id=1, source_target_pairs={{0,32},{32,64},{64,96},{96,0},{1,33},{33,65},{65,97},{97,1},{2,34}... | collective-permute-start | bytes 1572872 | tf_op jit(solution)/shard_map/ppermute | solution.py:377
  48.2 22.3 %collective-permute-start.3 = (bf16[128,2048]{1,0:T(8,128)(2,1)S(1)}, bf16[128,2048]{1,0:T(8,128)(2,1)S(1)}, u32[]{:S(2)}, u32[]{:S(2)}) collective-permute-start(bf16[128,2048]{1,0:T(8,128)(2,1)S(1)} %get-tuple-element.58.refs_0_), channel_id=1, source_target_pairs={{0,96},{32,0},{64,32},{96,64},{1,97},{33,1},{65,33},{97,65},{2,98}... | collective-permute-start | bytes 1572872 | tf_op jit(solution)/shard_map/ppermute | solution.py:377
  59.3 22.5 %collective-permute-start.6 = (bf16[128,2048]{1,0:T(8,128)(2,1)S(1)}, bf16[128,2048]{1,0:T(8,128)(2,1)S(1)}, u32[]{:S(2)}, u32[]{:S(2)}) collective-permute-start(bf16[128,2048]{1,0:T(8,128)(2,1)S(1)} %collective-permute-done.refs_2_.refs_0_), channel_id=1, source_target_pairs={{0,32},{32,64},{64,96},{96,0},{1,33},{33,65},{65,97},{97,1},{2,34}... | collective-permute-start | bytes 1572872 | tf_op jit(solution)/shard_map/ppermute | solution.py:377
  59.3 22.5 %collective-permute-start.7 = (bf16[128,2048]{1,0:T(8,128)(2,1)S(1)}, bf16[128,2048]{1,0:T(8,128)(2,1)S(1)}, u32[]{:S(2)}, u32[]{:S(2)}) collective-permute-start(bf16[128,2048]{1,0:T(8,128)(2,1)S(1)} %collective-permute-done.1.refs_3_.refs_1_), channel_id=1, source_target_pairs={{0,96},{32,0},{64,32},{96,64},{1,97},{33,1},{65,33},{97,65},{2,98}... | collective-permute-start | bytes 1572872 | tf_op jit(solution)/shard_map/ppermute | solution.py:377
  62.0 1.7 %copy-start.1 = (bf16[1,2048,640]{2,1,0:T(8,128)(2,1)S(1)}, bf16[1,2048,640]{2,1,0:T(8,128)(2,1)}, u32[]{:S(2)}) copy-start(bf16[1,2048,640]{2,1,0:T(8,128)(2,1)} %param.14) | copy-start | bytes 7864324
  63.7 1.9 %copy-start.2 = (bf16[1,640,2048]{2,1,0:T(8,128)(2,1)S(1)}, bf16[1,640,2048]{2,1,0:T(8,128)(2,1)}, u32[]{:S(2)}) copy-start(bf16[1,640,2048]{2,1,0:T(8,128)(2,1)} %param.15) | copy-start | bytes 7864324
  75.1 24.1 %collective-permute-start.4 = (bf16[128,2048]{1,0:T(8,128)(2,1)S(1)}, bf16[128,2048]{1,0:T(8,128)(2,1)S(1)}, u32[]{:S(2)}, u32[]{:S(2)}) collective-permute-start(bf16[128,2048]{1,0:T(8,128)(2,1)S(1)} %get-tuple-element.75), channel_id=1, source_target_pairs={{0,96},{32,0},{64,32},{96,64},{1,97},{33,1},{65,33},{97,65},{2,98}... | collective-permute-start | bytes 1572872 | tf_op jit(solution)/shard_map/ppermute | solution.py:377
  77.5 21.7 %collective-permute-start.5 = (bf16[128,2048]{1,0:T(8,128)(2,1)S(1)}, bf16[128,2048]{1,0:T(8,128)(2,1)S(1)}, u32[]{:S(2)}, u32[]{:S(2)}) collective-permute-start(bf16[128,2048]{1,0:T(8,128)(2,1)S(1)} %get-tuple-element.76), channel_id=1, source_target_pairs={{0,32},{32,64},{64,96},{96,0},{1,33},{33,65},{65,97},{97,1},{2,34}... | collective-permute-start | bytes 1572872 | tf_op jit(solution)/shard_map/ppermute | solution.py:377
  85.7 20.2 %collective-permute-start.8 = (bf16[128,2176]{1,0:T(8,128)(2,1)S(1)}, bf16[128,2176]{1,0:T(8,128)(2,1)S(1)}, u32[]{:S(2)}, u32[]{:S(2)}) collective-permute-start(bf16[128,2176]{1,0:T(8,128)(2,1)S(1)} %get-tuple-element.84), channel_id=1, source_target_pairs={{0,64},{32,96},{64,0},{96,32},{1,65},{33,97},{65,1},{97,33},{2,66}... | collective-permute-start | bytes 1671176 | tf_op jit(solution)/shard_map/ppermute | solution.py:377
  87.9 18.0 %collective-permute-start.9 = (f32[2,2048]{1,0:T(2,128)S(1)}, f32[2,2048]{1,0:T(2,128)S(1)}, u32[]{:S(2)}, u32[]{:S(2)}) collective-permute-start(f32[2,2048]{1,0:T(2,128)S(1)} %get-tuple-element.98.small_ref), channel_id=1, source_target_pairs={{0,32},{32,64},{64,96},{96,0},{1,33},{33,65},{65,97},{97,1},{2,34}... | collective-permute-start | bytes 49160 | tf_op jit(solution)/shard_map/ppermute | solution.py:377
  88.8 17.1 %collective-permute-start.10 = (f32[2,2048]{1,0:T(2,128)S(1)}, f32[2,2048]{1,0:T(2,128)S(1)}, u32[]{:S(2)}, u32[]{:S(2)}) collective-permute-start(f32[2,2048]{1,0:T(2,128)S(1)} %get-tuple-element.98.small_ref), channel_id=1, source_target_pairs={{0,96},{32,0},{64,32},{96,64},{1,97},{33,1},{65,33},{97,65},{2,98}... | collective-permute-start | bytes 49160 | tf_op jit(solution)/shard_map/ppermute | solution.py:377
  105.9 25.6 %copy-start.3 = (bf16[128,2048]{1,0:T(8,128)(2,1)S(1)}, bf16[128,2048]{1,0:T(8,128)(2,1)}, u32[]{:S(2)}) copy-start(bf16[128,2048]{1,0:T(8,128)(2,1)} %tokens_ref.3) | copy-start | bytes 1572868
  105.9 25.6 %copy-start.4 = (bf16[128,2048]{1,0:T(8,128)(2,1)S(1)}, bf16[128,2048]{1,0:T(8,128)(2,1)}, u32[]{:S(2)}) copy-start(bf16[128,2048]{1,0:T(8,128)(2,1)} %grad_ref.3) | copy-start | bytes 1572868
  105.9 25.6 %copy-start.5 = (bf16[256,128]{1,0:T(8,128)(2,1)S(1)}, bf16[256,128]{1,0:T(8,128)(2,1)}, u32[]{:S(2)}) copy-start(bf16[256,128]{1,0:T(8,128)(2,1)} %get-tuple-element.99.picker_ref) | copy-start | bytes 196612
  105.9 25.6 %copy-start.6 = (f32[2048]{0:T(1024)S(1)}, f32[2048]{0:T(1024)}, u32[]{:S(2)}) copy-start(f32[2048]{0:T(1024)} %param.11) | copy-start | bytes 24580

commit v5 on v4

--- a/solution.py
+++ b/solution.py
@@ -49,8 +49,8 @@
     return iota((total, tok_dev), 1).astype(F32) == name, live
 
 
-def pick_kernel(tokens_ref, grad_ref, gain_ref, slot_rows_ref, count_ref, slots_ref, picker_ref):
-    tok_dev = picker_ref.shape[1]
+def pick_kernel(tokens_ref, grad_ref, gain_ref, slot_rows_ref, count_ref, slots_ref):
+    tok_dev = tokens_ref.shape[0]
     slots = slot_rows_ref.shape[0]
     tok = tokens_ref[...].astype(F32)
     inv_rms = lax.rsqrt(jnp.mean(tok * tok, axis=1, keepdims=True) + 1e-06)
@@ -61,8 +61,6 @@
     rows = dot(both, jnp.concatenate([normed, grad_ref[...]], axis=0))
     slots_ref[...] = rows.astype(BF16)
     slots_ref[:, :128] = jnp.where(live, rows[:, :128], DEAD).astype(BF16)
-    hot, _ = one_hot_of_slots(slot_rows_ref, count_ref, tok_dev, 1)
-    picker_ref[...] = hot.astype(BF16)
 
 
 def pick(tokens, grad_out, norm_gain, slot_rows, slot_count):
@@ -70,21 +68,57 @@
     tok_dev, width = tokens.shape
     return pl.pallas_call(
         pick_kernel,
-        out_shape=(
-            jax.ShapeDtypeStruct((2 * total, width), BF16),
-            jax.ShapeDtypeStruct((total, tok_dev), BF16),
-        ),
+        out_shape=jax.ShapeDtypeStruct((2 * total, width), BF16),
         in_specs=[WHOLE] * 5,
-        out_specs=[WHOLE] * 2,
+        out_specs=WHOLE,
         compiler_params=pltpu.CompilerParams(vmem_limit_bytes=56 * 1024 * 1024),
         cost_estimate=COST,
         name="pick",
     )(tokens, grad_out, norm_gain, slot_rows, slot_count)
 
 
-def pack_kernel(slots, rows_ref, first_ref, second_ref, home_ref):
-    both = rows_ref.shape[0]
+def picker_kernel(slot_rows_ref, count_ref, picker_ref):
+    hot, _ = one_hot_of_slots(slot_rows_ref, count_ref, picker_ref.shape[1], 1)
+    picker_ref[...] = hot.astype(BF16)
+
+
+def picker_of(slot_rows, slot_count, tok_dev):
+    total = slot_rows.shape[0] * slot_rows.shape[1]
+    return pl.pallas_call(
+        picker_kernel,
+        out_shape=jax.ShapeDtypeStruct((total, tok_dev), BF16),
+        in_specs=[WHOLE] * 2,
+        out_specs=WHOLE,
+        compiler_params=PARAMS,
+        cost_estimate=COST,
+        name="picker_of",
+    )(slot_rows, slot_count)
+
+
+def home_kernel(slots, place_ref, home_ref):
     total, live_rows = home_ref.shape
+    slot = iota((total, 1), 0)
+    source = slot // slots * (2 * slots) + slot % slots
+    mine = (iota((total, 2 * total), 1) == source).astype(BF16)
+    home_ref[...] = dot(mine, place_ref[:, :live_rows]).astype(BF16)
+
+
+def home_of(place, slots):
+    both, total = place.shape
+    return pl.pallas_call(
+        functools.partial(home_kernel, slots),
+        out_shape=jax.ShapeDtypeStruct((total, total // 2), BF16),
+        in_specs=[WHOLE],
+        out_specs=WHOLE,
+        compiler_params=PARAMS,
+        cost_estimate=COST,
+        name="home_of",
+    )(place)
+
+
+def pack_kernel(slots, rows_ref, first_ref, second_ref, place_ref):
+    both, total = place_ref.shape
+    live_rows = total // 2
     half = live_rows // 2
     line = iota((both, 1), 0)
     kind = line // slots % 2
@@ -100,10 +134,7 @@
     first_ref[half:, :] = live[live_rows : live_rows + half]
     second_ref[:half, :] = live[half:live_rows]
     second_ref[half:, :] = live[live_rows + half :]
-    slot = iota((total, 1), 0)
-    source = slot // slots * (2 * slots) + slot % slots
-    mine = (iota((total, both), 1) == source).astype(BF16)
-    home_ref[...] = dot(mine, home[:, :live_rows]).astype(BF16)
+    place_ref[...] = home
 
 
 def pack(rows, slots):
@@ -114,7 +145,7 @@
         out_shape=(
             jax.ShapeDtypeStruct((total // 2, width), BF16),
             jax.ShapeDtypeStruct((total // 2, width), BF16),
-            jax.ShapeDtypeStruct((total, total // 2), BF16),
+            jax.ShapeDtypeStruct((both, total), BF16),
         ),
         in_specs=[WHOLE],
         out_specs=[WHOLE] * 3,
@@ -390,12 +421,12 @@
 
     expert = lax.axis_index("expert")
     rrow = lax.dynamic_slice_in_dim(router.T, expert, 1, axis=0).astype(F32)
-    both, picker = pick(
-        tokens, grad_out, norm_gain.reshape(1, width), slot_rows[0].T, slot_count
-    )
+    names = slot_rows[0].T
+    both = pick(tokens, grad_out, norm_gain.reshape(1, width), names, slot_count)
+    picker = picker_of(names, slot_count, tok_dev)
     both = exchange(both.reshape(experts, 2 * slots, width)).reshape(2 * total, width)
-    both, rrow = lax.optimization_barrier((both, rrow))
-    first, second, home = pack(both, slots)
+    both, rrow, picker = lax.optimization_barrier((both, rrow, picker))
+    first, second, place = pack(both, slots)
     weights = (w0, w1, wo, rrow)
     early = [shift(first, "dp", 1), shift(second, "dp", -1)]
     late = [shift(second, "dp", 1), shift(first, "dp", -1)]
@@ -406,10 +437,12 @@
     (dh_own,), grads_own, small = block([first, second], [mid_own], weights, small, one)
     late, small = lax.optimization_barrier((late, small))
     (mid_late,) = hidden([late], w0, w1)
+    place, small = lax.optimization_barrier((place, small))
+    home = home_of(place, slots)
     dh_near, grads_near, small = block(
         early + late, [mid_early, mid_late], weights, small, ((0, 0), (1, 1), (0, 1), (1, 0))
     )
-    far, small = lax.optimization_barrier((far, small))
+    far, small, home = lax.optimization_barrier((far, small, home))
     (mid_far,) = hidden([far], w0, w1)
     (dh_far,), grads_far, small = block(far, [mid_far], weights, small, one, TAIL)
     back_near = [shift(dh_near[0], "dp", -1), shift(dh_near[1], "dp", 1)]

time: 133 us -> 133 us (level)
    pallas_call x1 -> x3, Pallas kernels: 3.55 us -> 3.98 us  [the longest x1 3.53 us: pick(): pl.pallas_call(pick_kernel, out_shape=jax.ShapeDtypeStruct((2 * total, wi...]
where the time goes in v5:
time: 133 us
  waiting for transfers between devices  48.2 us (36%)
  Pallas kernels  30.9 us (23%)
  starting transfers between devices  25.4 us (19%)
  blocking collectives  25.2 us (19%)
  local copies, waits for them, and re-layouts  1.77 us (1%)
    all_to_all x1, waiting for transfers between devices, exchange(): lax.all_to_all(value, 'expert', split_axis=0, concat_axis=0, tiled=True)  27.3 us
    all_to_all x1, blocking collectives, exchange(): lax.all_to_all(value, 'expert', split_axis=0, concat_axis=0, tiled=True)  25.2 us
    ppermute x11, waiting for transfers between devices, shift(): return lax.ppermute(value, axis, [(i, (i + by) % n) for i in range(n)])  20.9 us
    ppermute x11, starting transfers between devices, shift(): return lax.ppermute(value, axis, [(i, (i + by) % n) for i in range(n)])  15.4 us
    all_to_all x1, starting transfers between devices, exchange(): lax.all_to_all(value, 'expert', split_axis=0, concat_axis=0, tiled=True)  9.93 us
    pallas_call x3, Pallas kernels, block(): pl.pallas_call(functools.partial(block_kernel, len(parts), len(mids), pla...  9.43 us
    pallas_call x2, Pallas kernels, weight_grads(): pl.pallas_call(functools.partial(kernel, len(parts)), grid=(width // tile...  8.6 us
    pallas_call x3, Pallas kernels, hidden(): pl.pallas_call(functools.partial(hidden_kernel, len(parts)), out_shape=[j...  3.89 us
  transfers between devices with their start and end apart: 12, of which 5 were waited for; matrix products, arithmetic and copies ran while one was open for 1% of the time, Pallas kernels for 17%

profile of v5, /device:TPU:1, one launch (start us, length us, event | category | flops | bytes accessed | tf_op | source)
XLA Modules:
  0.0 132.9 jit_solution(12723827345325234020)
XLA Ops:
  0.6 3.5 %pick.1 = bf16[512,2048]{1,0:T(8,128)(2,1)} custom-call(bf16[128,2048]{1,0:T(8,128)(2,1)} %tokens_ref.3, bf16[128,2048]{1,0:T(8,128)(2,1)} %grad_ref.3, f32[1,2048]{1,0:T(1,128)} %bitcast.36, s32[8,32]{1,0:T(8,128)} %bitcast.38, s32[1,32]{1,0:T(1,128)} %count_ref.3), custom_call_target="tpu_custom_call" | custom-call | flops 1 | bytes 1 | tf_op jit(solution)/shard_map/pick/pallas_call | solution.py:69
  4.2 9.9 %all-to-all-start = ((bf16[32,16,2048]{2,1,0:T(8,128)(2,1)}), bf16[32,16,2048]{2,1,0:T(8,128)(2,1)}, u32[]{:S(2)}, u32[]{:S(2)}) async-start(bf16[32,16,2048]{2,1,0:T(8,128)(2,1)} %bitcast.40), calls=%async_computation | async-start | bytes 4194304 | tf_op jit(solution)/shard_map/all_to_all | solution.py:412
  14.1 0.2 picker_of.1.picker_ref
  14.4 0.8 bitcast_convert_fusion.refs_8_.refs_13_
  15.1 27.3 %all-to-all-done = bf16[32,16,2048]{2,1,0:T(8,128)(2,1)} async-done(((bf16[32,16,2048]{2,1,0:T(8,128)(2,1)}), bf16[32,16,2048]{2,1,0:T(8,128)(2,1)}, u32[]{:S(2)}, u32[]{:S(2)}) %all-to-all-start) | async-done | bytes 2097184 | tf_op jit(solution)/shard_map/all_to_all | solution.py:412
  42.5 2.9 %pack.1 = (bf16[128,2048]{1,0:T(8,128)(2,1)S(1)}, bf16[128,2048]{1,0:T(8,128)(2,1)S(1)}, bf16[512,256]{1,0:T(8,128)(2,1)S(1)}) custom-call(bf16[512,2048]{1,0:T(8,128)(2,1)} %bitcast.4.rows_ref), custom_call_target="tpu_custom_call" | custom-call | flops 1 | bytes 1 | tf_op jit(solution)/shard_map/pack/pallas_call | solution.py:143
  45.3 1.3 collective-permute-start
  46.6 1.5 %collective-permute-start.1 = (bf16[128,2048]{1,0:T(8,128)(2,1)S(1)}, bf16[128,2048]{1,0:T(8,128)(2,1)S(1)}, u32[]{:S(2)}, u32[]{:S(2)}) collective-permute-start(bf16[128,2048]{1,0:T(8,128)(2,1)S(1)} %get-tuple-element.60.refs_1_), channel_id=1, source_target_pairs={{0,96},{32,0},{64,32},{96,64},{1,97},{33,1},{65,33},{97,65},{2,98}... | collective-permute-start | bytes 1572872 | tf_op jit(solution)/shard_map/ppermute | solution.py:408
  48.1 2.7 %collective-permute-start.3 = (bf16[128,2048]{1,0:T(8,128)(2,1)S(1)}, bf16[128,2048]{1,0:T(8,128)(2,1)S(1)}, u32[]{:S(2)}, u32[]{:S(2)}) collective-permute-start(bf16[128,2048]{1,0:T(8,128)(2,1)S(1)} %get-tuple-element.59.refs_0_), channel_id=1, source_target_pairs={{0,96},{32,0},{64,32},{96,64},{1,97},{33,1},{65,33},{97,65},{2,98}... | collective-permute-start | bytes 1572872 | tf_op jit(solution)/shard_map/ppermute | solution.py:408
  50.8 8.4 %collective-permute-done.refs_2_.refs_0_ = bf16[128,2048]{1,0:T(8,128)(2,1)S(1)} collective-permute-done((bf16[128,2048]{1,0:T(8,128)(2,1)S(1)}, bf16[128,2048]{1,0:T(8,128)(2,1)S(1)}, u32[]{:S(2)}, u32[]{:S(2)}) %collective-permute-start) | collective-permute-done | bytes 524320 | tf_op jit(solution)/shard_map/ppermute | solution.py:408
  59.2 2.7 %collective-permute-start.7 = (bf16[128,2048]{1,0:T(8,128)(2,1)S(1)}, bf16[128,2048]{1,0:T(8,128)(2,1)S(1)}, u32[]{:S(2)}, u32[]{:S(2)}) collective-permute-start(bf16[128,2048]{1,0:T(8,128)(2,1)S(1)} %collective-permute-done.1.refs_3_.refs_1_), channel_id=1, source_target_pairs={{0,96},{32,0},{64,32},{96,64},{1,97},{33,1},{65,33},{97,65},{2,98}... | collective-permute-start | bytes 1572872 | tf_op jit(solution)/shard_map/ppermute | solution.py:408
  61.9 1.7 %copy-done.1 = bf16[1,2048,640]{2,1,0:T(8,128)(2,1)S(1)} copy-done((bf16[1,2048,640]{2,1,0:T(8,128)(2,1)S(1)}, bf16[1,2048,640]{2,1,0:T(8,128)(2,1)}, u32[]{:S(2)}) %copy-start.1) | copy-done | bytes 2621464
  63.6 1.9 %hidden.3 = (f32[128,640]{1,0:T(8,128)S(1)}, f32[128,640]{1,0:T(8,128)S(1)}, f32[128,640]{1,0:T(8,128)S(1)}, f32[128,640]{1,0:T(8,128)S(1)}, f32[128,640]{1,0:T(8,128)S(1)}, /*index=5*/f32[128,640]{1,0:T(8,128)S(1)}) custom-call(bf16[128,2048]{1,0:T(8,128)(2,1)S(1)} %get-tuple-element.59.refs_0_, bf16[128,2048]{1,0:T(8,128)(2,1)S(1)} %get-tuple-element.60.refs_1_, ...), custom_call_target="tpu_custom_call" | custom-call | flops 1 | bytes 1 | tf_op jit(solution)/shard_map/hidden/pallas_call | solution.py:186
  65.5 2.9 %block.3 = (bf16[128,2048]{1,0:T(8,128)(2,1)S(1)}, bf16[128,640]{1,0:T(8,128)(2,1)S(1)}, bf16[128,640]{1,0:T(8,128)(2,1)S(1)}, bf16[128,640]{1,0:T(8,128)(2,1)S(1)}, f32[2,2048]{1,0:T(2,128)S(1)}) custom-call(bf16[128,2048]{1,0:T(8,128)(2,1)S(1)} %get-tuple-element.59.refs_0_, bf16[128,2048]{1,0:T(8,128)(2,1)S(1)} %get-tuple-element.60.refs_1_, ...), custom_call_target="tpu_custom_call" | custom-call | flops 1 | bytes 1 | tf_op jit(solution)/shard_map/block/pallas_call | solution.py:246
  68.5 2.0 %collective-permute-done.2.refs_0_.refs_2_.refs_4_ = bf16[128,2048]{1,0:T(8,128)(2,1)S(1)} collective-permute-done((bf16[128,2048]{1,0:T(8,128)(2,1)S(1)}, bf16[128,2048]{1,0:T(8,128)(2,1)S(1)}, u32[]{:S(2)}, u32[]{:S(2)}) %collective-permute-start.2) | collective-permute-done | bytes 524320 | tf_op jit(solution)/shard_map/ppermute | solution.py:408
  70.4 1.0 hidden.4
  71.4 3.5 %block.4 = (bf16[128,2048]{1,0:T(8,128)(2,1)S(1)}, bf16[128,2048]{1,0:T(8,128)(2,1)S(1)}, bf16[256,640]{1,0:T(8,128)(2,1)S(1)}, bf16[256,640]{1,0:T(8,128)(2,1)S...) custom-call(bf16[128,2048]{1,0:T(8,128)(2,1)S(1)} %collective-permute-done.refs_2_.refs_0_, ...), custom_call_target="tpu_custom_call" | custom-call | flops 1 | bytes 1 | tf_op jit(solution)/shard_map/block/pallas_call | solution.py:246
  75.0 2.4 %collective-permute-start.4 = (bf16[128,2048]{1,0:T(8,128)(2,1)S(1)}, bf16[128,2048]{1,0:T(8,128)(2,1)S(1)}, u32[]{:S(2)}, u32[]{:S(2)}) collective-permute-start(bf16[128,2048]{1,0:T(8,128)(2,1)S(1)} %get-tuple-element.78), channel_id=1, source_target_pairs={{0,96},{32,0},{64,32},{96,64},{1,97},{33,1},{65,33},{97,65},{2,98}... | collective-permute-start | bytes 1572872 | tf_op jit(solution)/shard_map/ppermute | solution.py:408
  77.4 0.2 home_of.1.home_ref
  77.6 4.0 %collective-permute-done.6.refs_0_.refs_6_ = bf16[128,2048]{1,0:T(8,128)(2,1)S(1)} collective-permute-done((bf16[128,2048]{1,0:T(8,128)(2,1)S(1)}, bf16[128,2048]{1,0:T(8,128)(2,1)S(1)}, u32[]{:S(2)}, u32[]{:S(2)}) %collective-permute-start.6) | collective-permute-done | bytes 524320 | tf_op jit(solution)/shard_map/ppermute | solution.py:408
  81.7 1.0 hidden.5
  82.7 3.0 %block.5 = (bf16[128,2176]{1,0:T(8,128)(2,1)S(1)}, bf16[128,640]{1,0:T(8,128)(2,1)S(1)}, bf16[128,640]{1,0:T(8,128)(2,1)S(1)}, bf16[128,640]{1,0:T(8,128)(2,1)S(1)}, f32[2,2048]{1,0:T(2,128)S(1)}) custom-call(bf16[128,2048]{1,0:T(8,128)(2,1)S(1)} %collective-permute-done.6.refs_0_.refs_6_, bf16[128,2048]{1,0:T(8,128)(2,1)S(1)} %collective-permute-done.7.refs_1_.refs_7_, ...), custom_call_target="tpu_custom_call" | custom-call | flops 1 | bytes 1 | tf_op jit(solution)/shard_map/block/pallas_call | solution.py:246
  85.6 2.2 %collective-permute-start.8 = (bf16[128,2176]{1,0:T(8,128)(2,1)S(1)}, bf16[128,2176]{1,0:T(8,128)(2,1)S(1)}, u32[]{:S(2)}, u32[]{:S(2)}) collective-permute-start(bf16[128,2176]{1,0:T(8,128)(2,1)S(1)} %get-tuple-element.88), channel_id=1, source_target_pairs={{0,64},{32,96},{64,0},{96,32},{1,65},{33,97},{65,1},{97,33},{2,66}... | collective-permute-start | bytes 1671176 | tf_op jit(solution)/shard_map/ppermute | solution.py:408
  87.9 0.8 collective-permute-start.9
  88.7 1.9 %collective-permute-start.10 = (f32[2,2048]{1,0:T(2,128)S(1)}, f32[2,2048]{1,0:T(2,128)S(1)}, u32[]{:S(2)}, u32[]{:S(2)}) collective-permute-start(f32[2,2048]{1,0:T(2,128)S(1)} %get-tuple-element.102.small_ref), channel_id=1, source_target_pairs={{0,96},{32,0},{64,32},{96,64},{1,97},{33,1},{65,33},{97,65},{2,98}... | collective-permute-start | bytes 49160 | tf_op jit(solution)/shard_map/ppermute | solution.py:408
  90.5 3.7 %weight_grads.3 = bf16[640,2048]{1,0:T(8,128)(2,1)} custom-call(bf16[128,2048]{1,0:T(8,128)(2,1)S(1)} %get-tuple-element.59.refs_0_, bf16[128,2048]{1,0:T(8,128)(2,1)S(1)} %get-tuple-element.60.refs_1_, bf16[128,2048]{1,0:T(8,128)(2,1)S(1)} %collective-permute-done.refs_2_.refs_0_, bf16[128,2048]{1,0:T(8,128)(2,1)S(1)} %collective-permute-done.1.refs_3_.refs_1_, ...), custom_call_target="tpu_custom_call" | custom-call | flops 2000000000 | bytes 1 | tf_op jit(solution)/shard_map/weight_grads/pallas_call | solution.py:387
  94.2 4.9 %weight_grads.2 = (bf16[2048,640]{1,0:T(8,128)(2,1)}, bf16[2048,640]{1,0:T(8,128)(2,1)}) custom-call(bf16[128,2048]{1,0:T(8,128)(2,1)S(1)} %get-tuple-element.59.refs_0_, bf16[128,2048]{1,0:T(8,128)(2,1)S(1)} %get-tuple-element.60.refs_1_, bf16[128,2048]{1,0:T(8,128)(2,1)S(1)} %collective-permute-done.refs_2_.refs_0_, ...), custom_call_target="tpu_custom_call" | custom-call | flops 2000000000 | bytes 1 | tf_op jit(solution)/shard_map/weight_grads/pallas_call | solution.py:387
  99.1 0.2 total_of.1.dh_ref
  99.3 6.5 %collective-permute-done.8.far_ref = bf16[128,2176]{1,0:T(8,128)(2,1)S(1)} collective-permute-done((bf16[128,2176]{1,0:T(8,128)(2,1)S(1)}, bf16[128,2176]{1,0:T(8,128)(2,1)S(1)}, u32[]{:S(2)}, u32[]{:S(2)}) %collective-permute-start.8) | collective-permute-done | bytes 557088 | tf_op jit(solution)/shard_map/ppermute | solution.py:408
  105.8 0.4 expand.1
  106.3 25.2 %all_to_all.10 = bf16[32,8,2560]{2,1,0:T(8,128)(2,1)S(1)} all-to-all(bf16[32,8,2560]{2,1,0:T(8,128)(2,1)S(1)} %bitcast.34), channel_id=1, replica_groups=mesh['dp'=4,'expert'=32] {'expert'}, dimensions={0} | all-to-all | bytes 2621440 | tf_op jit(solution)/shard_map/all_to_all | solution.py:412
  131.4 1.5 %finish.1 = (bf16[128,2048]{1,0:T(8,128)(2,1)}, f32[1,2048]{1,0:T(1,128)}, f32[32,2048]{1,0:T(8,128)}) custom-call(bf16[256,2560]{1,0:T(8,128)(2,1)S(1)} %bitcast.35, bf16[256,128]{1,0:T(8,128)(2,1)S(1)} %picker_of.1.picker_ref, bf16[128,2048]{1,0:T(8,128)(2,1)S(1)} %copy-done.3, bf16[128,2048]{1,0:T(8,128)(2,1)S(1)} %copy-done.4, f32[1,2048]{1,0:T(1,128)S(1)} %bitcast.37), custom_call_target="tpu_custom_call" | custom-call | flops 1 | bytes 1 | tf_op jit(solution)/shard_map/finish/pallas_call | solution.py:345
  (26 shorter events, 0.1 us)
Async XLA Ops:
  4.2 9.9 %copy-start.6 = (s32[1,32,8]{1,2,0:T(8,128)S(1)}, s32[1,32,8]{1,2,0:T(8,128)}, u32[]{:S(2)}) copy-start(s32[1,32,8]{1,2,0:T(8,128)} %param.16) | copy-start | bytes 3076
  4.2 10.0 %copy-start.7 = (s32[1,32]{1,0:T(1,128)S(1)}, s32[1,32]{1,0:T(1,128)}, u32[]{:S(2)}) copy-start(s32[1,32]{1,0:T(1,128)} %count_ref.3) | copy-start | bytes 388
  4.2 57.7 %copy-start = (bf16[1,2048,640]{2,1,0:T(8,128)(2,1)S(1)}, bf16[1,2048,640]{2,1,0:T(8,128)(2,1)}, u32[]{:S(2)}) copy-start(bf16[1,2048,640]{2,1,0:T(8,128)(2,1)} %param.13) | copy-start | bytes 7864324
  4.2 38.3 %all-to-all-start = ((bf16[32,16,2048]{2,1,0:T(8,128)(2,1)}), bf16[32,16,2048]{2,1,0:T(8,128)(2,1)}, u32[]{:S(2)}, u32[]{:S(2)}) async-start(bf16[32,16,2048]{2,1,0:T(8,128)(2,1)} %bitcast.40), calls=%async_computation | async-start | bytes 4194304 | tf_op jit(solution)/shard_map/all_to_all | solution.py:412
  45.3 13.8 %collective-permute-start = (bf16[128,2048]{1,0:T(8,128)(2,1)S(1)}, bf16[128,2048]{1,0:T(8,128)(2,1)S(1)}, u32[]{:S(2)}, u32[]{:S(2)}) collective-permute-start(bf16[128,2048]{1,0:T(8,128)(2,1)S(1)} %get-tuple-element.59.refs_0_), channel_id=1, source_target_pairs={{0,32},{32,64},{64,96},{96,0},{1,33},{33,65},{65,97},{97,1},{2,34}... | collective-permute-start | bytes 1572872 | tf_op jit(solution)/shard_map/ppermute | solution.py:408
  46.6 12.6 %collective-permute-start.1 = (bf16[128,2048]{1,0:T(8,128)(2,1)S(1)}, bf16[128,2048]{1,0:T(8,128)(2,1)S(1)}, u32[]{:S(2)}, u32[]{:S(2)}) collective-permute-start(bf16[128,2048]{1,0:T(8,128)(2,1)S(1)} %get-tuple-element.60.refs_1_), channel_id=1, source_target_pairs={{0,96},{32,0},{64,32},{96,64},{1,97},{33,1},{65,33},{97,65},{2,98}... | collective-permute-start | bytes 1572872 | tf_op jit(solution)/shard_map/ppermute | solution.py:408
  48.1 22.3 %collective-permute-start.2 = (bf16[128,2048]{1,0:T(8,128)(2,1)S(1)}, bf16[128,2048]{1,0:T(8,128)(2,1)S(1)}, u32[]{:S(2)}, u32[]{:S(2)}) collective-permute-start(bf16[128,2048]{1,0:T(8,128)(2,1)S(1)} %get-tuple-element.60.refs_1_), channel_id=1, source_target_pairs={{0,32},{32,64},{64,96},{96,0},{1,33},{33,65},{65,97},{97,1},{2,34}... | collective-permute-start | bytes 1572872 | tf_op jit(solution)/shard_map/ppermute | solution.py:408
  48.1 22.3 %collective-permute-start.3 = (bf16[128,2048]{1,0:T(8,128)(2,1)S(1)}, bf16[128,2048]{1,0:T(8,128)(2,1)S(1)}, u32[]{:S(2)}, u32[]{:S(2)}) collective-permute-start(bf16[128,2048]{1,0:T(8,128)(2,1)S(1)} %get-tuple-element.59.refs_0_), channel_id=1, source_target_pairs={{0,96},{32,0},{64,32},{96,64},{1,97},{33,1},{65,33},{97,65},{2,98}... | collective-permute-start | bytes 1572872 | tf_op jit(solution)/shard_map/ppermute | solution.py:408
  59.2 22.5 %collective-permute-start.6 = (bf16[128,2048]{1,0:T(8,128)(2,1)S(1)}, bf16[128,2048]{1,0:T(8,128)(2,1)S(1)}, u32[]{:S(2)}, u32[]{:S(2)}) collective-permute-start(bf16[128,2048]{1,0:T(8,128)(2,1)S(1)} %collective-permute-done.refs_2_.refs_0_), channel_id=1, source_target_pairs={{0,32},{32,64},{64,96},{96,0},{1,33},{33,65},{65,97},{97,1},{2,34}... | collective-permute-start | bytes 1572872 | tf_op jit(solution)/shard_map/ppermute | solution.py:408
  59.2 22.5 %collective-permute-start.7 = (bf16[128,2048]{1,0:T(8,128)(2,1)S(1)}, bf16[128,2048]{1,0:T(8,128)(2,1)S(1)}, u32[]{:S(2)}, u32[]{:S(2)}) collective-permute-start(bf16[128,2048]{1,0:T(8,128)(2,1)S(1)} %collective-permute-done.1.refs_3_.refs_1_), channel_id=1, source_target_pairs={{0,96},{32,0},{64,32},{96,64},{1,97},{33,1},{65,33},{97,65},{2,98}... | collective-permute-start | bytes 1572872 | tf_op jit(solution)/shard_map/ppermute | solution.py:408
  61.9 1.7 %copy-start.1 = (bf16[1,2048,640]{2,1,0:T(8,128)(2,1)S(1)}, bf16[1,2048,640]{2,1,0:T(8,128)(2,1)}, u32[]{:S(2)}) copy-start(bf16[1,2048,640]{2,1,0:T(8,128)(2,1)} %param.14) | copy-start | bytes 7864324
  63.6 1.9 %copy-start.2 = (bf16[1,640,2048]{2,1,0:T(8,128)(2,1)S(1)}, bf16[1,640,2048]{2,1,0:T(8,128)(2,1)}, u32[]{:S(2)}) copy-start(bf16[1,640,2048]{2,1,0:T(8,128)(2,1)} %param.15) | copy-start | bytes 7864324
  75.0 24.2 %collective-permute-start.4 = (bf16[128,2048]{1,0:T(8,128)(2,1)S(1)}, bf16[128,2048]{1,0:T(8,128)(2,1)S(1)}, u32[]{:S(2)}, u32[]{:S(2)}) collective-permute-start(bf16[128,2048]{1,0:T(8,128)(2,1)S(1)} %get-tuple-element.78), channel_id=1, source_target_pairs={{0,96},{32,0},{64,32},{96,64},{1,97},{33,1},{65,33},{97,65},{2,98}... | collective-permute-start | bytes 1572872 | tf_op jit(solution)/shard_map/ppermute | solution.py:408
  77.4 21.7 %collective-permute-start.5 = (bf16[128,2048]{1,0:T(8,128)(2,1)S(1)}, bf16[128,2048]{1,0:T(8,128)(2,1)S(1)}, u32[]{:S(2)}, u32[]{:S(2)}) collective-permute-start(bf16[128,2048]{1,0:T(8,128)(2,1)S(1)} %get-tuple-element.79), channel_id=1, source_target_pairs={{0,32},{32,64},{64,96},{96,0},{1,33},{33,65},{65,97},{97,1},{2,34}... | collective-permute-start | bytes 1572872 | tf_op jit(solution)/shard_map/ppermute | solution.py:408
  85.6 20.2 %collective-permute-start.8 = (bf16[128,2176]{1,0:T(8,128)(2,1)S(1)}, bf16[128,2176]{1,0:T(8,128)(2,1)S(1)}, u32[]{:S(2)}, u32[]{:S(2)}) collective-permute-start(bf16[128,2176]{1,0:T(8,128)(2,1)S(1)} %get-tuple-element.88), channel_id=1, source_target_pairs={{0,64},{32,96},{64,0},{96,32},{1,65},{33,97},{65,1},{97,33},{2,66}... | collective-permute-start | bytes 1671176 | tf_op jit(solution)/shard_map/ppermute | solution.py:408
  87.9 18.0 %collective-permute-start.9 = (f32[2,2048]{1,0:T(2,128)S(1)}, f32[2,2048]{1,0:T(2,128)S(1)}, u32[]{:S(2)}, u32[]{:S(2)}) collective-permute-start(f32[2,2048]{1,0:T(2,128)S(1)} %get-tuple-element.102.small_ref), channel_id=1, source_target_pairs={{0,32},{32,64},{64,96},{96,0},{1,33},{33,65},{65,97},{97,1},{2,34}... | collective-permute-start | bytes 49160 | tf_op jit(solution)/shard_map/ppermute | solution.py:408
  88.7 17.2 %collective-permute-start.10 = (f32[2,2048]{1,0:T(2,128)S(1)}, f32[2,2048]{1,0:T(2,128)S(1)}, u32[]{:S(2)}, u32[]{:S(2)}) collective-permute-start(f32[2,2048]{1,0:T(2,128)S(1)} %get-tuple-element.102.small_ref), channel_id=1, source_target_pairs={{0,96},{32,0},{64,32},{96,64},{1,97},{33,1},{65,33},{97,65},{2,98}... | collective-permute-start | bytes 49160 | tf_op jit(solution)/shard_map/ppermute | solution.py:408
  105.8 25.6 %copy-start.3 = (bf16[128,2048]{1,0:T(8,128)(2,1)S(1)}, bf16[128,2048]{1,0:T(8,128)(2,1)}, u32[]{:S(2)}) copy-start(bf16[128,2048]{1,0:T(8,128)(2,1)} %tokens_ref.3) | copy-start | bytes 1572868
  105.8 25.6 %copy-start.4 = (bf16[128,2048]{1,0:T(8,128)(2,1)S(1)}, bf16[128,2048]{1,0:T(8,128)(2,1)}, u32[]{:S(2)}) copy-start(bf16[128,2048]{1,0:T(8,128)(2,1)} %grad_ref.3) | copy-start | bytes 1572868
  105.8 25.6 %copy-start.5 = (f32[2048]{0:T(1024)S(1)}, f32[2048]{0:T(1024)}, u32[]{:S(2)}) copy-start(f32[2048]{0:T(1024)} %param.11) | copy-start | bytes 24580
